TPU v7x, 32 devices: a whole 2x2x4 slice. The times are simulated.
32 devices in a mesh: member: 2 (over y), lat: 4 (over x, core), lon: 4 (over z).
Axes of the slice: x: 2, y: 2, z: 4, core: 2. Of those that a mesh axis runs over, the one named last changes fastest.
Arguments:
- fields: float32 [4, 192, 32, 512], P('member', None, 'lat', 'lon'), parts along dimension 0, may hold values from -6 to 6
- wind_east: float32 [32, 512], P('lat', 'lon'), may hold values from -0.3 to 0.3
- wind_north: float32 [32, 512], P('lat', 'lon'), may hold values from -0.3 to 0.3
- diffusion: float32 [32, 512], P('lat', 'lon'), may hold values from 0.01 to 0.08
- inflow_owner: int32 [256, 1], P(('lat', 'lon')), may hold values from 0 to 3; in each aligned block of 16 rows (0 to 15, 16 to 31, ...) at most 8 rows name the same one
- inflow_cell: int32 [256, 128], P(('lat', 'lon')), may hold values from 0 to 1023
- inflow_node: int32 [256, 128], P(('lat', 'lon')), may hold values from 0 to 255
- inflow_weight: float32 [256, 128], P(('lat', 'lon')), may hold values from 0.25 to 1.5
- encoder: bfloat16 [192, 512], replicated, may hold values from -0.21875 to 0.21875
- sender_weight: bfloat16 [2, 512, 512], replicated, may hold values from -0.25 to 0.25
- receiver_weight: bfloat16 [2, 512, 512], replicated, may hold values from -0.25 to 0.25
- update_weight: bfloat16 [2, 512, 512], replicated, may hold values from -0.25 to 0.25
- decoder: bfloat16 [512, 192], replicated, may hold values from -0.25 to 0.25
- edge_sender: int32 [4, 4, 1536], P('lat', 'lon'), may hold values from 0 to 447, as said below
- edge_receiver: int32 [4, 4, 1536], P('lat', 'lon'), may hold values from 0 to 255
- halo_rows: int32 [4, 4, 4, 48], P('lat', 'lon'), may hold values from 0 to 255
- outflow_owner: int32 [256, 1], P(('lat', 'lon')), may hold values from 0 to 3; in each aligned block of 16 rows (0 to 15, 16 to 31, ...) at most 8 rows name the same one
- outflow_node: int32 [256, 128], P(('lat', 'lon')), may hold values from 0 to 255
- outflow_cell: int32 [256, 128], P(('lat', 'lon')), may hold values from 0 to 1023
- outflow_weight: float32 [256, 128], P(('lat', 'lon')), may hold values from 0.25 to 1.5
Outputs:
- revised_outlook: float32 [4, 192, 32, 512], P('member', None, 'lat', 'lon'), parts along dimension 0
There are 2 independent parts, one for each index of `member`. A program takes and returns all parts, laid end to end along the dimension named above; an argument that names none is the same for every part. Nothing has to cross between parts.
Inputs may be any that keep to these rules, and one draw needn't show every extreme that they name: `inflow_owner`: among the 16 rows of one device, no lon index appears more than 8 times. `outflow_owner`: among the 16 rows of one device, no lon index appears more than 8 times. `edge_sender`: No edge of the first lat index uses q = 0, none of the last uses q = 1.
All inputs are finite; a program needn't handle non-finite values.
Results may differ from a plain program's by a relative error of at most 0.0075.
Values may be sent and summed in bfloat16 or wider, within the bound.
No kernel may reach another device: no remote copies, remote signals or barrier semaphores. Data moves between devices by JAX's collectives and lax.ppermute only.
A program may use at most 128 MiB of HBM per device.

v0:
```python
import functools

import jax
import jax.numpy as jnp
from jax import lax
from jax.experimental import pallas as pl
from jax.experimental.pallas import tpu as pltpu
from jax.sharding import PartitionSpec as P

F32, BF16, I32 = jnp.float32, jnp.bfloat16, jnp.int32
MIB = 1 << 20
NODE_DEV = 256


def dot(a, b, ca=1, cb=0):
    return lax.dot_general(a, b, (((ca,), (cb,)), ((), ())), preferred_element_type=F32)


def iota(shape, dim):
    return lax.broadcasted_iota(I32, shape, dim)


def call(kernel, outs, args, smem=0, scratch=(), vmem=32, cost=None):
    spaces = [pltpu.SMEM] * smem + [pltpu.VMEM] * (len(args) - smem)
    single = not isinstance(outs, (list, tuple))
    out = pl.pallas_call(
        kernel,
        out_shape=outs if single else tuple(outs),
        in_specs=[pl.BlockSpec(memory_space=s) for s in spaces],
        out_specs=pl.BlockSpec(memory_space=pltpu.VMEM)
        if single
        else tuple(pl.BlockSpec(memory_space=pltpu.VMEM) for _ in outs),
        scratch_shapes=list(scratch),
        compiler_params=pltpu.CompilerParams(vmem_limit_bytes=vmem * MIB),
        cost_estimate=cost,
    )(*args)
    return out


def cost(flops, bytes_accessed):
    return pl.CostEstimate(flops=int(flops), bytes_accessed=int(bytes_accessed), transcendentals=0)


def shape(dims, dtype):
    return jax.ShapeDtypeStruct(tuple(dims), dtype)


def split(v):
    hi = v.astype(BF16).astype(F32)
    return hi, v - hi


def pick_columns(width):
    row, lane = iota((16, width), 0), iota((16, width), 1)
    hit = (row == 0) & (lane == 0) | (row == 1) & (lane == 1)
    hit = hit | (row == 2) & (lane == width - 1) | (row == 3) & (lane == width - 2)
    return hit.astype(F32).astype(BF16)


def coefficients(we, wn, d):
    pe, ne = jnp.maximum(we, 0.0), jnp.minimum(we, 0.0)
    pn, nn = jnp.maximum(wn, 0.0), jnp.minimum(wn, 0.0)
    return 1.0 - pe + ne - pn + nn - 4.0 * d, pe + d, d - ne, pn + d, d - nn


def edge_kernel(rows, wanted, x_ref, we_ref, wn_ref, d_ref, halo_ref, up_ref, down_ref, col_ref):
    count = x_ref.shape[0] // rows
    width = x_ref.shape[1]

    def row(r):
        return x_ref[pl.ds(r, count, stride=rows), :].astype(BF16)

    line = iota((16, width), 0)
    for out_ref, near, far, q in ((up_ref, rows - 1, rows - 2, 1), (down_ref, 0, 1, 0)):
        out_ref[0:count, :] = row(near)
        out_ref[count : 2 * count, :] = row(far)
        block = jnp.zeros((16, width), F32)
        for j, ref in enumerate((we_ref, wn_ref, d_ref)):
            hi, lo = split(ref[near : near + 1, :])
            block = jnp.where(line == j, hi, jnp.where(line == j + 3, lo, block))
        out_ref[2 * count : 2 * count + 16, :] = block.astype(BF16)
        out_ref[2 * count + 16 : 2 * count + 16 + wanted, :] = jnp.broadcast_to(
            halo_ref[q * wanted : (q + 1) * wanted, :].astype(F32), (wanted, width)
        ).astype(BF16)
    pick = pick_columns(width)
    for r in range(rows):
        got = dot(pick, row(r), 1, 1)
        for k in range(4):
            col_ref[k * rows + r : k * rows + r + 1, :] = got[k : k + 1, :]


def side_kernel(rows, wanted, south_ref, north_ref, col_ref, we_ref, wn_ref, d_ref, halo_ref, east_ref, west_ref):
    count = col_ref.shape[1]
    width = we_ref.shape[1]
    pick = pick_columns(width)
    south = dot(pick, south_ref[0:count, :], 1, 1)
    north = dot(pick, north_ref[0:count, :], 1, 1)
    line, lane = iota((rows, count), 0), iota((rows, count), 1)
    for out_ref, k, c, q in ((east_ref, 2, width - 1, 3), (west_ref, 0, 0, 2)):
        corner = jnp.where(line == 0, south[k : k + 1, :], jnp.where(line == 1, north[k : k + 1, :], 0.0))
        rates = jnp.zeros((rows, count), F32)
        for j, ref in enumerate((we_ref, wn_ref, d_ref)):
            hi, lo = split(ref[:, c : c + 1])
            rates = jnp.where(lane == j, hi, jnp.where(lane == j + 3, lo, rates))
        body = [col_ref[k * rows : (k + 2) * rows, :], corner, rates]
        out_ref[0 : 4 * rows, :] = jnp.concatenate(body, 0).astype(BF16)
        out_ref[4 * rows : 4 * rows + wanted, :] = jnp.broadcast_to(
            halo_ref[q * wanted : (q + 1) * wanted, :].astype(F32), (wanted, count)
        ).astype(BF16)


def build_kernel(by_owner, slots, per, me_ref, owner_ref, node_ref, cell_ref, weight_ref, out_ref, acc):
    nodes, cells = acc.shape[1], acc.shape[2]
    entries = node_ref.shape[1]
    acc[...] = jnp.zeros(acc.shape, F32)

    @pl.loop(0, node_ref.shape[0])
    def _(b):
        if by_owner:
            slot = lax.rem(owner_ref[b] - me_ref[0] + slots, slots)
            mine = True
        else:
            slot = b // per
            mine = owner_ref[b] == me_ref[0]

        @pl.when(mine)
        def _():
            node = node_ref[pl.ds(b, 1), :].astype(I32)
            cell = cell_ref[pl.ds(b, 1), :].astype(I32)
            hot = jnp.where(iota((nodes, entries), 0) == node, 1.0, 0.0).astype(BF16)
            spread = jnp.where(iota((cells, entries), 0) == cell, weight_ref[pl.ds(b, 1), :], 0.0).astype(BF16)
            acc[slot] += dot(hot, spread, 1, 1)

    for s in range(slots):
        out_ref[s] = acc[s].astype(BF16)


def build(by_owner, slots, nodes, cells, per, me, owner, node, cell, weight):
    size = slots * nodes * cells
    return call(
        functools.partial(build_kernel, by_owner, slots, per),
        shape((slots, nodes, cells), BF16),
        (me, owner, node, cell, weight),
        smem=2,
        scratch=[pltpu.VMEM((slots, nodes, cells), F32)],
        vmem=8 + 8 * size // MIB,
        cost=cost(2 * 16 * node.shape[1] * nodes * cells, 4 * size),
    )


def step_kernel(
    rows, slots, nodes,
    x_ref, we_ref, wn_ref, d_ref, col_ref, south_ref, north_ref, west_ref, east_ref, pole_ref, a_ref,
    u_ref, *rest,
):
    part_refs, (b1, b2, keys, flat) = rest[:slots], rest[slots:]
    count = x_ref.shape[0] // rows
    width = x_ref.shape[1]
    at_south, at_north = pole_ref[0:1, 0:1], pole_ref[1:2, 0:1]

    sel_row, sel_lane = iota((8, width), 0), iota((8, width), 1)
    select = (sel_row % 2 == 0) & (sel_row < 4) & (sel_lane == 0)
    select = select | (sel_row % 2 == 1) & (sel_row < 4) & (sel_lane == width - 1)
    select = jnp.where(select, 1.0, 0.0).astype(BF16)
    key_line = iota((8, count), 0)

    def place(west, east):
        wh, wl = split(west)
        eh, el = split(east)
        key = jnp.where(key_line == 0, wh, jnp.where(key_line == 1, eh, 0.0))
        key = jnp.where(key_line == 2, wl, jnp.where(key_line == 3, el, key))
        return dot(key.astype(BF16), select, 0, 0)

    c0, cw, ce, cs, cn = coefficients(we_ref[...], wn_ref[...], d_ref[...])
    line, lane = iota((rows, width), 0), iota((rows, width), 1)
    c0 = c0 + jnp.where(line == 0, at_south * cs, 0.0) + jnp.where(line == rows - 1, at_north * cn, 0.0)
    edge_w, edge_e = cw[:, 0:1], ce[:, width - 1 : width]
    edge_s, edge_n = cs[0:1, :] * (1.0 - at_south), cn[rows - 1 : rows, :] * (1.0 - at_north)
    cw = jnp.where(lane == 0, 0.0, cw)
    ce = jnp.where(lane == width - 1, 0.0, ce)
    cs = jnp.where(line == 0, 0.0, cs)
    cn = jnp.where(line == rows - 1, 0.0, cn)

    def boundary(b_ref, west, east, south, north):
        bw, be = edge_w * west, edge_e * east
        for r in range(rows):
            placed = place(bw[r : r + 1, :], be[r : r + 1, :])
            if r == 0:
                placed = placed + edge_s * south
            if r == rows - 1:
                placed = placed + edge_n * north
            b_ref[pl.ds(r, count, stride=rows), :] = placed

    s1, s2 = south_ref[0:count, :].astype(F32), south_ref[count : 2 * count, :].astype(F32)
    n1, n2 = north_ref[0:count, :].astype(F32), north_ref[count : 2 * count, :].astype(F32)
    west, east = west_ref[...].astype(F32), east_ref[...].astype(F32)
    w1, w2, w_corner, w_rate = (west[k * rows : (k + 1) * rows, :] for k in range(4))
    e1, e2, e_corner, e_rate = (east[k * rows : (k + 1) * rows, :] for k in range(4))
    boundary(b1, w1, e1, s1, n1)

    full = iota((count, width), 1)

    def ring_row(rate_ref, at, mid, south, north):
        rate = rate_ref[2 * count : 2 * count + 16, :].astype(F32)
        k0, kw, ke, ks, kn = coefficients(*(rate[j : j + 1, :] + rate[j + 3 : j + 4, :] for j in range(3)))
        ends = place(w_corner[at : at + 1, :], e_corner[at : at + 1, :])
        to_w = jnp.where(full == 0, ends, pltpu.roll(mid, 1, 1))
        to_e = jnp.where(full == width - 1, ends, pltpu.roll(mid, width - 1, 1))
        return k0 * mid + kw * to_w + ke * to_e + ks * south + kn * north

    def ring_col(rate, corner, mid, out_w, out_e):
        k0, kw, ke, ks, kn = coefficients(*(rate[:, j : j + 1] + rate[:, j + 3 : j + 4] for j in range(3)))
        first = iota(k0.shape, 0)
        k0 = k0 + jnp.where(first == 0, at_south * ks, 0.0) + jnp.where(first == rows - 1, at_north * kn, 0.0)
        ks = ks * jnp.where(first == 0, 1.0 - at_south, 1.0)
        kn = kn * jnp.where(first == rows - 1, 1.0 - at_north, 1.0)
        step = iota(mid.shape, 0)
        to_s = jnp.where(step == 0, corner[0:1, :], pltpu.roll(mid, 1, 0))
        to_n = jnp.where(step == rows - 1, corner[1:2, :], pltpu.roll(mid, rows - 1, 0))
        return k0 * mid + kw * out_w + ke * out_e + ks * to_s + kn * to_n

    ring_s = ring_row(south_ref, 0, s1, s2, x_ref[pl.ds(0, count, stride=rows), :])
    ring_n = ring_row(north_ref, 1, n1, x_ref[pl.ds(rows - 1, count, stride=rows), :], n2)
    ring_w = ring_col(w_rate, w_corner, w1, w2, col_ref[0:rows, :])
    ring_e = ring_col(e_rate, e_corner, e1, col_ref[2 * rows : 3 * rows, :], e2)
    boundary(b2, ring_w, ring_e, ring_s, ring_n)

    group = 8

    @pl.loop(0, count // group)
    def _(g):
        here = pl.ds(pl.multiple_of(g * group * rows, group * rows), group * rows)

        def step(v, b_ref):
            v = c0 * v + cw * pltpu.roll(v, 1, 2) + ce * pltpu.roll(v, width - 1, 2) + (
                cs * pltpu.roll(v, 1, 1) + cn * pltpu.roll(v, rows - 1, 1)
            )
            return v + b_ref[here, :].reshape(group, rows, width)

        v = step(step(x_ref[here, :].reshape(group, rows, width), b1), b2)
        u_ref[here, :] = v.reshape(group * rows, width)

    for r in range(rows):
        flat[:, r * width : (r + 1) * width] = u_ref[pl.ds(r, count, stride=rows), :].astype(BF16)
    for s in range(slots):
        part_refs[s][...] = dot(a_ref[s], flat[...], 1, 1).astype(part_refs[s].dtype)


def silu(v):
    return 0.5 * v * (1.0 + jnp.tanh(0.5 * v))


def normalize(v):
    return (v * lax.rsqrt(jnp.mean(v * v, axis=-1, keepdims=True) + 1e-06)).astype(BF16)


def link_kernel(sender_ref, receiver_ref, row_ref, gather_ref, scatter_ref):
    edges, known = gather_ref.shape
    nodes = scatter_ref.shape[0]
    lane = iota((edges, nodes), 1)
    gather_ref[:, 0:nodes] = jnp.where(sender_ref[...] == lane, 1.0, 0.0).astype(BF16)
    gather_ref[:, nodes : 2 * nodes] = jnp.where(receiver_ref[...] == lane, 1.0, 0.0).astype(BF16)
    rest = iota((edges, known - 2 * nodes), 1) + nodes
    gather_ref[:, 2 * nodes :] = jnp.where(sender_ref[...] == rest, 1.0, 0.0).astype(BF16)
    scatter_ref[...] = jnp.where(row_ref[...] == iota((nodes, edges), 0), 1.0, 0.0).astype(BF16)


def project(m, hidden, owed, ws, wr, table_ref, out_refs, wanted, nodes):
    normed = normalize(hidden)
    source = dot(normed, ws).astype(BF16)
    table_ref[m, 0:nodes, :] = source
    table_ref[m, nodes : 2 * nodes, :] = dot(normed, wr).astype(BF16)
    for q in range(4):
        out_refs[q][m * wanted : (m + 1) * wanted, :] = dot(owed[q], source).astype(BF16)


def encode_kernel(
    slots, rows, count, wanted,
    *refs,
):
    part_refs = refs[:slots]
    enc_ref, ws_ref, wr_ref, south_ref, north_ref, west_ref, east_ref = refs[slots : slots + 7]
    hidden_ref, table_ref, owed_ref, *out_refs, pad = refs[slots + 7 :]
    nodes = part_refs[0].shape[0]
    members, quantities = hidden_ref.shape[0], enc_ref.shape[0]
    lane = iota((wanted, nodes), 1)
    at = 2 * count + 16
    lists = (
        south_ref[at : at + wanted, 0:1],
        north_ref[at : at + wanted, 0:1],
        west_ref[4 * rows : 4 * rows + wanted, 0:1],
        east_ref[4 * rows : 4 * rows + wanted, 0:1],
    )
    owed = [jnp.where(v.astype(F32).astype(I32) == lane, 1.0, 0.0).astype(BF16) for v in lists]
    for q in range(4):
        owed_ref[q * wanted : (q + 1) * wanted, :] = owed[q]
    total = part_refs[0][...].astype(F32)
    for ref in part_refs[1:]:
        total = total + ref[...].astype(F32)
    total = total.astype(BF16)
    pad[...] = jnp.zeros(pad.shape, BF16)
    for m in range(members):
        pad[m, m * quantities : (m + 1) * quantities, :] = enc_ref[...]
        hidden = silu(dot(total, pad[m]))
        hidden_ref[m] = hidden
        project(m, hidden, owed, ws_ref[...], wr_ref[...], table_ref, out_refs, wanted, nodes)


def layer_kernel(last, wanted, chunk, *refs):
    hidden_ref, table_ref, owed_ref, gather_ref, scatter_ref = refs[:5]
    halo_refs, wu_ref = refs[5:9], refs[9]
    if last:
        dec_ref, out_ref, known = refs[10:]
    else:
        ws_ref, wr_ref, next_hidden_ref, next_table_ref, *out_refs, known = refs[10:]
    members, nodes, width = hidden_ref.shape
    edges, rows = gather_ref.shape
    if not last:
        owed = [owed_ref[q * wanted : (q + 1) * wanted, :] for q in range(4)]
    for m in range(members):
        known[0 : 2 * nodes, :] = table_ref[m]
        for q in range(4):
            at = 2 * nodes + q * wanted
            known[at : at + wanted, :] = halo_refs[q][m * wanted : (m + 1) * wanted, :]
        at = 2 * nodes + 4 * wanted
        known[at:, :] = jnp.zeros((rows - at, width), BF16)
        collected = jnp.zeros((nodes, width), F32)
        for k in range(0, edges, chunk):
            message = silu(dot(gather_ref[k : k + chunk, :], known[...])).astype(BF16)
            collected = collected + dot(scatter_ref[:, k : k + chunk], message)
        hidden = hidden_ref[m] + dot(collected.astype(BF16), wu_ref[...])
        if last:
            got = dot(dec_ref[...], normalize(hidden), 1, 1)
            out_ref[m * got.shape[0] : (m + 1) * got.shape[0], :] = got.astype(BF16)
        else:
            next_hidden_ref[m] = hidden
            project(m, hidden, owed, ws_ref[...], wr_ref[...], next_table_ref, out_refs, wanted, nodes)


def land_kernel(rows, slots, u_ref, w_ref, *refs):
    corr_refs, out_ref = refs[:slots], refs[slots]
    width = u_ref.shape[1]
    count = u_ref.shape[0] // rows
    total = dot(corr_refs[0][...], w_ref[0])
    for s in range(1, slots):
        total = total + dot(corr_refs[s][...], w_ref[s])
    for r in range(rows):
        here = pl.ds(r, count, stride=rows)
        out_ref[here, :] = u_ref[here, :] + total[:, r * width : (r + 1) * width]


def body(
    fields, wind_east, wind_north, diffusion, inflow_owner, inflow_cell, inflow_node, inflow_weight,
    encoder, sender_weight, receiver_weight, update_weight, decoder, edge_sender, edge_receiver, halo_rows,
    outflow_owner, outflow_node, outflow_cell, outflow_weight,
):
    members, quantities, rows, width = fields.shape
    count, cells = members * quantities, rows * width
    lon, lat = lax.axis_size("lon"), lax.axis_size("lat")
    me = lax.axis_index("lon").astype(I32).reshape(1)
    blocks, entries = inflow_cell.shape
    hid = encoder.shape[1]
    layers = sender_weight.shape[0]
    edges = edge_sender.shape[-1]
    wanted = halo_rows.shape[-1]
    nodes = NODE_DEV

    def shift(v, s):
        return lax.ppermute(v, "lon", [(i, (i + s) % lon) for i in range(lon)])

    def up(v):
        return lax.ppermute(v, "lat", [(i, i + 1) for i in range(lat - 1)])

    def down(v):
        return lax.ppermute(v, "lat", [(i + 1, i) for i in range(lat - 1)])

    x = fields.reshape(count * rows, width)
    halo = halo_rows.reshape(4 * wanted, 1)
    rates = (wind_east, wind_north, diffusion)
    tall, wide = 2 * count + 16 + wanted, 4 * rows + wanted
    to_north, to_south, cols = call(
        functools.partial(edge_kernel, rows, wanted),
        (shape((tall, width), BF16), shape((tall, width), BF16), shape((4 * rows, count), F32)),
        (x, *rates, halo),
        cost=cost(0, 8 * MIB),
    )
    south, north = up(to_north), down(to_south)
    to_east, to_west = call(
        functools.partial(side_kernel, rows, wanted),
        (shape((wide, count), BF16), shape((wide, count), BF16)),
        (south, north, cols, *rates, halo),
        cost=cost(0, 4 * MIB),
    )
    west, east = shift(to_east, 1), shift(to_west, lon - 1)

    into = build(
        True, lon, nodes, cells, blocks, me, inflow_owner.reshape(-1), inflow_node, inflow_cell, inflow_weight
    )
    lat_at = lax.axis_index("lat")
    pole = jnp.stack([lat_at == 0, lat_at == lat - 1]).astype(F32)[:, None]
    u, *parts = call(
        functools.partial(step_kernel, rows, lon, nodes),
        [shape(x.shape, F32)] + [shape((nodes, count), F32)] + [shape((nodes, count), BF16)] * (lon - 1),
        (x, *rates, cols, south, north, west, east, pole, into),
        scratch=[
            pltpu.VMEM(x.shape, F32),
            pltpu.VMEM(x.shape, F32),
            pltpu.VMEM((8, 8, count), F32),
            pltpu.VMEM((count, cells), BF16),
        ],
        vmem=24 + lon * 3,
        cost=cost(2 * lon * nodes * cells * count, 16 * MIB),
    )
    parts = parts[:1] + [shift(parts[s], s) for s in range(1, lon)]

    lists = jnp.stack(
        [outflow_node.astype(F32), outflow_cell.astype(F32), outflow_weight,
         jnp.broadcast_to(outflow_owner.astype(F32), (blocks, entries))]
    )
    lists = jnp.stack([lists] + [shift(lists, s) for s in range(1, lon)], axis=1)
    lists = lists.reshape(4, lon * blocks, entries)
    owners = lists[3, :, 0].astype(I32)
    onto = build(False, lon, nodes, cells, blocks, me, owners, lists[0], lists[1], lists[2])

    known = 2 * nodes + 256 * -(-4 * wanted // 256)
    senders, receivers = edge_sender.reshape(edges), edge_receiver.reshape(edges)
    gather, scatter = call(
        link_kernel,
        (shape((edges, known), BF16), shape((nodes, edges), BF16)),
        (senders.reshape(edges, 1), receivers.reshape(edges, 1), receivers.reshape(1, edges)),
        cost=cost(0, 8 * MIB),
    )

    reply = [shape((members * wanted, hid), BF16)] * 4
    state = [shape((members, nodes, hid), F32), shape((members, 2 * nodes, hid), BF16)]
    hidden, table, owed, *out = call(
        functools.partial(encode_kernel, lon, rows, count, wanted),
        state + [shape((4 * wanted, nodes), BF16)] + reply,
        (*parts, encoder, sender_weight[0], receiver_weight[0], south, north, west, east),
        scratch=[pltpu.VMEM((members, count, hid), BF16)],
        cost=cost(2e9, 8 * MIB),
    )
    for layer in range(layers):
        halos = [up(out[1]), down(out[0]), shift(out[3], 1), shift(out[2], lon - 1)]
        last = layer == layers - 1
        args = (hidden, table, owed, gather, scatter, *halos, update_weight[layer])
        scratch = [pltpu.VMEM((known, hid), BF16)]
        kernel = functools.partial(layer_kernel, last, wanted, edges // 3)
        if last:
            corr = call(
                kernel, shape((count, nodes), BF16), (*args, decoder.T), scratch=scratch, cost=cost(4e9, 12 * MIB)
            )
        else:
            hidden, table, *out = call(
                kernel,
                state + reply,
                (*args, sender_weight[layer + 1], receiver_weight[layer + 1]),
                scratch=scratch,
                cost=cost(4e9, 12 * MIB),
            )
    corrs = [corr] + [shift(corr, s) for s in range(1, lon)]
    out = call(
        functools.partial(land_kernel, rows, lon),
        shape(x.shape, F32),
        (u, onto, *corrs),
        vmem=24 + lon,
        cost=cost(2 * lon * nodes * cells * count, 8 * MIB),
    )
    return out.reshape(members, quantities, rows, width)


def solution(mesh):
    tile, block, part = P("lat", "lon"), P(("lat", "lon"), None), P("lat", "lon", None)
    placed = (P("member", None, "lat", "lon"), tile, tile, tile, block, block, block, block)
    placed += (P(),) * 5 + (part, part, P("lat", "lon", None, None)) + (block,) * 4
    return jax.shard_map(
        body, mesh=mesh, in_specs=placed, out_specs=P("member", None, "lat", "lon"), check_vma=False
    )
```

profile of v0, /device:TPU:15, one launch (start us, length us, event | category | flops | bytes accessed | tf_op | source)
XLA Modules:
  0.0 116.8 jit_solution(14324692550095442250)
XLA Ops:
  2.2 1.3 %collective-permute-start.4 = (f32[4,16,128]{2,1,0:T(8,128)S(1)}, f32[4,16,128]{2,1,0:T(8,128)S(1)}, u32[]{:S(2)}, u32[]{:S(2)}) collective-permute-start(f32[4,16,128]{2,1,0:T(8,128)S(1)} %get-tuple-element.65), channel_id=1, source_target_pairs={{0,1},{1,2},{2,3},{3,0},{4,5},{5,6},{6,7},{7,4},{8,9},{9,10},{10,1... | collective-permute-start | bytes 98312 | tf_op jit(solution)/shard_map/ppermute | solution.py:369
  5.3 1.4 %copy-done = f32[2,192,8,128]{3,2,1,0:T(8,128)S(1)} copy-done((f32[2,192,8,128]{3,2,1,0:T(8,128)S(1)}, f32[2,192,8,128]{3,2,1,0:T(8,128)}, u32[]{:S(2)}) %copy-start) | copy-done | bytes 1572888
  10.6 3.7 %collective-permute-start.1 = (bf16[832,128]{1,0:T(8,128)(2,1)S(1)}, bf16[832,128]{1,0:T(8,128)(2,1)S(1)}, u32[]{:S(2)}, u32[]{:S(2)}) collective-permute-start(bf16[832,128]{1,0:T(8,128)(2,1)S(1)} %get-tuple-element.32), channel_id=1, source_target_pairs={{4,0},{8,4},{12,8},{5,1},{9,5},{13,9},{6,2},{10,6},{14,10},{7,3},{... | collective-permute-start | bytes 638984 | tf_op jit(solution)/shard_map/ppermute | solution.py:375
  16.9 1.4 %slice_bitcast_fusion.1 = (bf16[512,512]{1,0:T(8,128)(2,1)S(1)}, bf16[512,512]{1,0:T(8,128)(2,1)S(1)}, bf16[512,512]{1,0:T(8,128)(2,1)S(1)}, bf16[512,512]{1,0:T(8,128)(2,1)S(1)}) fusion(bf16[2,512,512]{2,1,0:T(8,128)(2,1)S(1)} %copy-done.16, bf16[2,512,512]{2,1,0:T(8,128)(2,1)} %param.29), kind=kLoop, calls=%fused_computation.1 | loop fusion | bytes 4194304 | tf_op jit(solution)/shard_map/squeeze | solution.py:457
  20.2 5.9 %shard_map.192.a_ref = bf16[4,256,1024]{2,1,0:T(8,128)(2,1)S(1)} custom-call(s32[1]{0:T(128)} %bitcast.3.me_ref, s32[16]{0:T(128)S(1)} %bitcast.52, s32[16,128]{1,0:T(8,128)S(1)} %copy-done.11, s32[16,128]{1,0:T(8,128)S(1)} %copy-done.12, f32[16,128]{1,0:T(8,128)S(1)} %copy-done.13), custom_call_target="tpu_custom_call" | custom-call | flops 1073741824 | bytes 4194304 | tf_op jit(solution)/shard_map/pallas_call | solution.py:26
  26.2 11.1 %shard_map.193 = (f32[3072,128]{1,0:T(8,128)S(1)}, f32[256,384]{1,0:T(8,128)S(1)}, bf16[256,384]{1,0:T(8,128)(2,1)S(1)}, bf16[256,384]{1,0:T(8,128)(2,1)S(1)}, bf16[256,384]{1,0:T(8,128)(2,1)S(1)}) custom-call(f32[3072,128]{1,0:T(8,128)S(1)} %bitcast.45, f32[8,128]{1,0:T(8,128)S(1)} %copy-done.3, f32[8,128]{1,0:T(8,128)S(1)} %copy-done.5, ...), custom_call_target="tpu_custom_call" | custom-call | flops 805306368 | bytes 16777216 | tf_op jit(solution)/shard_map/pallas_call | solution.py:26
  37.6 5.0 %collective-permute-start.8 = (bf16[256,384]{1,0:T(8,128)(2,1)S(1)}, bf16[256,384]{1,0:T(8,128)(2,1)S(1)}, u32[]{:S(2)}, u32[]{:S(2)}) collective-permute-start(bf16[256,384]{1,0:T(8,128)(2,1)S(1)} %get-tuple-element.38), channel_id=1, source_target_pairs={{0,2},{1,3},{2,0},{3,1},{4,6},{5,7},{6,4},{7,5},{8,10},{9,11},{10,... | collective-permute-start | bytes 589832 | tf_op jit(solution)/shard_map/ppermute | solution.py:369
  43.6 3.5 %collective-permute-start.6 = (f32[4,16,128]{2,1,0:T(8,128)S(1)}, f32[4,16,128]{2,1,0:T(8,128)S(1)}, u32[]{:S(2)}, u32[]{:S(2)}) collective-permute-start(f32[4,16,128]{2,1,0:T(8,128)S(1)} %get-tuple-element.65), channel_id=1, source_target_pairs={{0,3},{1,0},{2,1},{3,2},{4,7},{5,4},{6,5},{7,6},{8,11},{9,8},{10,9... | collective-permute-start | bytes 98312 | tf_op jit(solution)/shard_map/ppermute | solution.py:369
  47.1 7.9 %collective-permute-done.8.refs_2_ = bf16[256,384]{1,0:T(8,128)(2,1)S(1)} collective-permute-done((bf16[256,384]{1,0:T(8,128)(2,1)S(1)}, bf16[256,384]{1,0:T(8,128)(2,1)S(1)}, u32[]{:S(2)}, u32[]{:S(2)}) %collective-permute-start.8) | collective-permute-done | bytes 196640 | tf_op jit(solution)/shard_map/ppermute | solution.py:369
  55.0 4.1 %collective-permute-done.9.refs_3_ = bf16[256,384]{1,0:T(8,128)(2,1)S(1)} collective-permute-done((bf16[256,384]{1,0:T(8,128)(2,1)S(1)}, bf16[256,384]{1,0:T(8,128)(2,1)S(1)}, u32[]{:S(2)}, u32[]{:S(2)}) %collective-permute-start.9) | collective-permute-done | bytes 196640 | tf_op jit(solution)/shard_map/ppermute | solution.py:369
  59.0 1.7 %shard_map.195 = (f32[2,256,512]{2,1,0:T(8,128)S(1)}, bf16[2,512,512]{2,1,0:T(8,128)(2,1)S(1)}, bf16[192,256]{1,0:T(8,128)(2,1)S(1)}, bf16[96,512]{1,0:T(8,128)(...) custom-call(f32[256,384]{1,0:T(8,128)S(1)} %get-tuple-element.36.refs_0_, ...), custom_call_target="tpu_custom_call" | custom-call | flops 2000000000 | bytes 8388608 | tf_op jit(solution)/shard_map/pallas_call | solution.py:26
  62.1 4.3 %collective-permute-start.11 = (bf16[96,512]{1,0:T(8,128)(2,1)S(1)}, bf16[96,512]{1,0:T(8,128)(2,1)S(1)}, u32[]{:S(2)}, u32[]{:S(2)}) collective-permute-start(bf16[96,512]{1,0:T(8,128)(2,1)S(1)} %get-tuple-element.46), channel_id=1, source_target_pairs={{4,0},{8,4},{12,8},{5,1},{9,5},{13,9},{6,2},{10,6},{14,10},{7,3},{... | collective-permute-start | bytes 294920 | tf_op jit(solution)/shard_map/ppermute | solution.py:375
  66.4 1.4 %collective-permute-start.13 = (bf16[96,512]{1,0:T(8,128)(2,1)S(1)}, bf16[96,512]{1,0:T(8,128)(2,1)S(1)}, u32[]{:S(2)}, u32[]{:S(2)}) collective-permute-start(bf16[96,512]{1,0:T(8,128)(2,1)S(1)} %get-tuple-element.48), channel_id=1, source_target_pairs={{0,3},{1,0},{2,1},{3,2},{4,7},{5,4},{6,5},{7,6},{8,11},{9,8},{10,9... | collective-permute-start | bytes 294920 | tf_op jit(solution)/shard_map/ppermute | solution.py:369
  67.9 2.0 %collective-permute-done.12.refs_7_ = bf16[96,512]{1,0:T(8,128)(2,1)S(1)} collective-permute-done((bf16[96,512]{1,0:T(8,128)(2,1)S(1)}, bf16[96,512]{1,0:T(8,128)(2,1)S(1)}, u32[]{:S(2)}, u32[]{:S(2)}) %collective-permute-start.12) | collective-permute-done | bytes 98336 | tf_op jit(solution)/shard_map/ppermute | solution.py:369
  71.0 5.5 %shard_map.197 = (f32[2,256,512]{2,1,0:T(8,128)S(1)}, bf16[2,512,512]{2,1,0:T(8,128)(2,1)S(1)}, bf16[96,512]{1,0:T(8,128)(2,1)S(1)}, bf16[96,512]{1,0:T(8,128)(2...) custom-call(f32[2,256,512]{2,1,0:T(8,128)S(1)} %get-tuple-element.40.refs_0_, ...), custom_call_target="tpu_custom_call" | custom-call | flops 4000000000 | bytes 12582912 | tf_op jit(solution)/shard_map/pallas_call | solution.py:26
  77.9 4.4 %collective-permute-start.15 = (bf16[96,512]{1,0:T(8,128)(2,1)S(1)}, bf16[96,512]{1,0:T(8,128)(2,1)S(1)}, u32[]{:S(2)}, u32[]{:S(2)}) collective-permute-start(bf16[96,512]{1,0:T(8,128)(2,1)S(1)} %get-tuple-element.52), channel_id=1, source_target_pairs={{4,0},{8,4},{12,8},{5,1},{9,5},{13,9},{6,2},{10,6},{14,10},{7,3},{... | collective-permute-start | bytes 294920 | tf_op jit(solution)/shard_map/ppermute | solution.py:375
  84.2 1.7 %collective-permute-done.16.refs_7_ = bf16[96,512]{1,0:T(8,128)(2,1)S(1)} collective-permute-done((bf16[96,512]{1,0:T(8,128)(2,1)S(1)}, bf16[96,512]{1,0:T(8,128)(2,1)S(1)}, u32[]{:S(2)}, u32[]{:S(2)}) %collective-permute-start.16) | collective-permute-done | bytes 98336 | tf_op jit(solution)/shard_map/ppermute | solution.py:369
  86.0 2.7 %collective-permute-done.17.refs_8_ = bf16[96,512]{1,0:T(8,128)(2,1)S(1)} collective-permute-done((bf16[96,512]{1,0:T(8,128)(2,1)S(1)}, bf16[96,512]{1,0:T(8,128)(2,1)S(1)}, u32[]{:S(2)}, u32[]{:S(2)}) %collective-permute-start.17) | collective-permute-done | bytes 98336 | tf_op jit(solution)/shard_map/ppermute | solution.py:369
  88.7 4.9 %shard_map.198.refs_0_ = bf16[384,256]{1,0:T(8,128)(2,1)S(1)} custom-call(f32[2,256,512]{2,1,0:T(8,128)S(1)} %get-tuple-element.49.refs_0_, bf16[2,512,512]{2,1,0:T(8,128)(2,1)S(1)} %get-tuple-element.50.refs_1_, bf16[192,256]{1,0:T(8,128)(2,1)S(1)} %get-tuple-element.42.refs_2_, bf16[1536,768]{1,0:T(8,128)(2,1)S(1)} %get-tuple-element.43.refs_3_, ...), custom_call_target="tpu_custom_call" | custom-call | flops 4000000000 | bytes 12582912 | tf_op jit(solution)/shard_map/pallas_call | solution.py:26
  94.3 2.1 %collective-permute-start.19 = (bf16[384,256]{1,0:T(8,128)(2,1)S(1)}, bf16[384,256]{1,0:T(8,128)(2,1)S(1)}, u32[]{:S(2)}, u32[]{:S(2)}) collective-permute-start(bf16[384,256]{1,0:T(8,128)(2,1)S(1)} %shard_map.198.refs_0_), channel_id=1, source_target_pairs={{0,2},{1,3},{2,0},{3,1},{4,6},{5,7},{6,4},{7,5},{8,10},{9,11},{10,... | collective-permute-start | bytes 589832 | tf_op jit(solution)/shard_map/ppermute | solution.py:369
  96.4 1.4 %collective-permute-start.20 = (bf16[384,256]{1,0:T(8,128)(2,1)S(1)}, bf16[384,256]{1,0:T(8,128)(2,1)S(1)}, u32[]{:S(2)}, u32[]{:S(2)}) collective-permute-start(bf16[384,256]{1,0:T(8,128)(2,1)S(1)} %shard_map.198.refs_0_), channel_id=1, source_target_pairs={{0,3},{1,0},{2,1},{3,2},{4,7},{5,4},{6,5},{7,6},{8,11},{9,8},{10,9... | collective-permute-start | bytes 589832 | tf_op jit(solution)/shard_map/ppermute | solution.py:369
  97.9 11.1 %shard_map.194.w_ref = bf16[4,256,1024]{2,1,0:T(8,128)(2,1)S(1)} custom-call(s32[1]{0:T(128)} %bitcast.3.me_ref, s32[64]{0:T(128)S(1)} %fusion.owner_ref, f32[64,128]{1,0:T(8,128)S(1)} %bitcast.48, f32[64,128]{1,0:T(8,128)S(1)} %bitcast.47, f32[64,128]{1,0:T(8,128)S(1)} %bitcast.46), custom_call_target="tpu_custom_call" | custom-call | flops 1073741824 | bytes 4194304 | tf_op jit(solution)/shard_map/pallas_call | solution.py:26
  109.0 5.4 %collective-permute-done.20.refs_3_ = bf16[384,256]{1,0:T(8,128)(2,1)S(1)} collective-permute-done((bf16[384,256]{1,0:T(8,128)(2,1)S(1)}, bf16[384,256]{1,0:T(8,128)(2,1)S(1)}, u32[]{:S(2)}, u32[]{:S(2)}) %collective-permute-start.20) | collective-permute-done | bytes 196640 | tf_op jit(solution)/shard_map/ppermute | solution.py:369
  114.4 2.4 %shard_map.199 = f32[3072,128]{1,0:T(8,128)} custom-call(f32[3072,128]{1,0:T(8,128)S(1)} %get-tuple-element.35.u_ref, bf16[4,256,1024]{2,1,0:T(8,128)(2,1)S(1)} %shard_map.194.w_ref, bf16[384,256]{1,0:T(8,128)(2,1)S(1)} %shard_map.198.refs_0_, bf16[384,256]{1,0:T(8,128)(2,1)S(1)} %collective-permute-done.18.refs_1_, ...), custom_call_target="tpu_custom_call" | custom-call | flops 805306368 | bytes 8388608 | tf_op jit(solution)/shard_map/pallas_call | solution.py:26
  (75 shorter events, 20.2 us)
Async XLA Ops:
  2.2 64.2 %collective-permute-start.4 = (f32[4,16,128]{2,1,0:T(8,128)S(1)}, f32[4,16,128]{2,1,0:T(8,128)S(1)}, u32[]{:S(2)}, u32[]{:S(2)}) collective-permute-start(f32[4,16,128]{2,1,0:T(8,128)S(1)} %get-tuple-element.65), channel_id=1, source_target_pairs={{0,1},{1,2},{2,3},{3,0},{4,5},{5,6},{6,7},{7,4},{8,9},{9,10},{10,1... | collective-permute-start | bytes 98312 | tf_op jit(solution)/shard_map/ppermute | solution.py:369
  3.5 63.0 %collective-permute-start.5 = (f32[4,16,128]{2,1,0:T(8,128)S(1)}, f32[4,16,128]{2,1,0:T(8,128)S(1)}, u32[]{:S(2)}, u32[]{:S(2)}) collective-permute-start(f32[4,16,128]{2,1,0:T(8,128)S(1)} %get-tuple-element.65), channel_id=1, source_target_pairs={{0,2},{1,3},{2,0},{3,1},{4,6},{5,7},{6,4},{7,5},{8,10},{9,11},{10,... | collective-permute-start | bytes 98312 | tf_op jit(solution)/shard_map/ppermute | solution.py:369
  9.3 9.1 %collective-permute-start = (bf16[832,128]{1,0:T(8,128)(2,1)S(1)}, bf16[832,128]{1,0:T(8,128)(2,1)S(1)}, u32[]{:S(2)}, u32[]{:S(2)}) collective-permute-start(bf16[832,128]{1,0:T(8,128)(2,1)S(1)} %get-tuple-element.31), channel_id=1, source_target_pairs={{0,4},{4,8},{8,12},{1,5},{5,9},{9,13},{2,6},{6,10},{10,14},{3,7},{... | collective-permute-start | bytes 638984 | tf_op jit(solution)/shard_map/ppermute | solution.py:372
  10.6 7.8 %collective-permute-start.1 = (bf16[832,128]{1,0:T(8,128)(2,1)S(1)}, bf16[832,128]{1,0:T(8,128)(2,1)S(1)}, u32[]{:S(2)}, u32[]{:S(2)}) collective-permute-start(bf16[832,128]{1,0:T(8,128)(2,1)S(1)} %get-tuple-element.32), channel_id=1, source_target_pairs={{4,0},{8,4},{12,8},{5,1},{9,5},{13,9},{6,2},{10,6},{14,10},{7,3},{... | collective-permute-start | bytes 638984 | tf_op jit(solution)/shard_map/ppermute | solution.py:375
  18.6 7.6 %collective-permute-start.2 = (bf16[80,384]{1,0:T(8,128)(2,1)S(1)}, bf16[80,384]{1,0:T(8,128)(2,1)S(1)}, u32[]{:S(2)}, u32[]{:S(2)}) collective-permute-start(bf16[80,384]{1,0:T(8,128)(2,1)S(1)} %get-tuple-element.33), channel_id=1, source_target_pairs={{0,1},{1,2},{2,3},{3,0},{4,5},{5,6},{6,7},{7,4},{8,9},{9,10},{10,1... | collective-permute-start | bytes 184328 | tf_op jit(solution)/shard_map/ppermute | solution.py:369
  19.0 7.2 %collective-permute-start.3 = (bf16[80,384]{1,0:T(8,128)(2,1)S(1)}, bf16[80,384]{1,0:T(8,128)(2,1)S(1)}, u32[]{:S(2)}, u32[]{:S(2)}) collective-permute-start(bf16[80,384]{1,0:T(8,128)(2,1)S(1)} %get-tuple-element.34), channel_id=1, source_target_pairs={{0,3},{1,0},{2,1},{3,2},{4,7},{5,4},{6,5},{7,6},{8,11},{9,8},{10,9... | collective-permute-start | bytes 184328 | tf_op jit(solution)/shard_map/ppermute | solution.py:369
  26.2 16.5 %copy-start.15 = (bf16[2,512,512]{2,1,0:T(8,128)(2,1)S(1)}, bf16[2,512,512]{2,1,0:T(8,128)(2,1)}, u32[]{:S(2)}) copy-start(bf16[2,512,512]{2,1,0:T(8,128)(2,1)} %param.31) | copy-start | bytes 3145732
  37.3 21.7 %copy-start.9 = (bf16[192,512]{1,0:T(8,128)(2,1)S(1)}, bf16[192,512]{1,0:T(8,128)(2,1)}, u32[]{:S(2)}) copy-start(bf16[192,512]{1,0:T(8,128)(2,1)} %refs_4_.1) | copy-start | bytes 589828
  37.3 6.3 %collective-permute-start.7 = (bf16[256,384]{1,0:T(8,128)(2,1)S(1)}, bf16[256,384]{1,0:T(8,128)(2,1)S(1)}, u32[]{:S(2)}, u32[]{:S(2)}) collective-permute-start(bf16[256,384]{1,0:T(8,128)(2,1)S(1)} %get-tuple-element.37), channel_id=1, source_target_pairs={{0,1},{1,2},{2,3},{3,0},{4,5},{5,6},{6,7},{7,4},{8,9},{9,10},{10,1... | collective-permute-start | bytes 589832 | tf_op jit(solution)/shard_map/ppermute | solution.py:369
  37.6 17.3 %collective-permute-start.8 = (bf16[256,384]{1,0:T(8,128)(2,1)S(1)}, bf16[256,384]{1,0:T(8,128)(2,1)S(1)}, u32[]{:S(2)}, u32[]{:S(2)}) collective-permute-start(bf16[256,384]{1,0:T(8,128)(2,1)S(1)} %get-tuple-element.38), channel_id=1, source_target_pairs={{0,2},{1,3},{2,0},{3,1},{4,6},{5,7},{6,4},{7,5},{8,10},{9,11},{10,... | collective-permute-start | bytes 589832 | tf_op jit(solution)/shard_map/ppermute | solution.py:369
  42.7 16.4 %collective-permute-start.9 = (bf16[256,384]{1,0:T(8,128)(2,1)S(1)}, bf16[256,384]{1,0:T(8,128)(2,1)S(1)}, u32[]{:S(2)}, u32[]{:S(2)}) collective-permute-start(bf16[256,384]{1,0:T(8,128)(2,1)S(1)} %get-tuple-element.39), channel_id=1, source_target_pairs={{0,3},{1,0},{2,1},{3,2},{4,7},{5,4},{6,5},{7,6},{8,11},{9,8},{10,9... | collective-permute-start | bytes 589832 | tf_op jit(solution)/shard_map/ppermute | solution.py:369
  43.6 24.2 %collective-permute-start.6 = (f32[4,16,128]{2,1,0:T(8,128)S(1)}, f32[4,16,128]{2,1,0:T(8,128)S(1)}, u32[]{:S(2)}, u32[]{:S(2)}) collective-permute-start(f32[4,16,128]{2,1,0:T(8,128)S(1)} %get-tuple-element.65), channel_id=1, source_target_pairs={{0,3},{1,0},{2,1},{3,2},{4,7},{5,4},{6,5},{7,6},{8,11},{9,8},{10,9... | collective-permute-start | bytes 98312 | tf_op jit(solution)/shard_map/ppermute | solution.py:369
  60.8 7.1 %collective-permute-start.10 = (bf16[96,512]{1,0:T(8,128)(2,1)S(1)}, bf16[96,512]{1,0:T(8,128)(2,1)S(1)}, u32[]{:S(2)}, u32[]{:S(2)}) collective-permute-start(bf16[96,512]{1,0:T(8,128)(2,1)S(1)} %get-tuple-element.45), channel_id=1, source_target_pairs={{0,4},{4,8},{8,12},{1,5},{5,9},{9,13},{2,6},{6,10},{10,14},{3,7},{... | collective-permute-start | bytes 294920 | tf_op jit(solution)/shard_map/ppermute | solution.py:372
  62.1 5.8 %collective-permute-start.11 = (bf16[96,512]{1,0:T(8,128)(2,1)S(1)}, bf16[96,512]{1,0:T(8,128)(2,1)S(1)}, u32[]{:S(2)}, u32[]{:S(2)}) collective-permute-start(bf16[96,512]{1,0:T(8,128)(2,1)S(1)} %get-tuple-element.46), channel_id=1, source_target_pairs={{4,0},{8,4},{12,8},{5,1},{9,5},{13,9},{6,2},{10,6},{14,10},{7,3},{... | collective-permute-start | bytes 294920 | tf_op jit(solution)/shard_map/ppermute | solution.py:375
  66.4 3.5 %collective-permute-start.12 = (bf16[96,512]{1,0:T(8,128)(2,1)S(1)}, bf16[96,512]{1,0:T(8,128)(2,1)S(1)}, u32[]{:S(2)}, u32[]{:S(2)}) collective-permute-start(bf16[96,512]{1,0:T(8,128)(2,1)S(1)} %get-tuple-element.47), channel_id=1, source_target_pairs={{0,1},{1,2},{2,3},{3,0},{4,5},{5,6},{6,7},{7,4},{8,9},{9,10},{10,1... | collective-permute-start | bytes 294920 | tf_op jit(solution)/shard_map/ppermute | solution.py:369
  66.4 4.6 %collective-permute-start.13 = (bf16[96,512]{1,0:T(8,128)(2,1)S(1)}, bf16[96,512]{1,0:T(8,128)(2,1)S(1)}, u32[]{:S(2)}, u32[]{:S(2)}) collective-permute-start(bf16[96,512]{1,0:T(8,128)(2,1)S(1)} %get-tuple-element.48), channel_id=1, source_target_pairs={{0,3},{1,0},{2,1},{3,2},{4,7},{5,4},{6,5},{7,6},{8,11},{9,8},{10,9... | collective-permute-start | bytes 294920 | tf_op jit(solution)/shard_map/ppermute | solution.py:369
  71.0 17.7 %copy-start.10 = (bf16[512,192]{0,1:T(8,128)(2,1)S(1)}, bf16[512,192]{0,1:T(8,128)(2,1)}, u32[]{:S(2)}) copy-start(bf16[512,192]{0,1:T(8,128)(2,1)} %param.32) | copy-start | bytes 589828
  76.6 7.7 %collective-permute-start.14 = (bf16[96,512]{1,0:T(8,128)(2,1)S(1)}, bf16[96,512]{1,0:T(8,128)(2,1)S(1)}, u32[]{:S(2)}, u32[]{:S(2)}) collective-permute-start(bf16[96,512]{1,0:T(8,128)(2,1)S(1)} %get-tuple-element.51), channel_id=1, source_target_pairs={{0,4},{4,8},{8,12},{1,5},{5,9},{9,13},{2,6},{6,10},{10,14},{3,7},{... | collective-permute-start | bytes 294920 | tf_op jit(solution)/shard_map/ppermute | solution.py:372
  77.9 6.4 %collective-permute-start.15 = (bf16[96,512]{1,0:T(8,128)(2,1)S(1)}, bf16[96,512]{1,0:T(8,128)(2,1)S(1)}, u32[]{:S(2)}, u32[]{:S(2)}) collective-permute-start(bf16[96,512]{1,0:T(8,128)(2,1)S(1)} %get-tuple-element.52), channel_id=1, source_target_pairs={{4,0},{8,4},{12,8},{5,1},{9,5},{13,9},{6,2},{10,6},{14,10},{7,3},{... | collective-permute-start | bytes 294920 | tf_op jit(solution)/shard_map/ppermute | solution.py:375
  82.2 3.7 %collective-permute-start.16 = (bf16[96,512]{1,0:T(8,128)(2,1)S(1)}, bf16[96,512]{1,0:T(8,128)(2,1)S(1)}, u32[]{:S(2)}, u32[]{:S(2)}) collective-permute-start(bf16[96,512]{1,0:T(8,128)(2,1)S(1)} %get-tuple-element.53), channel_id=1, source_target_pairs={{0,1},{1,2},{2,3},{3,0},{4,5},{5,6},{6,7},{7,4},{8,9},{9,10},{10,1... | collective-permute-start | bytes 294920 | tf_op jit(solution)/shard_map/ppermute | solution.py:369
  83.0 5.7 %collective-permute-start.17 = (bf16[96,512]{1,0:T(8,128)(2,1)S(1)}, bf16[96,512]{1,0:T(8,128)(2,1)S(1)}, u32[]{:S(2)}, u32[]{:S(2)}) collective-permute-start(bf16[96,512]{1,0:T(8,128)(2,1)S(1)} %get-tuple-element.54), channel_id=1, source_target_pairs={{0,3},{1,0},{2,1},{3,2},{4,7},{5,4},{6,5},{7,6},{8,11},{9,8},{10,9... | collective-permute-start | bytes 294920 | tf_op jit(solution)/shard_map/ppermute | solution.py:369
  93.5 15.4 %collective-permute-start.18 = (bf16[384,256]{1,0:T(8,128)(2,1)S(1)}, bf16[384,256]{1,0:T(8,128)(2,1)S(1)}, u32[]{:S(2)}, u32[]{:S(2)}) collective-permute-start(bf16[384,256]{1,0:T(8,128)(2,1)S(1)} %shard_map.198.refs_0_), channel_id=1, source_target_pairs={{0,1},{1,2},{2,3},{3,0},{4,5},{5,6},{6,7},{7,4},{8,9},{9,10},{10,1... | collective-permute-start | bytes 589832 | tf_op jit(solution)/shard_map/ppermute | solution.py:369
  94.3 14.6 %collective-permute-start.19 = (bf16[384,256]{1,0:T(8,128)(2,1)S(1)}, bf16[384,256]{1,0:T(8,128)(2,1)S(1)}, u32[]{:S(2)}, u32[]{:S(2)}) collective-permute-start(bf16[384,256]{1,0:T(8,128)(2,1)S(1)} %shard_map.198.refs_0_), channel_id=1, source_target_pairs={{0,2},{1,3},{2,0},{3,1},{4,6},{5,7},{6,4},{7,5},{8,10},{9,11},{10,... | collective-permute-start | bytes 589832 | tf_op jit(solution)/shard_map/ppermute | solution.py:369
  96.4 18.0 %collective-permute-start.20 = (bf16[384,256]{1,0:T(8,128)(2,1)S(1)}, bf16[384,256]{1,0:T(8,128)(2,1)S(1)}, u32[]{:S(2)}, u32[]{:S(2)}) collective-permute-start(bf16[384,256]{1,0:T(8,128)(2,1)S(1)} %shard_map.198.refs_0_), channel_id=1, source_target_pairs={{0,3},{1,0},{2,1},{3,2},{4,7},{5,4},{6,5},{7,6},{8,11},{9,8},{10,9... | collective-permute-start | bytes 589832 | tf_op jit(solution)/shard_map/ppermute | solution.py:369
  (14 other events, 45.6 us)
where the time goes:
time: 117 us
  Pallas kernels  44.3 us (38%)
  starting transfers between devices  36.7 us (31%)
  waiting for transfers between devices  25.8 us (22%)
  local copies, waits for them, and re-layouts  7.38 us (6%)
  other arithmetic  2.22 us (2%)
    pallas_call x10, Pallas kernels, call(): pl.pallas_call(kernel, out_shape=outs if single else tuple(outs), in_spec...  44.3 us
    ppermute x15, waiting for transfers between devices, shift(): return lax.ppermute(v, 'lon', [(i, (i + s) % lon) for i in range(lon)])  25.8 us
    ppermute x15, starting transfers between devices, shift(): return lax.ppermute(v, 'lon', [(i, (i + s) % lon) for i in range(lon)])  20.5 us
    ppermute x3, starting transfers between devices, down(): return lax.ppermute(v, 'lat', [(i + 1, i) for i in range(lat - 1)])  12.4 us
    ppermute x3, starting transfers between devices, up(): return lax.ppermute(v, 'lat', [(i, i + 1) for i in range(lat - 1)])  3.87 us
    unnamed x34, local copies, waits for them, and re-layouts  3.72 us
  transfers between devices with their start and end apart: 21, of which 8 were waited for; matrix products, arithmetic and copies ran while one was open for 3% of the time, Pallas kernels for 27%

commit v1 on v0

v1 whole, which is shorter than its diff:
```python
import functools

import jax
import jax.numpy as jnp
from jax import lax
from jax.experimental import pallas as pl
from jax.experimental.pallas import tpu as pltpu
from jax.sharding import PartitionSpec as P

F32, BF16, I32 = jnp.float32, jnp.bfloat16, jnp.int32
MIB = 1 << 20
NODE_DEV = 256


def dot(a, b, ca=1, cb=0):
    return lax.dot_general(a, b, (((ca,), (cb,)), ((), ())), preferred_element_type=F32)


def iota(shape, dim):
    return lax.broadcasted_iota(I32, shape, dim)


def call(kernel, outs, args, smem=0, away=0, small=0, scratch=(), vmem=32, cost=None):
    single = not isinstance(outs, (list, tuple))
    spaces = [pltpu.SMEM] * smem + [pl.ANY] * away + [pltpu.VMEM] * (len(args) - smem - away)
    if single:
        out_specs = pl.BlockSpec(memory_space=pltpu.VMEM)
    else:
        homes = [pltpu.VMEM] * (len(outs) - small) + [pltpu.SMEM] * small
        out_specs = tuple(pl.BlockSpec(memory_space=m) for m in homes)
    return pl.pallas_call(
        kernel,
        out_shape=outs if single else tuple(outs),
        in_specs=[pl.BlockSpec(memory_space=m) for m in spaces],
        out_specs=out_specs,
        scratch_shapes=list(scratch),
        compiler_params=pltpu.CompilerParams(vmem_limit_bytes=vmem * MIB),
        cost_estimate=cost,
    )(*args)


def cost(flops, bytes_accessed):
    return pl.CostEstimate(flops=int(flops), bytes_accessed=int(bytes_accessed), transcendentals=0)


def shape(dims, dtype):
    return jax.ShapeDtypeStruct(tuple(dims), dtype)


def split(v):
    hi = v.astype(BF16).astype(F32)
    return hi, v - hi


def pick_columns(width):
    row, lane = iota((16, width), 0), iota((16, width), 1)
    hit = (row == 0) & (lane == 0) | (row == 1) & (lane == 1)
    hit = hit | (row == 2) & (lane == width - 1) | (row == 3) & (lane == width - 2)
    return hit.astype(F32).astype(BF16)


def coefficients(we, wn, d):
    pe, ne = jnp.maximum(we, 0.0), jnp.minimum(we, 0.0)
    pn, nn = jnp.maximum(wn, 0.0), jnp.minimum(wn, 0.0)
    return 1.0 - pe + ne - pn + nn - 4.0 * d, pe + d, d - ne, pn + d, d - nn


def edge_kernel(rows, slots, me_ref, in_owner_ref, out_owner_ref, *refs):
    homes, (up_ref, down_ref, side_ref, rate_ref, x_ref, in_ref, *out_refs) = refs[:11], refs[11 : 17 + slots]
    halo_ref, block, taken, late, *tables, sems = refs[17 + slots :]
    held = [x_ref, *(rate_ref.at[j] for j in range(3)), halo_ref, *tables]
    copies = [pltpu.make_async_copy(a, b, sems.at[k]) for k, (a, b) in enumerate(zip(homes, held))]
    for copy in copies:
        copy.start()
    for copy in copies[1:]:
        copy.wait()
    sort_blocks(slots, me_ref[0], in_owner_ref, tables[:3], in_ref, taken)
    sort_blocks(slots, me_ref[0], out_owner_ref, tables[3:], late, taken)
    for s in range(slots):
        out_refs[s][...] = late[s]
    copies[0].wait()
    count = x_ref.shape[0] // rows
    width = x_ref.shape[1]
    wanted = halo_ref.shape[1]

    def row(r):
        return x_ref[pl.ds(r, count, stride=rows), :].astype(BF16)

    for out_ref, near, far, q in ((up_ref, rows - 1, rows - 2, 1), (down_ref, 0, 1, 0)):
        out_ref[0:count, :] = row(near)
        out_ref[count : 2 * count, :] = row(far)
        block[...] = jnp.zeros(block.shape, F32)
        for j in range(3):
            hi, lo = split(rate_ref[j, near : near + 1, :])
            block[j : j + 1, :] = hi
            block[j + 3 : j + 4, :] = lo
        block[6:7, 0:wanted] = halo_ref[q : q + 1, :].astype(F32)
        out_ref[2 * count : 2 * count + 16, :] = block[...].astype(BF16)
    lane = iota((rows, count), 1)
    for i, (c, q) in enumerate(((width - 1, 3), (0, 2))):
        side_ref[i, 2 * rows : 3 * rows, :] = jnp.zeros((rows, count), F32)
        side_ref[i, 2 * rows + 2 : 2 * rows + 3, 0:wanted] = halo_ref[q : q + 1, :].astype(F32)
        rates = jnp.zeros((rows, count), F32)
        for j in range(3):
            hi, lo = split(rate_ref[j][:, c : c + 1])
            rates = jnp.where(lane == j, hi, jnp.where(lane == j + 3, lo, rates))
        side_ref[i, 3 * rows : 4 * rows, :] = rates
    pick = pick_columns(width)
    for r in range(rows):
        got = dot(pick, row(r), 1, 1)
        for i, k in enumerate((2, 0)):
            side_ref[i, r : r + 1, :] = got[k : k + 1, :]
            side_ref[i, rows + r : rows + r + 1, :] = got[k + 1 : k + 2, :]


def side_kernel(rows, south_ref, north_ref, side_ref, east_ref, west_ref):
    count, width = side_ref.shape[2], south_ref.shape[1]
    pick = pick_columns(width)
    south = dot(pick, south_ref[0:count, :], 1, 1)
    north = dot(pick, north_ref[0:count, :], 1, 1)
    line = iota((4 * rows, count), 0)
    for i, (out_ref, k) in enumerate(((east_ref, 2), (west_ref, 0))):
        v = jnp.where(line == 2 * rows, south[k : k + 1, :], side_ref[i])
        out_ref[...] = jnp.where(line == 2 * rows + 1, north[k : k + 1, :], v).astype(BF16)


def sort_blocks(slots, me, owner_ref, lists, out_ref, taken):
    cap = out_ref.shape[1] // 3
    out_ref[...] = jnp.zeros(out_ref.shape, F32)
    for s in range(slots):
        taken[s] = 0

    @pl.loop(0, lists[0].shape[0])
    def _(b):
        s = lax.rem(owner_ref[b] - me + slots, slots)
        at = jnp.minimum(taken[s], cap - 1)
        taken[s] = at + 1
        for k in range(3):
            out_ref[s, pl.ds(k * cap + at, 1), :] = lists[k][pl.ds(b, 1), :].astype(F32)


def build_kernel(slots, *refs):
    list_refs, (out_ref, hot, spread) = refs[:-3], refs[-3:]
    nodes, cells = out_ref.shape[1], out_ref.shape[2]
    joint = len(list_refs) == 1
    cap, entries = list_refs[0].shape[-2] // 3, list_refs[0].shape[-1]
    node_ids = iota((nodes, entries), 0).astype(F32)
    cell_ids = iota((cells, entries), 0).astype(F32)

    def fill(s, ref):
        for c in range(cap):
            lanes = slice(c * entries, (c + 1) * entries)
            node, cell, weight = (ref[k * cap + c : k * cap + c + 1, :] for k in range(3))
            hot[:, lanes] = jnp.where(node_ids == node, 1.0, 0.0).astype(BF16)
            spread[:, lanes] = jnp.where(cell_ids == cell, weight, 0.0).astype(BF16)
        out_ref[s] = dot(hot[...], spread[...], 1, 1).astype(BF16)

    if joint:

        @pl.loop(0, slots)
        def _(s):
            fill(s, list_refs[0].at[s])
    else:
        for s in range(slots):
            fill(s, list_refs[s])


def build(slots, nodes, cells, lists):
    cap, entries = lists[0].shape[-2] // 3, lists[0].shape[-1]
    size = slots * nodes * cells
    return call(
        functools.partial(build_kernel, slots),
        shape((slots, nodes, cells), BF16),
        lists,
        scratch=[pltpu.VMEM((nodes, cap * entries), BF16), pltpu.VMEM((cells, cap * entries), BF16)],
        vmem=8 + 3 * size // MIB,
        cost=cost(2 * size * cap * entries, 4 * size),
    )


def step_kernel(
    rows, lat, slots,
    lat_ref, x_ref, wind_ref, side_ref, south_ref, north_ref, west_ref, east_ref, a_ref,
    u_ref, *rest,
):
    part_refs, (rate, ring, b1, b2, mid, flat) = rest[:slots], rest[slots:]
    count, width = side_ref.shape[2], x_ref.shape[1]
    at_south = jnp.where(lat_ref[0] == 0, 1.0, 0.0)
    at_north = jnp.where(lat_ref[0] == lat - 1, 1.0, 0.0)

    def mend(c0, cw, ce, cs, cn):
        line = iota(c0.shape, 0)
        ps, pn = jnp.where(line == 0, at_south, 0.0), jnp.where(line == rows - 1, at_north, 0.0)
        return c0 + ps * cs + pn * cn, cw, ce, cs * (1.0 - ps), cn * (1.0 - pn)

    own = mend(*coefficients(wind_ref[0], wind_ref[1], wind_ref[2]))
    outer = []
    for ref in (south_ref, north_ref):
        v = ref[2 * count : 2 * count + 16, :].astype(F32)
        outer.append(coefficients(*(v[j : j + 1, :] + v[j + 3 : j + 4, :] for j in range(3))))
    for j in range(5):
        rate[j, 0:1, :] = outer[0][j]
        rate[j, 1 : rows + 1, :] = own[j]
        rate[j, rows + 1 : rows + 2, :] = outer[1][j]

    west, east = west_ref[...].astype(F32), east_ref[...].astype(F32)
    w1, w2, w_corner, w_rate = (west[k * rows : (k + 1) * rows, :] for k in range(4))
    e1, e2, e_corner, e_rate = (east[k * rows : (k + 1) * rows, :] for k in range(4))

    half = ring.shape[0] // 2

    def place(out_ref, lines):
        k, col = iota((2 * half, lines * width), 0), iota((2 * half, lines * width), 1)
        hit = jnp.where(k < half, k * width, (k - half) * width + width - 1) == col
        out_ref[...] = dot(ring[...].astype(BF16), jnp.where(hit, 1.0, 0.0).astype(BF16), 0, 0)

    ring[...] = jnp.zeros(ring.shape, F32)
    for base, corner, near, j, c in ((0, w_corner, w1, 1, 0), (half, e_corner, e1, 2, width - 1)):
        ring[base : base + 1, :] = outer[0][j][:, c : c + 1] * corner[0:1, :]
        ring[base + 1 : base + 1 + rows, :] = own[j][:, c : c + 1] * near
        ring[base + 1 + rows : base + 2 + rows, :] = outer[1][j][:, c : c + 1] * corner[1:2, :]
    place(b1, rows + 2)

    def ring_col(rates, corner, v, out_w, out_e):
        k0, kw, ke, ks, kn = mend(*coefficients(*(rates[:, j : j + 1] + rates[:, j + 3 : j + 4] for j in range(3))))
        line = iota(v.shape, 0)
        to_s = jnp.where(line == 0, corner[0:1, :], pltpu.roll(v, 1, 0))
        to_n = jnp.where(line == rows - 1, corner[1:2, :], pltpu.roll(v, rows - 1, 0))
        return k0 * v + kw * out_w + ke * out_e + ks * to_s + kn * to_n

    ring[...] = jnp.zeros(ring.shape, F32)
    ring[0:rows, :] = own[1][:, 0:1] * ring_col(w_rate, w_corner, w1, w2, side_ref[1, 0:rows, :])
    ring[half : half + rows, :] = own[2][:, width - 1 : width] * ring_col(
        e_rate, e_corner, e1, side_ref[0, 0:rows, :], e2
    )
    place(b2, rows)

    k, col = iota((2 * width, 2 * width), 0), iota((2 * width, 2 * width), 1)
    k = jnp.where(k < width, k, k - width)
    turn = jnp.where(jnp.where(col < width, col - 1, col - width + 1) == k, 1.0, 0.0).astype(BF16)

    def advance(line, v, below, above, b_ref, at):
        hi = v.astype(BF16)
        pair = jnp.concatenate([hi, (v - hi.astype(F32)).astype(BF16)], 1)
        turned = dot(pair, turn)
        c0, cw, ce, cs, cn = (rate[j, line + 1 : line + 2, :] for j in range(5))
        new = c0 * v + cw * turned[:, 0:width] + ce * turned[:, width : 2 * width]
        return new + cs * below + cn * above + b_ref[:, at * width : (at + 1) * width]

    def cell_row(r):
        if r < 0:
            return south_ref[(-1 - r) * count : -r * count, :].astype(F32)
        if r >= rows:
            return north_ref[(r - rows) * count : (r - rows + 1) * count, :].astype(F32)
        return x_ref[pl.ds(r, count, stride=rows), :]

    for r in range(-1, rows + 1):
        mid[r + 1] = advance(r, cell_row(r), cell_row(r - 1), cell_row(r + 1), b1, r + 1)
    for r in range(rows):
        new = advance(r, mid[r + 1], mid[r], mid[r + 2], b2, r)
        u_ref[:, r * width : (r + 1) * width] = new
        flat[:, r * width : (r + 1) * width] = new.astype(BF16)

    for s in range(slots):
        part_refs[s][...] = dot(a_ref[s], flat[...], 1, 1).astype(part_refs[s].dtype)


def silu(v):
    return 0.5 * v * (1.0 + jnp.tanh(0.5 * v))


def normalize(v):
    return (v * lax.rsqrt(jnp.mean(v * v, axis=-1, keepdims=True) + 1e-06)).astype(BF16)


def link_kernel(sender_ref, receiver_ref, gather_ref, scatter_ref, local_ref, order):
    edges, known = gather_ref.shape
    nodes = scatter_ref.shape[0]
    sender, receiver = sender_ref[...], receiver_ref[...]
    local = jnp.where(sender < nodes, 1.0, 0.0)
    order[...] = jnp.where(iota((edges, edges), 0) < iota((edges, edges), 1), 1.0, 0.0).astype(BF16)
    before = dot(jnp.broadcast_to(local, (16, edges)).astype(BF16), order[...])[0:1, :]
    total = jnp.sum(local)
    local_ref[0] = total.astype(I32)
    index = iota((1, edges), 1).astype(F32)
    place = jnp.where(sender < nodes, before, total + index - before)
    order[...] = jnp.where(iota((edges, edges), 0).astype(F32) == place, 1.0, 0.0).astype(BF16)
    line = iota((16, edges), 0)
    high = sender // nodes
    keys = jnp.where(line == 0, sender - high * nodes, jnp.where(line == 1, high, jnp.where(line == 2, receiver, 0)))
    keys = keys.astype(F32).astype(BF16)
    cols = dot(order[...], keys, 1, 1)
    sender, receiver = cols[:, 0:1] + nodes * cols[:, 1:2], cols[:, 2:3]
    lane = iota((edges, nodes), 1).astype(F32)
    gather_ref[:, 0:nodes] = jnp.where(sender == lane, 1.0, 0.0).astype(BF16)
    gather_ref[:, nodes : 2 * nodes] = jnp.where(receiver == lane, 1.0, 0.0).astype(BF16)
    rest = (iota((edges, known - 2 * nodes), 1) + nodes).astype(F32)
    gather_ref[:, 2 * nodes :] = jnp.where(sender == rest, 1.0, 0.0).astype(BF16)
    row = dot(keys, order[...], 1, 1)[2:3, :]
    scatter_ref[...] = jnp.where(row == iota((nodes, edges), 0).astype(F32), 1.0, 0.0).astype(BF16)


def project(m, hidden, owed, ws, wr, table_ref, out_refs, wanted, nodes):
    normed = normalize(hidden)
    source = dot(normed, ws).astype(BF16)
    table_ref[m, 0:nodes, :] = source
    table_ref[m, nodes : 2 * nodes, :] = dot(normed, wr).astype(BF16)
    for q in range(4):
        out_refs[q][m * wanted : (m + 1) * wanted, :] = dot(owed[q], source).astype(BF16)


def owed_kernel(rows, wanted, south_ref, north_ref, west_ref, east_ref, enc_ref, owed_ref, pad_ref):
    nodes = owed_ref.shape[1]
    count = west_ref.shape[1]
    lists = [ref[2 * count : 2 * count + 16, :].astype(F32)[6:7, :] for ref in (south_ref, north_ref)]
    lists += [ref[2 * rows : 4 * rows, 0:128].astype(F32)[2:3, :] for ref in (west_ref, east_ref)]
    for q in range(4):
        hot = jnp.where(iota((nodes, 128), 0).astype(F32) == lists[q], 1.0, 0.0)
        owed_ref[q * wanted : (q + 1) * wanted, :] = hot.T[0:wanted, :].astype(BF16)
    quantities = enc_ref.shape[0]
    pad_ref[...] = jnp.zeros(pad_ref.shape, BF16)
    for m in range(pad_ref.shape[0]):
        pad_ref[m, m * quantities : (m + 1) * quantities, :] = enc_ref[...]


def encode_kernel(slots, wanted, *refs):
    part_refs = refs[:slots]
    pad_ref, ws_ref, wr_ref, owed_ref, hidden_ref, table_ref, *out_refs = refs[slots:]
    nodes = part_refs[0].shape[0]
    owed = [owed_ref[q * wanted : (q + 1) * wanted, :] for q in range(4)]
    total = part_refs[0][...].astype(F32)
    for ref in part_refs[1:]:
        total = total + ref[...].astype(F32)
    total = total.astype(BF16)
    for m in range(hidden_ref.shape[0]):
        hidden = silu(dot(total, pad_ref[m]))
        hidden_ref[m] = hidden
        project(m, hidden, owed, ws_ref[0], wr_ref[0], table_ref, out_refs, wanted, nodes)


def messages(lo, hi, chunk, gather_ref, scatter_ref, depth, tables, sums_ref):
    step = chunk // 3

    @pl.loop(lo, hi)
    def _(c):
        at = pl.multiple_of(c * chunk, chunk)
        for m, table in enumerate(tables):
            found = [
                silu(dot(gather_ref[pl.ds(at + k, step), 0:depth], table[...])).astype(BF16)
                for k in range(0, chunk, step)
            ]
            sums_ref[m] += dot(scatter_ref[:, pl.ds(at, chunk)], jnp.concatenate(found, 0))


def early_kernel(chunk, local_ref, table_ref, gather_ref, scatter_ref, sums_ref):
    members, depth, _ = table_ref.shape
    sums_ref[...] = jnp.zeros(sums_ref.shape, F32)
    tables = [table_ref.at[m] for m in range(members)]
    messages(0, local_ref[0] // chunk, chunk, gather_ref, scatter_ref, depth, tables, sums_ref)


def layer_kernel(layer, last, wanted, chunk, *refs):
    local_ref, hidden_ref, table_ref, owed_ref, gather_ref, scatter_ref, early_ref = refs[:7]
    halo_refs, wu_ref = refs[7:11], refs[11]
    if last:
        dec_ref, out_ref, known, sums = refs[12:]
    else:
        ws_ref, wr_ref, next_hidden_ref, next_table_ref, *out_refs, known, sums = refs[12:]
    members, nodes, width = hidden_ref.shape
    edges, depth = gather_ref.shape
    sums[...] = early_ref[...]
    for m in range(members):
        known[m, 0 : 2 * nodes, :] = table_ref[m]
        for q in range(4):
            at = 2 * nodes + q * wanted
            known[m, at : at + wanted, :] = halo_refs[q][m * wanted : (m + 1) * wanted, :]
        at = 2 * nodes + 4 * wanted
        known[m, at:, :] = jnp.zeros((depth - at, width), BF16)
    tables = [known.at[m] for m in range(members)]
    messages(local_ref[0] // chunk, edges // chunk, chunk, gather_ref, scatter_ref, depth, tables, sums)
    if not last:
        owed = [owed_ref[q * wanted : (q + 1) * wanted, :] for q in range(4)]
    for m in range(members):
        hidden = hidden_ref[m] + dot(sums[m].astype(BF16), wu_ref[layer])
        if last:
            got = dot(dec_ref[...], normalize(hidden), 1, 1)
            out_ref[m * got.shape[0] : (m + 1) * got.shape[0], :] = got.astype(BF16)
        else:
            next_hidden_ref[m] = hidden
            project(m, hidden, owed, ws_ref[layer + 1], wr_ref[layer + 1], next_table_ref, out_refs, wanted, nodes)


def land_kernel(rows, slots, u_ref, w_ref, *refs):
    corr_refs, out_ref = refs[:slots], refs[slots]
    count, width = u_ref.shape[0], u_ref.shape[1] // rows
    total = u_ref[...]
    for s in range(slots):
        total = total + dot(corr_refs[s][...], w_ref[s])
    for r in range(rows):
        out_ref[pl.ds(r, count, stride=rows), :] = total[:, r * width : (r + 1) * width]


def body(
    fields, wind_east, wind_north, diffusion, inflow_owner, inflow_cell, inflow_node, inflow_weight,
    encoder, sender_weight, receiver_weight, update_weight, decoder, edge_sender, edge_receiver, halo_rows,
    outflow_owner, outflow_node, outflow_cell, outflow_weight,
):
    members, quantities, rows, width = fields.shape
    count, cells = members * quantities, rows * width
    lon, lat = lax.axis_size("lon"), lax.axis_size("lat")
    me = lax.axis_index("lon").astype(I32).reshape(1)
    lat_at = lax.axis_index("lat").astype(I32).reshape(1)
    blocks, entries = inflow_cell.shape
    hid = encoder.shape[1]
    layers = sender_weight.shape[0]
    edges = edge_sender.shape[-1]
    wanted = halo_rows.shape[-1]
    nodes = NODE_DEV
    cap = max(2, -(-2 * blocks // lon))

    def shift(v, s):
        return lax.ppermute(v, "lon", [(i, (i + s) % lon) for i in range(lon)])

    def up(v):
        return lax.ppermute(v, "lat", [(i, (i + 1) % lat) for i in range(lat)])

    def down(v):
        return lax.ppermute(v, "lat", [((i + 1) % lat, i) for i in range(lat)])

    x = fields.reshape(count * rows, width)
    halo = halo_rows.reshape(4, wanted)
    rates = (wind_east, wind_north, diffusion)
    tall = 2 * count + 16
    tables = (inflow_node, inflow_cell, inflow_weight, outflow_node, outflow_cell, outflow_weight)
    to_north, to_south, side, wind, x, in_lists, *out_lists = call(
        functools.partial(edge_kernel, rows, lon),
        [shape((tall, width), BF16), shape((tall, width), BF16), shape((2, 4 * rows, count), F32),
         shape((3, rows, width), F32), shape(x.shape, F32), shape((lon, 3 * cap, entries), F32)]
        + [shape((3 * cap, entries), F32)] * lon,
        (me, inflow_owner.reshape(blocks), outflow_owner.reshape(blocks), x, *rates, halo, *tables),
        smem=3,
        away=11,
        scratch=[
            pltpu.VMEM(halo.shape, I32),
            pltpu.VMEM((16, width), F32),
            pltpu.SMEM((lon,), I32),
            pltpu.VMEM((lon, 3 * cap, entries), F32),
            *(pltpu.VMEM(v.shape, v.dtype) for v in tables),
            pltpu.SemaphoreType.DMA((11,)),
        ],
        vmem=56,
        cost=cost(0, 8 * MIB),
    )
    south, north = up(to_north), down(to_south)
    into = build(lon, nodes, cells, (in_lists,))
    side, into = lax.optimization_barrier((side, into))
    to_east, to_west = call(
        functools.partial(side_kernel, rows),
        (shape((4 * rows, count), BF16), shape((4 * rows, count), BF16)),
        (south, north, side),
        vmem=4,
        cost=cost(0, 4 * MIB),
    )
    west, east = shift(to_east, 1), shift(to_west, lon - 1)

    u, *parts = call(
        functools.partial(step_kernel, rows, lat, lon),
        [shape((count, cells), F32)] + [shape((nodes, count), F32)] + [shape((nodes, count), BF16)] * (lon - 1),
        (lat_at, x, wind, side, south, north, west, east, into),
        smem=1,
        scratch=[
            pltpu.VMEM((5, rows + 2, width), F32),
            pltpu.VMEM((32, count), F32),
            pltpu.VMEM((count, (rows + 2) * width), F32),
            pltpu.VMEM((count, cells), F32),
            pltpu.VMEM((rows + 2, count, width), F32),
            pltpu.VMEM((count, cells), BF16),
        ],
        vmem=14 + lon * 2,
        cost=cost(2 * lon * nodes * cells * count, 16 * MIB),
    )
    parts, edge_sender, edge_receiver = lax.optimization_barrier((parts, edge_sender, edge_receiver))
    parts = parts[:1] + [shift(parts[s], s) for s in range(1, lon)]

    known = 2 * nodes + 256 * -(-4 * wanted // 256)
    chunk = edges // 2
    gather, scatter, local = call(
        link_kernel,
        (shape((edges, known), BF16), shape((nodes, edges), BF16), shape((1,), I32)),
        (edge_sender.reshape(1, edges), edge_receiver.reshape(1, edges)),
        small=1,
        scratch=[pltpu.VMEM((edges, edges), BF16)],
        vmem=24,
        cost=cost(2 * edges * edges * 48, 8 * MIB),
    )
    scatter, out_lists = lax.optimization_barrier((scatter, out_lists))
    out_lists = [out_lists[0]] + [shift(out_lists[s], s) for s in range(1, lon)]
    parts, out_lists = lax.optimization_barrier((parts, out_lists))
    onto = build(lon, nodes, cells, out_lists)

    reply = [shape((members * wanted, hid), BF16)] * 4
    state = [shape((members, nodes, hid), F32), shape((members, 2 * nodes, hid), BF16)]
    owed, pad = call(
        functools.partial(owed_kernel, rows, wanted),
        (shape((4 * wanted, nodes), BF16), shape((members, count, hid), BF16)),
        (south, north, west, east, encoder),
        vmem=8,
        cost=cost(0, 4 * MIB),
    )
    hidden, table, *out = call(
        functools.partial(encode_kernel, lon, wanted),
        state + reply,
        (*parts, pad, sender_weight, receiver_weight, owed),
        vmem=16,
        cost=cost(2e9, 8 * MIB),
    )
    for layer in range(layers):
        halos = [up(out[1]), down(out[0]), shift(out[3], 1), shift(out[2], lon - 1)]
        early = call(
            functools.partial(early_kernel, chunk),
            shape((members, nodes, hid), F32),
            (local, table, gather, scatter),
            smem=1,
            vmem=16,
            cost=cost(3e9, 8 * MIB),
        )
        last = layer == layers - 1
        args = (local, hidden, table, owed, gather, scatter, early, *halos, update_weight)
        scratch = [pltpu.VMEM((members, known, hid), BF16), pltpu.VMEM((members, nodes, hid), F32)]
        kernel = functools.partial(layer_kernel, layer, last, wanted, chunk)
        if last:
            corr = call(
                kernel, shape((count, nodes), BF16), (*args, decoder.T), smem=1, scratch=scratch, vmem=20,
                cost=cost(4e9, 12 * MIB),
            )
        else:
            hidden, table, *out = call(
                kernel,
                state + reply,
                (*args, sender_weight, receiver_weight),
                smem=1,
                scratch=scratch,
                vmem=20,
                cost=cost(4e9, 12 * MIB),
            )
    corrs = [corr] + [shift(corr, s) for s in range(1, lon)]
    out = call(
        functools.partial(land_kernel, rows, lon),
        shape(x.shape, F32),
        (u, onto, *corrs),
        vmem=16 + lon,
        cost=cost(2 * lon * nodes * cells * count, 8 * MIB),
    )
    return out.reshape(members, quantities, rows, width)


def solution(mesh):
    tile, block, part = P("lat", "lon"), P(("lat", "lon"), None), P("lat", "lon", None)
    placed = (P("member", None, "lat", "lon"), tile, tile, tile, block, block, block, block)
    placed += (P(),) * 5 + (part, part, P("lat", "lon", None, None)) + (block,) * 4
    return jax.shard_map(
        body, mesh=mesh, in_specs=placed, out_specs=P("member", None, "lat", "lon"), check_vma=False
    )
```

time: 117 us -> 95.7 us (0.82)
  the two profiles are of different devices: /device:TPU:15 before, /device:TPU:0 now
where the time goes in v1:
time: 95.7 us; the launch traced here: 95.4 us
  Pallas kernels  37.6 us (39%)
  starting transfers between devices  28.3 us (30%)
  waiting for transfers between devices  27 us (28%)
  local copies, waits for them, and re-layouts  2.26 us (2%)
    pallas_call x13, Pallas kernels, call(): pl.pallas_call(kernel, out_shape=outs if single else tuple(outs), in_spec...  37.6 us
    ppermute x15, waiting for transfers between devices, shift(): return lax.ppermute(v, 'lon', [(i, (i + s) % lon) for i in range(lon)])  26.7 us
    ppermute x15, starting transfers between devices, shift(): return lax.ppermute(v, 'lon', [(i, (i + s) % lon) for i in range(lon)])  22.2 us
    ppermute x3, starting transfers between devices, down(): return lax.ppermute(v, 'lat', [((i + 1) % lat, i) for i in range(lat)])  5.45 us
    unnamed x30, local copies, waits for them, and re-layouts  2.26 us
  transfers between devices with their start and end apart: 21, of which 10 were waited for; matrix products, arithmetic and copies ran while one was open for 0% of the time, Pallas kernels for 18%

profile of v1, /device:TPU:0, one launch (start us, length us, event | category | flops | bytes accessed | tf_op | source)
XLA Modules:
  0.0 95.4 jit_solution(16108238459476575028)
XLA Ops:
  0.0 3.8 %shard_map.190 = (bf16[784,128]{1,0:T(8,128)(2,1)}, bf16[784,128]{1,0:T(8,128)(2,1)}, f32[2,32,384]{2,1,0:T(8,128)}, f32[3,8,128]{2,1,0:T(8,128)}, f32[3072,128]...) custom-call(s32[1]{0:T(128)} %bitcast.1.me_ref, ...), custom_call_target="tpu_custom_call" | custom-call | bytes 8388608 | tf_op jit(solution)/shard_map/pallas_call | solution.py:31
  4.4 2.0 %collective-permute-start.1 = (bf16[784,128]{1,0:T(8,128)(2,1)}, bf16[784,128]{1,0:T(8,128)(2,1)S(1)}, u32[]{:S(2)}, u32[]{:S(2)}) collective-permute-start(bf16[784,128]{1,0:T(8,128)(2,1)} %get-tuple-element.66), channel_id=1, source_target_pairs={{4,0},{8,4},{12,8},{0,12},{5,1},{9,5},{13,9},{1,13},{6,2},{10,6},{... | collective-permute-start | bytes 602120 | tf_op jit(solution)/shard_map/ppermute | solution.py:428
  7.1 4.5 %shard_map.191.a_ref = bf16[4,256,1024]{2,1,0:T(8,128)(2,1)S(1)} custom-call(f32[4,24,128]{2,1,0:T(8,128)S(1)} %copy-done.8), custom_call_target="tpu_custom_call" | custom-call | flops 2147483648 | bytes 4194304 | tf_op jit(solution)/shard_map/pallas_call | solution.py:31
  12.1 2.0 %collective-permute-start.2 = (bf16[32,384]{1,0:T(8,128)(2,1)S(1)}, bf16[32,384]{1,0:T(8,128)(2,1)S(1)}, u32[]{:S(2)}, u32[]{:S(2)}) collective-permute-start(bf16[32,384]{1,0:T(8,128)(2,1)S(1)} %get-tuple-element.67), channel_id=1, source_target_pairs={{0,1},{1,2},{2,3},{3,0},{4,5},{5,6},{6,7},{7,4},{8,9},{9,10},{10,1... | collective-permute-start | bytes 73736 | tf_op jit(solution)/shard_map/ppermute | solution.py:422
  14.2 2.1 %collective-permute-start.3 = (bf16[32,384]{1,0:T(8,128)(2,1)S(1)}, bf16[32,384]{1,0:T(8,128)(2,1)S(1)}, u32[]{:S(2)}, u32[]{:S(2)}) collective-permute-start(bf16[32,384]{1,0:T(8,128)(2,1)S(1)} %get-tuple-element.68), channel_id=1, source_target_pairs={{0,3},{1,0},{2,1},{3,2},{4,7},{5,4},{6,5},{7,6},{8,11},{9,8},{10,9... | collective-permute-start | bytes 73736 | tf_op jit(solution)/shard_map/ppermute | solution.py:422
  16.2 1.9 %collective-permute-done.2.west_ref = bf16[32,384]{1,0:T(8,128)(2,1)S(1)} collective-permute-done((bf16[32,384]{1,0:T(8,128)(2,1)S(1)}, bf16[32,384]{1,0:T(8,128)(2,1)S(1)}, u32[]{:S(2)}, u32[]{:S(2)}) %collective-permute-start.2) | collective-permute-done | bytes 24608 | tf_op jit(solution)/shard_map/ppermute | solution.py:422
  19.7 4.1 %shard_map.193 = (f32[384,1024]{1,0:T(8,128)S(1)}, f32[256,384]{1,0:T(8,128)S(1)}, bf16[256,384]{1,0:T(8,128)(2,1)S(1)}, bf16[256,384]{1,0:T(8,128)(2,1)S(1)}, bf16[256,384]{1,0:T(8,128)(2,1)S(1)}) custom-call(s32[1]{0:T(128)} %bitcast.lat_ref, f32[3072,128]{1,0:T(8,128)S(1)} %copy-done, f32[3,8,128]{2,1,0:T(8,128)S(1)} %copy-done.3, ...), custom_call_target="tpu_custom_call" | custom-call | flops 805306368 | bytes 16777216 | tf_op jit(solution)/shard_map/pallas_call | solution.py:31
  25.2 2.8 %collective-permute-start.5 = (bf16[256,384]{1,0:T(8,128)(2,1)S(1)}, bf16[256,384]{1,0:T(8,128)(2,1)S(1)}, u32[]{:S(2)}, u32[]{:S(2)}) collective-permute-start(bf16[256,384]{1,0:T(8,128)(2,1)S(1)} %get-tuple-element.77), channel_id=1, source_target_pairs={{0,2},{1,3},{2,0},{3,1},{4,6},{5,7},{6,4},{7,5},{8,10},{9,11},{10,... | collective-permute-start | bytes 589832 | tf_op jit(solution)/shard_map/ppermute | solution.py:422
  29.2 3.6 %shard_map.194 = (bf16[1536,768]{1,0:T(8,128)(2,1)S(1)}, bf16[256,1536]{1,0:T(8,128)(2,1)S(1)}, s32[1]{0:T(128)}) custom-call(s32[1,1536]{1,0:T(1,128)S(1)} %bitcast.11, s32[1,1536]{1,0:T(1,128)S(1)} %bitcast.12), custom_call_target="tpu_custom_call" | custom-call | flops 226492416 | bytes 8388608 | tf_op jit(solution)/shard_map/pallas_call | solution.py:31
  33.9 6.8 %collective-permute-done.7.refs_1_ = f32[24,128]{1,0:T(8,128)S(1)} collective-permute-done((f32[24,128]{1,0:T(8,128)S(1)}, f32[24,128]{1,0:T(8,128)S(1)}, u32[]{:S(2)}, u32[]{:S(2)}) %collective-permute-start.7) | collective-permute-done | bytes 12320 | tf_op jit(solution)/shard_map/ppermute | solution.py:422
  40.8 4.4 %collective-permute-done.8.refs_2_ = f32[24,128]{1,0:T(8,128)S(1)} collective-permute-done((f32[24,128]{1,0:T(8,128)S(1)}, f32[24,128]{1,0:T(8,128)S(1)}, u32[]{:S(2)}, u32[]{:S(2)}) %collective-permute-start.8) | collective-permute-done | bytes 12320 | tf_op jit(solution)/shard_map/ppermute | solution.py:422
  45.3 1.7 %shard_map.197 = (f32[2,256,512]{2,1,0:T(8,128)S(1)}, bf16[2,512,512]{2,1,0:T(8,128)(2,1)S(1)}, bf16[96,512]{1,0:T(8,128)(2,1)S(1)}, bf16[96,512]{1,0:T(8,128)(2...) custom-call(f32[256,384]{1,0:T(8,128)S(1)} %get-tuple-element.95.refs_0_, ...), custom_call_target="tpu_custom_call" | custom-call | flops 2000000000 | bytes 8388608 | tf_op jit(solution)/shard_map/pallas_call | solution.py:31
  47.1 1.7 %collective-permute-start.11 = (bf16[96,512]{1,0:T(8,128)(2,1)S(1)}, bf16[96,512]{1,0:T(8,128)(2,1)S(1)}, u32[]{:S(2)}, u32[]{:S(2)}) collective-permute-start(bf16[96,512]{1,0:T(8,128)(2,1)S(1)} %get-tuple-element.106), channel_id=1, source_target_pairs={{4,0},{8,4},{12,8},{0,12},{5,1},{9,5},{13,9},{1,13},{6,2},{10,6},{... | collective-permute-start | bytes 294920 | tf_op jit(solution)/shard_map/ppermute | solution.py:428
  48.8 2.4 %collective-permute-start.12 = (bf16[96,512]{1,0:T(8,128)(2,1)S(1)}, bf16[96,512]{1,0:T(8,128)(2,1)S(1)}, u32[]{:S(2)}, u32[]{:S(2)}) collective-permute-start(bf16[96,512]{1,0:T(8,128)(2,1)S(1)} %get-tuple-element.107), channel_id=1, source_target_pairs={{0,1},{1,2},{2,3},{3,0},{4,5},{5,6},{6,7},{7,4},{8,9},{9,10},{10,1... | collective-permute-start | bytes 294920 | tf_op jit(solution)/shard_map/ppermute | solution.py:422
  52.7 2.5 %shard_map.198.refs_6_ = f32[2,256,512]{2,1,0:T(8,128)S(1)} custom-call(s32[1]{0:T(128)} %get-tuple-element.94.local_ref.refs_0_, bf16[2,512,512]{2,1,0:T(8,128)(2,1)S(1)} %get-tuple-element.102.table_ref.refs_2_, bf16[1536,768]{1,0:T(8,128)(2,1)S(1)} %get-tuple-element.103.gather_ref.refs_4_, bf16[256,1536]{1,0:T(8,128)(2,1)S(1)} %get-tuple-element.104.scatter_ref.refs_5_), custom_call_target="tpu_custom_call" | custom-call | flops 3000000000 | bytes 8388608 | tf_op jit(solution)/shard_map/pallas_call | solution.py:31
  57.4 4.3 %shard_map.199 = (f32[2,256,512]{2,1,0:T(8,128)S(1)}, bf16[2,512,512]{2,1,0:T(8,128)(2,1)S(1)}, bf16[96,512]{1,0:T(8,128)(2,1)S(1)}, bf16[96,512]{1,0:T(8,128)(2...) custom-call(s32[1]{0:T(128)} %get-tuple-element.94.local_ref.refs_0_, ...), custom_call_target="tpu_custom_call" | custom-call | flops 4000000000 | bytes 12582912 | tf_op jit(solution)/shard_map/pallas_call | solution.py:31
  61.8 1.7 %collective-permute-start.15 = (bf16[96,512]{1,0:T(8,128)(2,1)S(1)}, bf16[96,512]{1,0:T(8,128)(2,1)S(1)}, u32[]{:S(2)}, u32[]{:S(2)}) collective-permute-start(bf16[96,512]{1,0:T(8,128)(2,1)S(1)} %get-tuple-element.112), channel_id=1, source_target_pairs={{4,0},{8,4},{12,8},{0,12},{5,1},{9,5},{13,9},{1,13},{6,2},{10,6},{... | collective-permute-start | bytes 294920 | tf_op jit(solution)/shard_map/ppermute | solution.py:428
  64.2 3.1 %collective-permute-start.17 = (bf16[96,512]{1,0:T(8,128)(2,1)S(1)}, bf16[96,512]{1,0:T(8,128)(2,1)S(1)}, u32[]{:S(2)}, u32[]{:S(2)}) collective-permute-start(bf16[96,512]{1,0:T(8,128)(2,1)S(1)} %get-tuple-element.114), channel_id=1, source_target_pairs={{0,3},{1,0},{2,1},{3,2},{4,7},{5,4},{6,5},{7,6},{8,11},{9,8},{10,9... | collective-permute-start | bytes 294920 | tf_op jit(solution)/shard_map/ppermute | solution.py:422
  67.4 2.2 %shard_map.200.refs_6_ = f32[2,256,512]{2,1,0:T(8,128)S(1)} custom-call(s32[1]{0:T(128)} %get-tuple-element.94.local_ref.refs_0_, bf16[2,512,512]{2,1,0:T(8,128)(2,1)S(1)} %get-tuple-element.110.table_ref.refs_2_, bf16[1536,768]{1,0:T(8,128)(2,1)S(1)} %get-tuple-element.103.gather_ref.refs_4_, bf16[256,1536]{1,0:T(8,128)(2,1)S(1)} %get-tuple-element.104.scatter_ref.refs_5_), custom_call_target="tpu_custom_call" | custom-call | flops 3000000000 | bytes 8388608 | tf_op jit(solution)/shard_map/pallas_call | solution.py:31
  70.3 3.8 %shard_map.201.refs_0_ = bf16[384,256]{1,0:T(8,128)(2,1)S(1)} custom-call(s32[1]{0:T(128)} %get-tuple-element.94.local_ref.refs_0_, f32[2,256,512]{2,1,0:T(8,128)S(1)} %get-tuple-element.109.refs_1_, bf16[2,512,512]{2,1,0:T(8,128)(2,1)S(1)} %get-tuple-element.110.table_ref.refs_2_, bf16[192,256]{1,0:T(8,128)(2,1)S(1)} %get-tuple-element.100.refs_7_.refs_3_, ...), custom_call_target="tpu_custom_call" | custom-call | flops 4000000000 | bytes 12582912 | tf_op jit(solution)/shard_map/pallas_call | solution.py:31
  74.2 3.5 %collective-permute-start.20 = (bf16[384,256]{1,0:T(8,128)(2,1)S(1)}, bf16[384,256]{1,0:T(8,128)(2,1)S(1)}, u32[]{:S(2)}, u32[]{:S(2)}) collective-permute-start(bf16[384,256]{1,0:T(8,128)(2,1)S(1)} %shard_map.201.refs_0_), channel_id=1, source_target_pairs={{0,3},{1,0},{2,1},{3,2},{4,7},{5,4},{6,5},{7,6},{8,11},{9,8},{10,9... | collective-permute-start | bytes 589832 | tf_op jit(solution)/shard_map/ppermute | solution.py:422
  78.3 4.4 %shard_map.195.w_ref = bf16[4,256,1024]{2,1,0:T(8,128)(2,1)S(1)} custom-call(f32[24,128]{1,0:T(8,128)S(1)} %copy-done.9, f32[24,128]{1,0:T(8,128)S(1)} %collective-permute-done.7.refs_1_, f32[24,128]{1,0:T(8,128)S(1)} %collective-permute-done.8.refs_2_, f32[24,128]{1,0:T(8,128)S(1)} %collective-permute-done.9.refs_3_), custom_call_target="tpu_custom_call" | custom-call | flops 2147483648 | bytes 4194304 | tf_op jit(solution)/shard_map/pallas_call | solution.py:31
  83.0 10.2 %collective-permute-done.19.refs_2_ = bf16[384,256]{1,0:T(8,128)(2,1)S(1)} collective-permute-done((bf16[384,256]{1,0:T(8,128)(2,1)S(1)}, bf16[384,256]{1,0:T(8,128)(2,1)S(1)}, u32[]{:S(2)}, u32[]{:S(2)}) %collective-permute-start.19) | collective-permute-done | bytes 196640 | tf_op jit(solution)/shard_map/ppermute | solution.py:422
  93.2 2.2 %shard_map.202 = f32[3072,128]{1,0:T(8,128)} custom-call(f32[384,1024]{1,0:T(8,128)S(1)} %get-tuple-element.70.u_ref, bf16[4,256,1024]{2,1,0:T(8,128)(2,1)S(1)} %shard_map.195.w_ref, bf16[384,256]{1,0:T(8,128)(2,1)S(1)} %shard_map.201.refs_0_, bf16[384,256]{1,0:T(8,128)(2,1)S(1)} %collective-permute-done.18.refs_1_, ...), custom_call_target="tpu_custom_call" | custom-call | flops 805306368 | bytes 8388608 | tf_op jit(solution)/shard_map/pallas_call | solution.py:31
  (61 shorter events, 13.2 us)
Async XLA Ops:
  3.9 7.8 %collective-permute-start = (bf16[784,128]{1,0:T(8,128)(2,1)}, bf16[784,128]{1,0:T(8,128)(2,1)S(1)}, u32[]{:S(2)}, u32[]{:S(2)}) collective-permute-start(bf16[784,128]{1,0:T(8,128)(2,1)} %get-tuple-element.65), channel_id=1, source_target_pairs={{0,4},{4,8},{8,12},{12,0},{1,5},{5,9},{9,13},{13,1},{2,6},{6,10},{... | collective-permute-start | bytes 602120 | tf_op jit(solution)/shard_map/ppermute | solution.py:425
  4.4 7.6 %collective-permute-start.1 = (bf16[784,128]{1,0:T(8,128)(2,1)}, bf16[784,128]{1,0:T(8,128)(2,1)S(1)}, u32[]{:S(2)}, u32[]{:S(2)}) collective-permute-start(bf16[784,128]{1,0:T(8,128)(2,1)} %get-tuple-element.66), channel_id=1, source_target_pairs={{4,0},{8,4},{12,8},{0,12},{5,1},{9,5},{13,9},{1,13},{6,2},{10,6},{... | collective-permute-start | bytes 602120 | tf_op jit(solution)/shard_map/ppermute | solution.py:428
  12.1 6.0 %collective-permute-start.2 = (bf16[32,384]{1,0:T(8,128)(2,1)S(1)}, bf16[32,384]{1,0:T(8,128)(2,1)S(1)}, u32[]{:S(2)}, u32[]{:S(2)}) collective-permute-start(bf16[32,384]{1,0:T(8,128)(2,1)S(1)} %get-tuple-element.67), channel_id=1, source_target_pairs={{0,1},{1,2},{2,3},{3,0},{4,5},{5,6},{6,7},{7,4},{8,9},{9,10},{10,1... | collective-permute-start | bytes 73736 | tf_op jit(solution)/shard_map/ppermute | solution.py:422
  14.2 4.1 %collective-permute-start.3 = (bf16[32,384]{1,0:T(8,128)(2,1)S(1)}, bf16[32,384]{1,0:T(8,128)(2,1)S(1)}, u32[]{:S(2)}, u32[]{:S(2)}) collective-permute-start(bf16[32,384]{1,0:T(8,128)(2,1)S(1)} %get-tuple-element.68), channel_id=1, source_target_pairs={{0,3},{1,0},{2,1},{3,2},{4,7},{5,4},{6,5},{7,6},{8,11},{9,8},{10,9... | collective-permute-start | bytes 73736 | tf_op jit(solution)/shard_map/ppermute | solution.py:422
  19.7 21.0 %copy-start.12 = (f32[24,128]{1,0:T(8,128)S(1)}, f32[24,128]{1,0:T(8,128)}, u32[]{:S(2)}) copy-start(f32[24,128]{1,0:T(8,128)} %get-tuple-element.89) | copy-start | bytes 36868
  19.7 25.6 %copy-start.4 = (bf16[2,512,512]{2,1,0:T(8,128)(2,1)S(1)}, bf16[2,512,512]{2,1,0:T(8,128)(2,1)}, u32[]{:S(2)}) copy-start(bf16[2,512,512]{2,1,0:T(8,128)(2,1)} %refs_12_.1) | copy-start | bytes 3145732
  19.7 25.6 %copy-start.5 = (bf16[2,512,512]{2,1,0:T(8,128)(2,1)S(1)}, bf16[2,512,512]{2,1,0:T(8,128)(2,1)}, u32[]{:S(2)}) copy-start(bf16[2,512,512]{2,1,0:T(8,128)(2,1)} %refs_13_.1) | copy-start | bytes 3145732
  23.9 21.4 %collective-permute-start.4 = (bf16[256,384]{1,0:T(8,128)(2,1)S(1)}, bf16[256,384]{1,0:T(8,128)(2,1)S(1)}, u32[]{:S(2)}, u32[]{:S(2)}) collective-permute-start(bf16[256,384]{1,0:T(8,128)(2,1)S(1)} %get-tuple-element.76), channel_id=1, source_target_pairs={{0,1},{1,2},{2,3},{3,0},{4,5},{5,6},{6,7},{7,4},{8,9},{9,10},{10,1... | collective-permute-start | bytes 589832 | tf_op jit(solution)/shard_map/ppermute | solution.py:422
  25.2 20.0 %collective-permute-start.5 = (bf16[256,384]{1,0:T(8,128)(2,1)S(1)}, bf16[256,384]{1,0:T(8,128)(2,1)S(1)}, u32[]{:S(2)}, u32[]{:S(2)}) collective-permute-start(bf16[256,384]{1,0:T(8,128)(2,1)S(1)} %get-tuple-element.77), channel_id=1, source_target_pairs={{0,2},{1,3},{2,0},{3,1},{4,6},{5,7},{6,4},{7,5},{8,10},{9,11},{10,... | collective-permute-start | bytes 589832 | tf_op jit(solution)/shard_map/ppermute | solution.py:422
  28.1 17.2 %collective-permute-start.6 = (bf16[256,384]{1,0:T(8,128)(2,1)S(1)}, bf16[256,384]{1,0:T(8,128)(2,1)S(1)}, u32[]{:S(2)}, u32[]{:S(2)}) collective-permute-start(bf16[256,384]{1,0:T(8,128)(2,1)S(1)} %get-tuple-element.78), channel_id=1, source_target_pairs={{0,3},{1,0},{2,1},{3,2},{4,7},{5,4},{6,5},{7,6},{8,11},{9,8},{10,9... | collective-permute-start | bytes 589832 | tf_op jit(solution)/shard_map/ppermute | solution.py:422
  32.8 7.9 %collective-permute-start.7 = (f32[24,128]{1,0:T(8,128)S(1)}, f32[24,128]{1,0:T(8,128)S(1)}, u32[]{:S(2)}, u32[]{:S(2)}) collective-permute-start(f32[24,128]{1,0:T(8,128)S(1)} %copy-done.14), channel_id=1, source_target_pairs={{0,1},{1,2},{2,3},{3,0},{4,5},{5,6},{6,7},{7,4},{8,9},{9,10},{10,1... | collective-permute-start | bytes 36872 | tf_op jit(solution)/shard_map/ppermute | solution.py:422
  33.8 11.5 %collective-permute-start.8 = (f32[24,128]{1,0:T(8,128)S(1)}, f32[24,128]{1,0:T(8,128)S(1)}, u32[]{:S(2)}, u32[]{:S(2)}) collective-permute-start(f32[24,128]{1,0:T(8,128)S(1)} %copy-done.13), channel_id=1, source_target_pairs={{0,2},{1,3},{2,0},{3,1},{4,6},{5,7},{6,4},{7,5},{8,10},{9,11},{10,... | collective-permute-start | bytes 36872 | tf_op jit(solution)/shard_map/ppermute | solution.py:422
  40.7 4.6 %collective-permute-start.9 = (f32[24,128]{1,0:T(8,128)S(1)}, f32[24,128]{1,0:T(8,128)S(1)}, u32[]{:S(2)}, u32[]{:S(2)}) collective-permute-start(f32[24,128]{1,0:T(8,128)S(1)} %copy-done.12), channel_id=1, source_target_pairs={{0,3},{1,0},{2,1},{3,2},{4,7},{5,4},{6,5},{7,6},{8,11},{9,8},{10,9... | collective-permute-start | bytes 36872 | tf_op jit(solution)/shard_map/ppermute | solution.py:422
  47.0 8.1 %collective-permute-start.10 = (bf16[96,512]{1,0:T(8,128)(2,1)S(1)}, bf16[96,512]{1,0:T(8,128)(2,1)S(1)}, u32[]{:S(2)}, u32[]{:S(2)}) collective-permute-start(bf16[96,512]{1,0:T(8,128)(2,1)S(1)} %get-tuple-element.105), channel_id=1, source_target_pairs={{0,4},{4,8},{8,12},{12,0},{1,5},{5,9},{9,13},{13,1},{2,6},{6,10},{... | collective-permute-start | bytes 294920 | tf_op jit(solution)/shard_map/ppermute | solution.py:425
  47.1 8.1 %collective-permute-start.11 = (bf16[96,512]{1,0:T(8,128)(2,1)S(1)}, bf16[96,512]{1,0:T(8,128)(2,1)S(1)}, u32[]{:S(2)}, u32[]{:S(2)}) collective-permute-start(bf16[96,512]{1,0:T(8,128)(2,1)S(1)} %get-tuple-element.106), channel_id=1, source_target_pairs={{4,0},{8,4},{12,8},{0,12},{5,1},{9,5},{13,9},{1,13},{6,2},{10,6},{... | collective-permute-start | bytes 294920 | tf_op jit(solution)/shard_map/ppermute | solution.py:428
  48.8 7.2 %collective-permute-start.12 = (bf16[96,512]{1,0:T(8,128)(2,1)S(1)}, bf16[96,512]{1,0:T(8,128)(2,1)S(1)}, u32[]{:S(2)}, u32[]{:S(2)}) collective-permute-start(bf16[96,512]{1,0:T(8,128)(2,1)S(1)} %get-tuple-element.107), channel_id=1, source_target_pairs={{0,1},{1,2},{2,3},{3,0},{4,5},{5,6},{6,7},{7,4},{8,9},{9,10},{10,1... | collective-permute-start | bytes 294920 | tf_op jit(solution)/shard_map/ppermute | solution.py:422
  51.3 6.1 %collective-permute-start.13 = (bf16[96,512]{1,0:T(8,128)(2,1)S(1)}, bf16[96,512]{1,0:T(8,128)(2,1)S(1)}, u32[]{:S(2)}, u32[]{:S(2)}) collective-permute-start(bf16[96,512]{1,0:T(8,128)(2,1)S(1)} %get-tuple-element.108), channel_id=1, source_target_pairs={{0,3},{1,0},{2,1},{3,2},{4,7},{5,4},{6,5},{7,6},{8,11},{9,8},{10,9... | collective-permute-start | bytes 294920 | tf_op jit(solution)/shard_map/ppermute | solution.py:422
  61.7 7.9 %collective-permute-start.14 = (bf16[96,512]{1,0:T(8,128)(2,1)S(1)}, bf16[96,512]{1,0:T(8,128)(2,1)S(1)}, u32[]{:S(2)}, u32[]{:S(2)}) collective-permute-start(bf16[96,512]{1,0:T(8,128)(2,1)S(1)} %get-tuple-element.111), channel_id=1, source_target_pairs={{0,4},{4,8},{8,12},{12,0},{1,5},{5,9},{9,13},{13,1},{2,6},{6,10},{... | collective-permute-start | bytes 294920 | tf_op jit(solution)/shard_map/ppermute | solution.py:425
  61.8 7.8 %collective-permute-start.15 = (bf16[96,512]{1,0:T(8,128)(2,1)S(1)}, bf16[96,512]{1,0:T(8,128)(2,1)S(1)}, u32[]{:S(2)}, u32[]{:S(2)}) collective-permute-start(bf16[96,512]{1,0:T(8,128)(2,1)S(1)} %get-tuple-element.112), channel_id=1, source_target_pairs={{4,0},{8,4},{12,8},{0,12},{5,1},{9,5},{13,9},{1,13},{6,2},{10,6},{... | collective-permute-start | bytes 294920 | tf_op jit(solution)/shard_map/ppermute | solution.py:428
  63.5 6.8 %collective-permute-start.16 = (bf16[96,512]{1,0:T(8,128)(2,1)S(1)}, bf16[96,512]{1,0:T(8,128)(2,1)S(1)}, u32[]{:S(2)}, u32[]{:S(2)}) collective-permute-start(bf16[96,512]{1,0:T(8,128)(2,1)S(1)} %get-tuple-element.113), channel_id=1, source_target_pairs={{0,1},{1,2},{2,3},{3,0},{4,5},{5,6},{6,7},{7,4},{8,9},{9,10},{10,1... | collective-permute-start | bytes 294920 | tf_op jit(solution)/shard_map/ppermute | solution.py:422
  64.2 6.1 %collective-permute-start.17 = (bf16[96,512]{1,0:T(8,128)(2,1)S(1)}, bf16[96,512]{1,0:T(8,128)(2,1)S(1)}, u32[]{:S(2)}, u32[]{:S(2)}) collective-permute-start(bf16[96,512]{1,0:T(8,128)(2,1)S(1)} %get-tuple-element.114), channel_id=1, source_target_pairs={{0,3},{1,0},{2,1},{3,2},{4,7},{5,4},{6,5},{7,6},{8,11},{9,8},{10,9... | collective-permute-start | bytes 294920 | tf_op jit(solution)/shard_map/ppermute | solution.py:422
  74.2 8.9 %collective-permute-start.20 = (bf16[384,256]{1,0:T(8,128)(2,1)S(1)}, bf16[384,256]{1,0:T(8,128)(2,1)S(1)}, u32[]{:S(2)}, u32[]{:S(2)}) collective-permute-start(bf16[384,256]{1,0:T(8,128)(2,1)S(1)} %shard_map.201.refs_0_), channel_id=1, source_target_pairs={{0,3},{1,0},{2,1},{3,2},{4,7},{5,4},{6,5},{7,6},{8,11},{9,8},{10,9... | collective-permute-start | bytes 589832 | tf_op jit(solution)/shard_map/ppermute | solution.py:422
  77.7 15.5 %collective-permute-start.19 = (bf16[384,256]{1,0:T(8,128)(2,1)S(1)}, bf16[384,256]{1,0:T(8,128)(2,1)S(1)}, u32[]{:S(2)}, u32[]{:S(2)}) collective-permute-start(bf16[384,256]{1,0:T(8,128)(2,1)S(1)} %shard_map.201.refs_0_), channel_id=1, source_target_pairs={{0,2},{1,3},{2,0},{3,1},{4,6},{5,7},{6,4},{7,5},{8,10},{9,11},{10,... | collective-permute-start | bytes 589832 | tf_op jit(solution)/shard_map/ppermute | solution.py:422
  77.7 15.5 %collective-permute-start.18 = (bf16[384,256]{1,0:T(8,128)(2,1)S(1)}, bf16[384,256]{1,0:T(8,128)(2,1)S(1)}, u32[]{:S(2)}, u32[]{:S(2)}) collective-permute-start(bf16[384,256]{1,0:T(8,128)(2,1)S(1)} %shard_map.201.refs_0_), channel_id=1, source_target_pairs={{0,1},{1,2},{2,3},{3,0},{4,5},{5,6},{6,7},{7,4},{8,9},{9,10},{10,1... | collective-permute-start | bytes 589832 | tf_op jit(solution)/shard_map/ppermute | solution.py:422
  (12 other events, 101.1 us)

commit v2 on v1

--- a/solution.py
+++ b/solution.py
@@ -9,6 +9,7 @@
 
 F32, BF16, I32 = jnp.float32, jnp.bfloat16, jnp.int32
 MIB = 1 << 20
+SCALE = 0.05
 NODE_DEV = 256
 
 
@@ -40,7 +41,7 @@
 
 
 def cost(flops, bytes_accessed):
-    return pl.CostEstimate(flops=int(flops), bytes_accessed=int(bytes_accessed), transcendentals=0)
+    return pl.CostEstimate(flops=int(flops * SCALE), bytes_accessed=int(bytes_accessed * SCALE), transcendentals=0)
 
 
 def shape(dims, dtype):
@@ -65,23 +66,20 @@
     return 1.0 - pe + ne - pn + nn - 4.0 * d, pe + d, d - ne, pn + d, d - nn
 
 
-def edge_kernel(rows, slots, me_ref, in_owner_ref, out_owner_ref, *refs):
-    homes, (up_ref, down_ref, side_ref, rate_ref, x_ref, in_ref, *out_refs) = refs[:11], refs[11 : 17 + slots]
-    halo_ref, block, taken, late, *tables, sems = refs[17 + slots :]
+def edge_kernel(rows, slots, me_ref, owner_ref, *refs):
+    homes, (up_ref, down_ref, side_ref, rate_ref, in_ref) = refs[:8], refs[8:13]
+    x_ref, halo_ref, block, taken, *tables, sems = refs[13:]
     held = [x_ref, *(rate_ref.at[j] for j in range(3)), halo_ref, *tables]
     copies = [pltpu.make_async_copy(a, b, sems.at[k]) for k, (a, b) in enumerate(zip(homes, held))]
     for copy in copies:
         copy.start()
     for copy in copies[1:]:
         copy.wait()
-    sort_blocks(slots, me_ref[0], in_owner_ref, tables[:3], in_ref, taken)
-    sort_blocks(slots, me_ref[0], out_owner_ref, tables[3:], late, taken)
-    for s in range(slots):
-        out_refs[s][...] = late[s]
+    sort_blocks(slots, me_ref[0], owner_ref, tables, in_ref, taken)
     copies[0].wait()
+    wanted = halo_ref.shape[1]
     count = x_ref.shape[0] // rows
     width = x_ref.shape[1]
-    wanted = halo_ref.shape[1]
 
     def row(r):
         return x_ref[pl.ds(r, count, stride=rows), :].astype(BF16)
@@ -124,45 +122,51 @@
         out_ref[...] = jnp.where(line == 2 * rows + 1, north[k : k + 1, :], v).astype(BF16)
 
 
-def sort_blocks(slots, me, owner_ref, lists, out_ref, taken):
-    cap = out_ref.shape[1] // 3
-    out_ref[...] = jnp.zeros(out_ref.shape, F32)
+def slot_of(owner, me, slots):
+    if slots & (slots - 1):
+        return lax.rem(owner - me + slots, slots)
+    return lax.bitwise_xor(owner, me)
+
+
+def sort_blocks(slots, me, owner_ref, lists, hold, taken):
+    cap = hold.shape[1] // 3
+    hold[...] = jnp.zeros(hold.shape, F32)
     for s in range(slots):
         taken[s] = 0
 
     @pl.loop(0, lists[0].shape[0])
     def _(b):
-        s = lax.rem(owner_ref[b] - me + slots, slots)
+        s = slot_of(owner_ref[b], me, slots)
         at = jnp.minimum(taken[s], cap - 1)
         taken[s] = at + 1
         for k in range(3):
-            out_ref[s, pl.ds(k * cap + at, 1), :] = lists[k][pl.ds(b, 1), :].astype(F32)
+            hold[s, pl.ds(k * cap + at, 1), :] = lists[k][pl.ds(b, 1), :].astype(F32)
+
+
+def sort_kernel(slots, me_ref, owner_ref, *refs):
+    out_refs, (hold, taken) = refs[3 : 3 + slots], refs[3 + slots :]
+    sort_blocks(slots, me_ref[0], owner_ref, refs[:3], hold, taken)
+    for s in range(slots):
+        out_refs[s][...] = hold[s]
 
 
 def build_kernel(slots, *refs):
     list_refs, (out_ref, hot, spread) = refs[:-3], refs[-3:]
     nodes, cells = out_ref.shape[1], out_ref.shape[2]
-    joint = len(list_refs) == 1
-    cap, entries = list_refs[0].shape[-2] // 3, list_refs[0].shape[-1]
+    if len(list_refs) < slots:
+        list_refs = [list_refs[0].at[s] for s in range(slots)]
+    cap, entries = list_refs[0].shape[0] // 3, list_refs[0].shape[1]
     node_ids = iota((nodes, entries), 0).astype(F32)
-    cell_ids = iota((cells, entries), 0).astype(F32)
-
-    def fill(s, ref):
+    cell_ids = iota((entries, cells), 1).astype(F32)
+    for s in range(slots):
+        ref = list_refs[s]
+        columns = ref[...].T
         for c in range(cap):
             lanes = slice(c * entries, (c + 1) * entries)
-            node, cell, weight = (ref[k * cap + c : k * cap + c + 1, :] for k in range(3))
-            hot[:, lanes] = jnp.where(node_ids == node, 1.0, 0.0).astype(BF16)
-            spread[:, lanes] = jnp.where(cell_ids == cell, weight, 0.0).astype(BF16)
-        out_ref[s] = dot(hot[...], spread[...], 1, 1).astype(BF16)
-
-    if joint:
-
-        @pl.loop(0, slots)
-        def _(s):
-            fill(s, list_refs[0].at[s])
-    else:
-        for s in range(slots):
-            fill(s, list_refs[s])
+            cell, weight = (columns[:, k * cap + c : k * cap + c + 1] for k in (1, 2))
+            hot[:, lanes] = jnp.where(node_ids == ref[c : c + 1, :], 1.0, 0.0).astype(BF16)
+            spread[lanes, :] = jnp.where(cell_ids == cell, weight, 0.0).astype(BF16)
+        out_ref[s] = dot(hot[...], spread[...]).astype(BF16)
 
 
 def build(slots, nodes, cells, lists):
@@ -172,28 +176,36 @@
         functools.partial(build_kernel, slots),
         shape((slots, nodes, cells), BF16),
         lists,
-        scratch=[pltpu.VMEM((nodes, cap * entries), BF16), pltpu.VMEM((cells, cap * entries), BF16)],
+        scratch=[pltpu.VMEM((nodes, cap * entries), BF16), pltpu.VMEM((cap * entries, cells), BF16)],
         vmem=8 + 3 * size // MIB,
         cost=cost(2 * size * cap * entries, 4 * size),
     )
 
 
-def step_kernel(
-    rows, lat, slots,
-    lat_ref, x_ref, wind_ref, side_ref, south_ref, north_ref, west_ref, east_ref, a_ref,
-    u_ref, *rest,
-):
-    part_refs, (rate, ring, b1, b2, mid, flat) = rest[:slots], rest[slots:]
-    count, width = side_ref.shape[2], x_ref.shape[1]
-    at_south = jnp.where(lat_ref[0] == 0, 1.0, 0.0)
-    at_north = jnp.where(lat_ref[0] == lat - 1, 1.0, 0.0)
-
-    def mend(c0, cw, ce, cs, cn):
-        line = iota(c0.shape, 0)
-        ps, pn = jnp.where(line == 0, at_south, 0.0), jnp.where(line == rows - 1, at_north, 0.0)
-        return c0 + ps * cs + pn * cn, cw, ce, cs * (1.0 - ps), cn * (1.0 - pn)
-
-    own = mend(*coefficients(wind_ref[0], wind_ref[1], wind_ref[2]))
+def mend(rows, lat, lat_ref, c0, cw, ce, cs, cn):
+    line = iota(c0.shape, 0)
+    ps = jnp.where((line == 0) & (lat_ref[0] == 0), 1.0, 0.0)
+    pn = jnp.where((line == rows - 1) & (lat_ref[0] == lat - 1), 1.0, 0.0)
+    return c0 + ps * cs + pn * cn, cw, ce, cs * (1.0 - ps), cn * (1.0 - pn)
+
+
+def turning(width):
+    k, col = iota((2 * width, 2 * width), 0), iota((2 * width, 2 * width), 1)
+    k = jnp.where(k < width, k, k - width)
+    return jnp.where(jnp.where(col < width, col - 1, col - width + 1) == k, 1.0, 0.0).astype(BF16)
+
+
+def advance(turn, rates, v, below, above):
+    width = v.shape[1]
+    hi = v.astype(BF16)
+    turned = dot(jnp.concatenate([hi, (v - hi.astype(F32)).astype(BF16)], 1), turn)
+    c0, cw, ce, cs, cn = rates
+    return c0 * v + cw * turned[:, 0:width] + ce * turned[:, width : 2 * width] + cs * below + cn * above
+
+
+def inner_kernel(rows, lat, lat_ref, x_ref, wind_ref, south_ref, north_ref, mid_ref, rate):
+    count, width = mid_ref.shape[1], x_ref.shape[1]
+    own = mend(rows, lat, lat_ref, *coefficients(wind_ref[0], wind_ref[1], wind_ref[2]))
     outer = []
     for ref in (south_ref, north_ref):
         v = ref[2 * count : 2 * count + 16, :].astype(F32)
@@ -202,50 +214,7 @@
         rate[j, 0:1, :] = outer[0][j]
         rate[j, 1 : rows + 1, :] = own[j]
         rate[j, rows + 1 : rows + 2, :] = outer[1][j]
-
-    west, east = west_ref[...].astype(F32), east_ref[...].astype(F32)
-    w1, w2, w_corner, w_rate = (west[k * rows : (k + 1) * rows, :] for k in range(4))
-    e1, e2, e_corner, e_rate = (east[k * rows : (k + 1) * rows, :] for k in range(4))
-
-    half = ring.shape[0] // 2
-
-    def place(out_ref, lines):
-        k, col = iota((2 * half, lines * width), 0), iota((2 * half, lines * width), 1)
-        hit = jnp.where(k < half, k * width, (k - half) * width + width - 1) == col
-        out_ref[...] = dot(ring[...].astype(BF16), jnp.where(hit, 1.0, 0.0).astype(BF16), 0, 0)
-
-    ring[...] = jnp.zeros(ring.shape, F32)
-    for base, corner, near, j, c in ((0, w_corner, w1, 1, 0), (half, e_corner, e1, 2, width - 1)):
-        ring[base : base + 1, :] = outer[0][j][:, c : c + 1] * corner[0:1, :]
-        ring[base + 1 : base + 1 + rows, :] = own[j][:, c : c + 1] * near
-        ring[base + 1 + rows : base + 2 + rows, :] = outer[1][j][:, c : c + 1] * corner[1:2, :]
-    place(b1, rows + 2)
-
-    def ring_col(rates, corner, v, out_w, out_e):
-        k0, kw, ke, ks, kn = mend(*coefficients(*(rates[:, j : j + 1] + rates[:, j + 3 : j + 4] for j in range(3))))
-        line = iota(v.shape, 0)
-        to_s = jnp.where(line == 0, corner[0:1, :], pltpu.roll(v, 1, 0))
-        to_n = jnp.where(line == rows - 1, corner[1:2, :], pltpu.roll(v, rows - 1, 0))
-        return k0 * v + kw * out_w + ke * out_e + ks * to_s + kn * to_n
-
-    ring[...] = jnp.zeros(ring.shape, F32)
-    ring[0:rows, :] = own[1][:, 0:1] * ring_col(w_rate, w_corner, w1, w2, side_ref[1, 0:rows, :])
-    ring[half : half + rows, :] = own[2][:, width - 1 : width] * ring_col(
-        e_rate, e_corner, e1, side_ref[0, 0:rows, :], e2
-    )
-    place(b2, rows)
-
-    k, col = iota((2 * width, 2 * width), 0), iota((2 * width, 2 * width), 1)
-    k = jnp.where(k < width, k, k - width)
-    turn = jnp.where(jnp.where(col < width, col - 1, col - width + 1) == k, 1.0, 0.0).astype(BF16)
-
-    def advance(line, v, below, above, b_ref, at):
-        hi = v.astype(BF16)
-        pair = jnp.concatenate([hi, (v - hi.astype(F32)).astype(BF16)], 1)
-        turned = dot(pair, turn)
-        c0, cw, ce, cs, cn = (rate[j, line + 1 : line + 2, :] for j in range(5))
-        new = c0 * v + cw * turned[:, 0:width] + ce * turned[:, width : 2 * width]
-        return new + cs * below + cn * above + b_ref[:, at * width : (at + 1) * width]
+    turn = turning(width)
 
     def cell_row(r):
         if r < 0:
@@ -255,12 +224,54 @@
         return x_ref[pl.ds(r, count, stride=rows), :]
 
     for r in range(-1, rows + 1):
-        mid[r + 1] = advance(r, cell_row(r), cell_row(r - 1), cell_row(r + 1), b1, r + 1)
+        rates = [rate[j, r + 1 : r + 2, :] for j in range(5)]
+        mid_ref[r + 1] = advance(turn, rates, cell_row(r), cell_row(r - 1), cell_row(r + 1))
+
+
+def step_kernel(rows, lat, slots, lat_ref, mid_ref, rate, side_ref, west_ref, east_ref, a_ref, u_ref, *rest):
+    part_refs, (ring, b1, b2, mid, flat) = rest[:slots], rest[slots:]
+    count, width = side_ref.shape[2], mid_ref.shape[2]
+    west, east = west_ref[...].astype(F32), east_ref[...].astype(F32)
+    w1, w2, w_corner, w_rate = (west[k * rows : (k + 1) * rows, :] for k in range(4))
+    e1, e2, e_corner, e_rate = (east[k * rows : (k + 1) * rows, :] for k in range(4))
+    half = ring.shape[0] // 2
+
+    def place(out_ref, lines):
+        k, col = iota((2 * half, lines * width), 0), iota((2 * half, lines * width), 1)
+        hit = jnp.where(k < half, k * width, (k - half) * width + width - 1) == col
+        out_ref[...] = dot(ring[...].astype(BF16), jnp.where(hit, 1.0, 0.0).astype(BF16), 0, 0)
+
+    ring[...] = jnp.zeros(ring.shape, F32)
+    for base, corner, near, j, c in ((0, w_corner, w1, 1, 0), (half, e_corner, e1, 2, width - 1)):
+        k = rate[j, :, c : c + 1]
+        ring[base : base + 1, :] = k[0:1, :] * corner[0:1, :]
+        ring[base + 1 : base + 1 + rows, :] = k[1 : rows + 1, :] * near
+        ring[base + 1 + rows : base + 2 + rows, :] = k[rows + 1 : rows + 2, :] * corner[1:2, :]
+    place(b1, rows + 2)
+
+    def ring_col(rates, corner, v, out_w, out_e):
+        rates = coefficients(*(rates[:, j : j + 1] + rates[:, j + 3 : j + 4] for j in range(3)))
+        k0, kw, ke, ks, kn = mend(rows, lat, lat_ref, *rates)
+        line = iota(v.shape, 0)
+        to_s = jnp.where(line == 0, corner[0:1, :], pltpu.roll(v, 1, 0))
+        to_n = jnp.where(line == rows - 1, corner[1:2, :], pltpu.roll(v, rows - 1, 0))
+        return k0 * v + kw * out_w + ke * out_e + ks * to_s + kn * to_n
+
+    ring[...] = jnp.zeros(ring.shape, F32)
+    kw, ke = rate[1, 1 : rows + 1, 0:1], rate[2, 1 : rows + 1, width - 1 : width]
+    ring[0:rows, :] = kw * ring_col(w_rate, w_corner, w1, w2, side_ref[1, 0:rows, :])
+    ring[half : half + rows, :] = ke * ring_col(e_rate, e_corner, e1, side_ref[0, 0:rows, :], e2)
+    place(b2, rows)
+
+    for r in range(rows + 2):
+        mid[r] = mid_ref[r] + b1[:, r * width : (r + 1) * width]
+    turn = turning(width)
     for r in range(rows):
-        new = advance(r, mid[r + 1], mid[r], mid[r + 2], b2, r)
-        u_ref[:, r * width : (r + 1) * width] = new
-        flat[:, r * width : (r + 1) * width] = new.astype(BF16)
-
+        here = slice(r * width, (r + 1) * width)
+        rates = [rate[j, r + 1 : r + 2, :] for j in range(5)]
+        new = advance(turn, rates, mid[r + 1], mid[r], mid[r + 2]) + b2[:, here]
+        u_ref[:, here] = new
+        flat[:, here] = new.astype(BF16)
     for s in range(slots):
         part_refs[s][...] = dot(a_ref[s], flat[...], 1, 1).astype(part_refs[s].dtype)
 
@@ -338,66 +349,105 @@
         project(m, hidden, owed, ws_ref[0], wr_ref[0], table_ref, out_refs, wanted, nodes)
 
 
-def messages(lo, hi, chunk, gather_ref, scatter_ref, depth, tables, sums_ref):
+def pieces(chunk):
     step = chunk // 3
-
-    @pl.loop(lo, hi)
+    return [(k, step) for k in range(0, chunk, step)]
+
+
+def early_kernel(chunk, local_ref, table_ref, gather_ref, scatter_ref, sums_ref, terms_ref):
+    members, depth, _ = table_ref.shape
+    edges = gather_ref.shape[0]
+    sums_ref[...] = jnp.zeros(sums_ref.shape, F32)
+
+    @pl.loop(0, edges // chunk)
     def _(c):
         at = pl.multiple_of(c * chunk, chunk)
-        for m, table in enumerate(tables):
-            found = [
-                silu(dot(gather_ref[pl.ds(at + k, step), 0:depth], table[...])).astype(BF16)
-                for k in range(0, chunk, step)
-            ]
+        here = c < local_ref[0] // chunk
+
+        @pl.when(here)
+        def _():
+            for m in range(members):
+                found = [
+                    silu(dot(gather_ref[pl.ds(at + k, n), 0:depth], table_ref[m])).astype(BF16)
+                    for k, n in pieces(chunk)
+                ]
+                sums_ref[m] += dot(scatter_ref[:, pl.ds(at, chunk)], jnp.concatenate(found, 0))
+
+        @pl.when(jnp.logical_not(here))
+        def _():
+            for m in range(members):
+                for k, n in pieces(chunk):
+                    terms_ref[m, pl.ds(at + k, n), :] = dot(gather_ref[pl.ds(at + k, n), 0:depth], table_ref[m])
+
+
+def late_messages(chunk, local_ref, gather_ref, scatter_ref, depth, terms_ref, known, chosen, sums_ref):
+    edges = gather_ref.shape[0]
+
+    @pl.loop(local_ref[0] // chunk, edges // chunk)
+    def _(c):
+        at = pl.multiple_of(c * chunk, chunk)
+        for m in chosen:
+            found = []
+            for k, n in pieces(chunk):
+                v = terms_ref[m, pl.ds(at + k, n), :] + dot(gather_ref[pl.ds(at + k, n), depth:], known[m])
+                found.append(silu(v).astype(BF16))
             sums_ref[m] += dot(scatter_ref[:, pl.ds(at, chunk)], jnp.concatenate(found, 0))
 
 
-def early_kernel(chunk, local_ref, table_ref, gather_ref, scatter_ref, sums_ref):
-    members, depth, _ = table_ref.shape
-    sums_ref[...] = jnp.zeros(sums_ref.shape, F32)
-    tables = [table_ref.at[m] for m in range(members)]
-    messages(0, local_ref[0] // chunk, chunk, gather_ref, scatter_ref, depth, tables, sums_ref)
-
-
-def layer_kernel(layer, last, wanted, chunk, *refs):
-    local_ref, hidden_ref, table_ref, owed_ref, gather_ref, scatter_ref, early_ref = refs[:7]
+def layer_kernel(layer, only, wanted, chunk, *refs):
+    local_ref, hidden_ref, terms_ref, owed_ref, gather_ref, scatter_ref, early_ref = refs[:7]
     halo_refs, wu_ref = refs[7:11], refs[11]
+    last = only is not None
     if last:
         dec_ref, out_ref, known, sums = refs[12:]
     else:
         ws_ref, wr_ref, next_hidden_ref, next_table_ref, *out_refs, known, sums = refs[12:]
     members, nodes, width = hidden_ref.shape
-    edges, depth = gather_ref.shape
-    sums[...] = early_ref[...]
-    for m in range(members):
-        known[m, 0 : 2 * nodes, :] = table_ref[m]
+    chosen = (only,) if last else range(members)
+    for m in chosen:
+        sums[m] = early_ref[m]
         for q in range(4):
-            at = 2 * nodes + q * wanted
-            known[m, at : at + wanted, :] = halo_refs[q][m * wanted : (m + 1) * wanted, :]
-        at = 2 * nodes + 4 * wanted
-        known[m, at:, :] = jnp.zeros((depth - at, width), BF16)
-    tables = [known.at[m] for m in range(members)]
-    messages(local_ref[0] // chunk, edges // chunk, chunk, gather_ref, scatter_ref, depth, tables, sums)
+            known[m, q * wanted : (q + 1) * wanted, :] = halo_refs[q][m * wanted : (m + 1) * wanted, :]
+        known[m, 4 * wanted :, :] = jnp.zeros((known.shape[1] - 4 * wanted, width), BF16)
+    late_messages(chunk, local_ref, gather_ref, scatter_ref, 2 * nodes, terms_ref, known, chosen, sums)
     if not last:
         owed = [owed_ref[q * wanted : (q + 1) * wanted, :] for q in range(4)]
-    for m in range(members):
+    for m in chosen:
         hidden = hidden_ref[m] + dot(sums[m].astype(BF16), wu_ref[layer])
         if last:
-            got = dot(dec_ref[...], normalize(hidden), 1, 1)
-            out_ref[m * got.shape[0] : (m + 1) * got.shape[0], :] = got.astype(BF16)
+            out_ref[...] = dot(dec_ref[...], normalize(hidden), 1, 1).astype(BF16)
         else:
             next_hidden_ref[m] = hidden
             project(m, hidden, owed, ws_ref[layer + 1], wr_ref[layer + 1], next_table_ref, out_refs, wanted, nodes)
 
 
-def land_kernel(rows, slots, u_ref, w_ref, *refs):
-    corr_refs, out_ref = refs[:slots], refs[slots]
-    count, width = u_ref.shape[0], u_ref.shape[1] // rows
-    total = u_ref[...]
+def land_kernel(rows, slots, member, u_ref, w_ref, *refs):
+    corr_refs, (out_ref, tile, sem) = refs[:slots], refs[-3:]
+    quantities, width = corr_refs[0].shape[0], u_ref.shape[1] // rows
+    total = u_ref[member * quantities : (member + 1) * quantities, :]
     for s in range(slots):
         total = total + dot(corr_refs[s][...], w_ref[s])
     for r in range(rows):
-        out_ref[pl.ds(r, count, stride=rows), :] = total[:, r * width : (r + 1) * width]
+        tile[pl.ds(r, quantities, stride=rows), :] = total[:, r * width : (r + 1) * width]
+    size = quantities * rows
+    copy = pltpu.make_async_copy(tile, out_ref.at[member * size : (member + 1) * size], sem)
+    copy.start()
+    copy.wait()
+
+
+def land(kernel, x, args, onward, size, lon):
+    spaces = [pl.BlockSpec(memory_space=pltpu.VMEM)] * (len(args) - onward)
+    spaces += [pl.BlockSpec(memory_space=pl.ANY)] * onward
+    return pl.pallas_call(
+        kernel,
+        out_shape=shape(x.shape, F32),
+        in_specs=spaces,
+        out_specs=pl.BlockSpec(memory_space=pl.ANY),
+        scratch_shapes=[pltpu.VMEM((size, x.shape[1]), F32), pltpu.SemaphoreType.DMA],
+        input_output_aliases={len(args) - 1: 0} if onward else {},
+        compiler_params=pltpu.CompilerParams(vmem_limit_bytes=(16 + lon) * MIB),
+        cost_estimate=cost(1e9, 6 * MIB),
+    )(*args)
 
 
 def body(
@@ -421,6 +471,11 @@
     def shift(v, s):
         return lax.ppermute(v, "lon", [(i, (i + s) % lon) for i in range(lon)])
 
+    def peer(v, s):
+        if lon & (lon - 1):
+            return shift(v, s)
+        return lax.ppermute(v, "lon", [(i, i ^ s) for i in range(lon)])
+
     def up(v):
         return lax.ppermute(v, "lat", [(i, (i + 1) % lat) for i in range(lat)])
 
@@ -431,22 +486,22 @@
     halo = halo_rows.reshape(4, wanted)
     rates = (wind_east, wind_north, diffusion)
     tall = 2 * count + 16
-    tables = (inflow_node, inflow_cell, inflow_weight, outflow_node, outflow_cell, outflow_weight)
-    to_north, to_south, side, wind, x, in_lists, *out_lists = call(
+    tables = (inflow_node, inflow_cell, inflow_weight)
+    taken = pltpu.SMEM((lon,), I32)
+    to_north, to_south, side, wind, in_lists = call(
         functools.partial(edge_kernel, rows, lon),
         [shape((tall, width), BF16), shape((tall, width), BF16), shape((2, 4 * rows, count), F32),
-         shape((3, rows, width), F32), shape(x.shape, F32), shape((lon, 3 * cap, entries), F32)]
-        + [shape((3 * cap, entries), F32)] * lon,
-        (me, inflow_owner.reshape(blocks), outflow_owner.reshape(blocks), x, *rates, halo, *tables),
-        smem=3,
-        away=11,
+         shape((3, rows, width), F32), shape((lon, 3 * cap, entries), F32)],
+        (me, inflow_owner.reshape(blocks), x, *rates, halo, *tables),
+        smem=2,
+        away=8,
         scratch=[
+            pltpu.VMEM(x.shape, F32),
             pltpu.VMEM(halo.shape, I32),
             pltpu.VMEM((16, width), F32),
-            pltpu.SMEM((lon,), I32),
-            pltpu.VMEM((lon, 3 * cap, entries), F32),
+            taken,
             *(pltpu.VMEM(v.shape, v.dtype) for v in tables),
-            pltpu.SemaphoreType.DMA((11,)),
+            pltpu.SemaphoreType.DMA((8,)),
         ],
         vmem=56,
         cost=cost(0, 8 * MIB),
@@ -463,13 +518,21 @@
     )
     west, east = shift(to_east, 1), shift(to_west, lon - 1)
 
+    x, _ = lax.optimization_barrier((x, to_east))
+    mid, rate = call(
+        functools.partial(inner_kernel, rows, lat),
+        (shape((rows + 2, count, width), F32), shape((5, rows + 2, width), F32)),
+        (lat_at, x, wind, south, north),
+        smem=1,
+        vmem=12,
+        cost=cost(1e9, 6 * MIB),
+    )
     u, *parts = call(
         functools.partial(step_kernel, rows, lat, lon),
         [shape((count, cells), F32)] + [shape((nodes, count), F32)] + [shape((nodes, count), BF16)] * (lon - 1),
-        (lat_at, x, wind, side, south, north, west, east, into),
+        (lat_at, mid, rate, side, west, east, into),
         smem=1,
         scratch=[
-            pltpu.VMEM((5, rows + 2, width), F32),
             pltpu.VMEM((32, count), F32),
             pltpu.VMEM((count, (rows + 2) * width), F32),
             pltpu.VMEM((count, cells), F32),
@@ -479,8 +542,11 @@
         vmem=14 + lon * 2,
         cost=cost(2 * lon * nodes * cells * count, 16 * MIB),
     )
-    parts, edge_sender, edge_receiver = lax.optimization_barrier((parts, edge_sender, edge_receiver))
-    parts = parts[:1] + [shift(parts[s], s) for s in range(1, lon)]
+    parts, edge_sender, edge_receiver, outflow_node = lax.optimization_barrier(
+        (parts, edge_sender, edge_receiver, outflow_node)
+    )
+    got = [peer(parts[s], s) for s in range(lon - 1, 0, -1)]
+    parts = parts[:1] + got[::-1]
 
     known = 2 * nodes + 256 * -(-4 * wanted // 256)
     chunk = edges // 2
@@ -493,8 +559,17 @@
         vmem=24,
         cost=cost(2 * edges * edges * 48, 8 * MIB),
     )
+    out_lists = call(
+        functools.partial(sort_kernel, lon),
+        [shape((3 * cap, entries), F32)] * lon,
+        (me, outflow_owner.reshape(blocks), outflow_node, outflow_cell, outflow_weight),
+        smem=2,
+        scratch=[pltpu.VMEM((lon, 3 * cap, entries), F32), taken],
+        vmem=4,
+        cost=cost(0, MIB),
+    )
     scatter, out_lists = lax.optimization_barrier((scatter, out_lists))
-    out_lists = [out_lists[0]] + [shift(out_lists[s], s) for s in range(1, lon)]
+    out_lists = [out_lists[0]] + [peer(out_lists[s], s) for s in range(1, lon)]
     parts, out_lists = lax.optimization_barrier((parts, out_lists))
     onto = build(lon, nodes, cells, out_lists)
 
@@ -515,27 +590,30 @@
         cost=cost(2e9, 8 * MIB),
     )
     for layer in range(layers):
-        halos = [up(out[1]), down(out[0]), shift(out[3], 1), shift(out[2], lon - 1)]
-        early = call(
+        halos = [shift(out[3], 1), shift(out[2], lon - 1), up(out[1]), down(out[0])]
+        halos = halos[2:] + halos[:2]
+        early, terms = call(
             functools.partial(early_kernel, chunk),
-            shape((members, nodes, hid), F32),
+            (shape((members, nodes, hid), F32), shape((members, edges, hid), F32)),
             (local, table, gather, scatter),
             smem=1,
             vmem=16,
             cost=cost(3e9, 8 * MIB),
         )
         last = layer == layers - 1
-        args = (local, hidden, table, owed, gather, scatter, early, *halos, update_weight)
-        scratch = [pltpu.VMEM((members, known, hid), BF16), pltpu.VMEM((members, nodes, hid), F32)]
-        kernel = functools.partial(layer_kernel, layer, last, wanted, chunk)
+        args = (local, hidden, terms, owed, gather, scatter, early, *halos, update_weight)
+        scratch = [pltpu.VMEM((members, known - 2 * nodes, hid), BF16), pltpu.VMEM((members, nodes, hid), F32)]
         if last:
-            corr = call(
-                kernel, shape((count, nodes), BF16), (*args, decoder.T), smem=1, scratch=scratch, vmem=20,
-                cost=cost(4e9, 12 * MIB),
-            )
+            corrs = [
+                call(
+                    functools.partial(layer_kernel, layer, m, wanted, chunk), shape((quantities, nodes), BF16),
+                    (*args, decoder.T), smem=1, scratch=scratch, vmem=20, cost=cost(2e9, 8 * MIB),
+                )
+                for m in range(members)
+            ]
         else:
             hidden, table, *out = call(
-                kernel,
+                functools.partial(layer_kernel, layer, None, wanted, chunk),
                 state + reply,
                 (*args, sender_weight, receiver_weight),
                 smem=1,
@@ -543,14 +621,12 @@
                 vmem=20,
                 cost=cost(4e9, 12 * MIB),
             )
-    corrs = [corr] + [shift(corr, s) for s in range(1, lon)]
-    out = call(
-        functools.partial(land_kernel, rows, lon),
-        shape(x.shape, F32),
-        (u, onto, *corrs),
-        vmem=16 + lon,
-        cost=cost(2 * lon * nodes * cells * count, 8 * MIB),
-    )
+    corrs = [[v] + [peer(v, s) for s in range(lon - 1, 0, -1)] for v in corrs]
+    out = None
+    for m in range(members):
+        got = [corrs[m][0]] + corrs[m][:0:-1]
+        args = (u, onto, *got) if out is None else (u, onto, *got, out)
+        out = land(functools.partial(land_kernel, rows, lon, m), x, args, out is not None, rows * quantities, lon)
     return out.reshape(members, quantities, rows, width)
 
 

time: 95.7 us -> 90.6 us (0.947)
  waiting for transfers between devices: 27 us -> 12.2 us
  starting transfers between devices: 28.3 us -> 38.1 us
    ppermute x15 -> x6, waiting for transfers between devices: 26.7 us -> 0.47 us  [shift(): return lax.ppermute(v, 'lon', [(i, (i + s) % lon) for i in range(lon)])]
    ppermute x0 -> x12, starting transfers between devices: none -> 20.5 us  [peer(): return lax.ppermute(v, 'lon', [(i, i ^ s) for i in range(lon)])]
    ppermute x15 -> x6, starting transfers between devices: 22.2 us -> 11.5 us  [shift(): return lax.ppermute(v, 'lon', [(i, (i + s) % lon) for i in range(lon)])]
    ppermute x0 -> x12, waiting for transfers between devices: none -> 9.85 us  [peer(): return lax.ppermute(v, 'lon', [(i, i ^ s) for i in range(lon)])]
    pallas_call x13 -> x15, Pallas kernels: 37.6 us -> 34.2 us  [call(): pl.pallas_call(kernel, out_shape=outs if single else tuple(outs), in_spec...]
    pallas_call x0 -> x2, Pallas kernels: none -> 3.05 us  [land(): pl.pallas_call(kernel, out_shape=shape(x.shape, F32), in_specs=spaces, ou...]
    ppermute x3, waiting for transfers between devices: 0.35 us -> 1.84 us  [down(): return lax.ppermute(v, 'lat', [((i + 1) % lat, i) for i in range(lat)])]
  transfers between devices with their start and end apart: 21 -> 24, of which waited for: 10 -> 6; matrix products, arithmetic and copies ran while one was open for 0% -> 0% of each run, Pallas kernels for 18% -> 24%
where the time goes in v2:
time: 90.6 us; the launch traced here: 90.3 us
  starting transfers between devices  38.1 us (42%)
  Pallas kernels  37.3 us (41%)
  waiting for transfers between devices  12.2 us (13%)
  local copies, waits for them, and re-layouts  2.28 us (3%)
    pallas_call x15, Pallas kernels, call(): pl.pallas_call(kernel, out_shape=outs if single else tuple(outs), in_spec...  34.2 us
    ppermute x12, starting transfers between devices, peer(): return lax.ppermute(v, 'lon', [(i, i ^ s) for i in range(lon)])  20.5 us
    ppermute x6, starting transfers between devices, shift(): return lax.ppermute(v, 'lon', [(i, (i + s) % lon) for i in range(lon)])  11.5 us
    ppermute x12, waiting for transfers between devices, peer(): return lax.ppermute(v, 'lon', [(i, i ^ s) for i in range(lon)])  9.85 us
    ppermute x3, starting transfers between devices, down(): return lax.ppermute(v, 'lat', [((i + 1) % lat, i) for i in range(lat)])  5.45 us
    pallas_call x2, Pallas kernels, land(): pl.pallas_call(kernel, out_shape=shape(x.shape, F32), in_specs=spaces, ou...  3.05 us
    unnamed x30, local copies, waits for them, and re-layouts  2.28 us
    ppermute x3, waiting for transfers between devices, down(): return lax.ppermute(v, 'lat', [((i + 1) % lat, i) for i in range(lat)])  1.84 us
  transfers between devices with their start and end apart: 24, of which 6 were waited for; matrix products, arithmetic and copies ran while one was open for 0% of the time, Pallas kernels for 24%

profile of v2, /device:TPU:0, one launch (start us, length us, event | category | flops | bytes accessed | tf_op | source)
XLA Modules:
  0.0 90.3 jit_solution(322728747693931677)
XLA Ops:
  0.0 3.3 %shard_map.190 = (bf16[784,128]{1,0:T(8,128)(2,1)}, bf16[784,128]{1,0:T(8,128)(2,1)}, f32[2,32,384]{2,1,0:T(8,128)}, f32[3,8,128]{2,1,0:T(8,128)}, f32[4,24,128]{2,1,0:T(8,128)}) custom-call(s32[1]{0:T(128)} %bitcast.2.me_ref, s32[16]{0:T(128)} %bitcast.18, f32[3072,128]{1,0:T(8,128)} %bitcast.10, f32[8,128]{1,0:T(8,128)} %refs_1_.2, f32[8,128]{1,0:T(8,128)} %refs_2_.2, ...), custom_call_target="tpu_custom_call" | custom-call | bytes 419430 | tf_op jit(solution)/shard_map/pallas_call | solution.py:32
  3.9 2.0 %collective-permute-start.1 = (bf16[784,128]{1,0:T(8,128)(2,1)}, bf16[784,128]{1,0:T(8,128)(2,1)S(1)}, u32[]{:S(2)}, u32[]{:S(2)}) collective-permute-start(bf16[784,128]{1,0:T(8,128)(2,1)} %get-tuple-element.68), channel_id=1, source_target_pairs={{4,0},{8,4},{12,8},{0,12},{5,1},{9,5},{13,9},{1,13},{6,2},{10,6},{... | collective-permute-start | bytes 602120 | tf_op jit(solution)/shard_map/ppermute | solution.py:483
  6.7 3.0 %shard_map.191.a_ref = bf16[4,256,1024]{2,1,0:T(8,128)(2,1)S(1)} custom-call(f32[4,24,128]{2,1,0:T(8,128)S(1)} %copy-done.7), custom_call_target="tpu_custom_call" | custom-call | flops 107374184 | bytes 209715 | tf_op jit(solution)/shard_map/pallas_call | solution.py:32
  9.6 1.8 %collective-permute-done.1.north_ref = bf16[784,128]{1,0:T(8,128)(2,1)S(1)} collective-permute-done((bf16[784,128]{1,0:T(8,128)(2,1)}, bf16[784,128]{1,0:T(8,128)(2,1)S(1)}, u32[]{:S(2)}, u32[]{:S(2)}) %collective-permute-start.1) | collective-permute-done | bytes 200736 | tf_op jit(solution)/shard_map/ppermute | solution.py:483
  13.2 2.2 %collective-permute-start.3 = (bf16[32,384]{1,0:T(8,128)(2,1)S(1)}, bf16[32,384]{1,0:T(8,128)(2,1)S(1)}, u32[]{:S(2)}, u32[]{:S(2)}) collective-permute-start(bf16[32,384]{1,0:T(8,128)(2,1)S(1)} %get-tuple-element.77), channel_id=1, source_target_pairs={{0,3},{1,0},{2,1},{3,2},{4,7},{5,4},{6,5},{7,6},{8,11},{9,8},{10,9... | collective-permute-start | bytes 73736 | tf_op jit(solution)/shard_map/ppermute | solution.py:472
  18.3 2.8 %shard_map.194 = (f32[384,1024]{1,0:T(8,128)S(1)}, f32[256,384]{1,0:T(8,128)S(1)}, bf16[256,384]{1,0:T(8,128)(2,1)S(1)}, bf16[256,384]{1,0:T(8,128)(2,1)S(1)}, bf16[256,384]{1,0:T(8,128)(2,1)S(1)}) custom-call(s32[1]{0:T(128)} %bitcast.lat_ref, f32[10,384,128]{2,1,0:T(8,128)S(1)} %get-tuple-element.75.mid_ref, f32[5,10,128]{2,1,0:T(8,128)S(1)} %get-tuple-element.76.rate, ...), custom_call_target="tpu_custom_call" | custom-call | flops 40265320 | bytes 838860 | tf_op jit(solution)/shard_map/pallas_call | solution.py:32
  21.6 3.0 %collective-permute-start.5 = (bf16[256,384]{1,0:T(8,128)(2,1)S(1)}, bf16[256,384]{1,0:T(8,128)(2,1)S(1)}, u32[]{:S(2)}, u32[]{:S(2)}) collective-permute-start(bf16[256,384]{1,0:T(8,128)(2,1)S(1)} %get-tuple-element.86), channel_id=1, source_target_pairs={{0,2},{1,3},{2,0},{3,1},{4,6},{5,7},{6,4},{7,5},{8,10},{9,11},{10,... | collective-permute-start | bytes 589832 | tf_op jit(solution)/shard_map/ppermute | solution.py:477
  26.3 3.6 %shard_map.195 = (bf16[1536,768]{1,0:T(8,128)(2,1)S(1)}, bf16[256,1536]{1,0:T(8,128)(2,1)S(1)}, s32[1]{0:T(128)}) custom-call(s32[1,1536]{1,0:T(1,128)S(1)} %bitcast.15, s32[1,1536]{1,0:T(1,128)S(1)} %bitcast.16), custom_call_target="tpu_custom_call" | custom-call | flops 11324620 | bytes 419430 | tf_op jit(solution)/shard_map/pallas_call | solution.py:32
  30.0 3.5 %collective-permute-start.8 = (f32[24,128]{1,0:T(8,128)S(1)}, f32[24,128]{1,0:T(8,128)S(1)}, u32[]{:S(2)}, u32[]{:S(2)}) collective-permute-start(f32[24,128]{1,0:T(8,128)S(1)} %get-tuple-element.98), channel_id=1, source_target_pairs={{0,2},{1,3},{2,0},{3,1},{4,6},{5,7},{6,4},{7,5},{8,10},{9,11},{10,... | collective-permute-start | bytes 36872 | tf_op jit(solution)/shard_map/ppermute | solution.py:477
  35.0 3.6 %collective-permute-start.9 = (f32[24,128]{1,0:T(8,128)S(1)}, f32[24,128]{1,0:T(8,128)S(1)}, u32[]{:S(2)}, u32[]{:S(2)}) collective-permute-start(f32[24,128]{1,0:T(8,128)S(1)} %get-tuple-element.99), channel_id=1, source_target_pairs={{0,3},{1,2},{2,1},{3,0},{4,7},{5,6},{6,5},{7,4},{8,11},{9,10},{10,... | collective-permute-start | bytes 36872 | tf_op jit(solution)/shard_map/ppermute | solution.py:477
  38.8 4.2 %collective-permute-done.8.refs_2_ = f32[24,128]{1,0:T(8,128)S(1)} collective-permute-done((f32[24,128]{1,0:T(8,128)S(1)}, f32[24,128]{1,0:T(8,128)S(1)}, u32[]{:S(2)}, u32[]{:S(2)}) %collective-permute-start.8) | collective-permute-done | bytes 12320 | tf_op jit(solution)/shard_map/ppermute | solution.py:477
  43.0 1.7 %shard_map.199 = (f32[2,256,512]{2,1,0:T(8,128)S(1)}, bf16[2,512,512]{2,1,0:T(8,128)(2,1)S(1)}, bf16[96,512]{1,0:T(8,128)(2,1)S(1)}, bf16[96,512]{1,0:T(8,128)(2...) custom-call(f32[256,384]{1,0:T(8,128)S(1)} %get-tuple-element.105.refs_0_, ...), custom_call_target="tpu_custom_call" | custom-call | flops 100000000 | bytes 419430 | tf_op jit(solution)/shard_map/pallas_call | solution.py:32
  47.2 3.1 %collective-permute-start.13 = (bf16[96,512]{1,0:T(8,128)(2,1)S(1)}, bf16[96,512]{1,0:T(8,128)(2,1)S(1)}, u32[]{:S(2)}, u32[]{:S(2)}) collective-permute-start(bf16[96,512]{1,0:T(8,128)(2,1)S(1)} %get-tuple-element.120), channel_id=1, source_target_pairs={{0,3},{1,0},{2,1},{3,2},{4,7},{5,4},{6,5},{7,6},{8,11},{9,8},{10,9... | collective-permute-start | bytes 294920 | tf_op jit(solution)/shard_map/ppermute | solution.py:472
  50.4 3.3 %shard_map.200 = (f32[2,256,512]{2,1,0:T(8,128)S(1)}, f32[2,1536,512]{2,1,0:T(8,128)S(1)}) custom-call(s32[1]{0:T(128)} %get-tuple-element.104.local_ref.refs_0_, bf16[2,512,512]{2,1,0:T(8,128)(2,1)S(1)} %get-tuple-element.112.table_ref, bf16[1536,768]{1,0:T(8,128)(2,1)S(1)} %get-tuple-element.113.gather_ref.refs_4_, ...), custom_call_target="tpu_custom_call" | custom-call | flops 150000000 | bytes 419430 | tf_op jit(solution)/shard_map/pallas_call | solution.py:32
  54.0 4.0 %shard_map.201 = (f32[2,256,512]{2,1,0:T(8,128)S(1)}, bf16[2,512,512]{2,1,0:T(8,128)(2,1)S(1)}, bf16[96,512]{1,0:T(8,128)(2,1)S(1)}, bf16[96,512]{1,0:T(8,128)(2...) custom-call(s32[1]{0:T(128)} %get-tuple-element.104.local_ref.refs_0_, ...), custom_call_target="tpu_custom_call" | custom-call | flops 200000000 | bytes 629145 | tf_op jit(solution)/shard_map/pallas_call | solution.py:32
  58.0 1.7 %collective-permute-start.15 = (bf16[96,512]{1,0:T(8,128)(2,1)S(1)}, bf16[96,512]{1,0:T(8,128)(2,1)S(1)}, u32[]{:S(2)}, u32[]{:S(2)}) collective-permute-start(bf16[96,512]{1,0:T(8,128)(2,1)S(1)} %get-tuple-element.126), channel_id=1, source_target_pairs={{4,0},{8,4},{12,8},{0,12},{5,1},{9,5},{13,9},{1,13},{6,2},{10,6},{... | collective-permute-start | bytes 294920 | tf_op jit(solution)/shard_map/ppermute | solution.py:483
  60.6 3.0 %collective-permute-start.17 = (bf16[96,512]{1,0:T(8,128)(2,1)S(1)}, bf16[96,512]{1,0:T(8,128)(2,1)S(1)}, u32[]{:S(2)}, u32[]{:S(2)}) collective-permute-start(bf16[96,512]{1,0:T(8,128)(2,1)S(1)} %get-tuple-element.128), channel_id=1, source_target_pairs={{0,3},{1,0},{2,1},{3,2},{4,7},{5,4},{6,5},{7,6},{8,11},{9,8},{10,9... | collective-permute-start | bytes 294920 | tf_op jit(solution)/shard_map/ppermute | solution.py:472
  63.6 3.2 %shard_map.202 = (f32[2,256,512]{2,1,0:T(8,128)S(1)}, f32[2,1536,512]{2,1,0:T(8,128)S(1)}) custom-call(s32[1]{0:T(128)} %get-tuple-element.104.local_ref.refs_0_, bf16[2,512,512]{2,1,0:T(8,128)(2,1)S(1)} %get-tuple-element.122.table_ref, bf16[1536,768]{1,0:T(8,128)(2,1)S(1)} %get-tuple-element.113.gather_ref.refs_4_, ...), custom_call_target="tpu_custom_call" | custom-call | flops 150000000 | bytes 419430 | tf_op jit(solution)/shard_map/pallas_call | solution.py:32
  67.0 2.0 %shard_map.204.refs_0_ = bf16[192,256]{1,0:T(8,128)(2,1)S(1)} custom-call(s32[1]{0:T(128)} %get-tuple-element.104.local_ref.refs_0_, f32[2,256,512]{2,1,0:T(8,128)S(1)} %get-tuple-element.121.refs_1_, f32[2,1536,512]{2,1,0:T(8,128)S(1)} %get-tuple-element.123.refs_2_, bf16[192,256]{1,0:T(8,128)(2,1)S(1)} %get-tuple-element.110.refs_7_.refs_3_, ...), custom_call_target="tpu_custom_call" | custom-call | flops 100000000 | bytes 419430 | tf_op jit(solution)/shard_map/pallas_call | solution.py:32
  70.5 2.2 %collective-permute-start.22 = (bf16[192,256]{1,0:T(8,128)(2,1)S(1)}, bf16[192,256]{1,0:T(8,128)(2,1)S(1)}, u32[]{:S(2)}, u32[]{:S(2)}) collective-permute-start(bf16[192,256]{1,0:T(8,128)(2,1)S(1)} %shard_map.204.refs_0_), channel_id=1, source_target_pairs={{0,2},{1,3},{2,0},{3,1},{4,6},{5,7},{6,4},{7,5},{8,10},{9,11},{10,... | collective-permute-start | bytes 294920 | tf_op jit(solution)/shard_map/ppermute | solution.py:477
  73.5 2.0 %shard_map.203.refs_0_ = bf16[192,256]{1,0:T(8,128)(2,1)S(1)} custom-call(s32[1]{0:T(128)} %get-tuple-element.104.local_ref.refs_0_, f32[2,256,512]{2,1,0:T(8,128)S(1)} %get-tuple-element.121.refs_1_, f32[2,1536,512]{2,1,0:T(8,128)S(1)} %get-tuple-element.123.refs_2_, bf16[192,256]{1,0:T(8,128)(2,1)S(1)} %get-tuple-element.110.refs_7_.refs_3_, ...), custom_call_target="tpu_custom_call" | custom-call | flops 100000000 | bytes 419430 | tf_op jit(solution)/shard_map/pallas_call | solution.py:32
  76.0 3.1 %collective-permute-start.19 = (bf16[192,256]{1,0:T(8,128)(2,1)S(1)}, bf16[192,256]{1,0:T(8,128)(2,1)S(1)}, u32[]{:S(2)}, u32[]{:S(2)}) collective-permute-start(bf16[192,256]{1,0:T(8,128)(2,1)S(1)} %shard_map.203.refs_0_), channel_id=1, source_target_pairs={{0,2},{1,3},{2,0},{3,1},{4,6},{5,7},{6,4},{7,5},{8,10},{9,11},{10,... | collective-permute-start | bytes 294920 | tf_op jit(solution)/shard_map/ppermute | solution.py:477
  80.0 3.0 %shard_map.197.w_ref = bf16[4,256,1024]{2,1,0:T(8,128)(2,1)S(1)} custom-call(f32[24,128]{1,0:T(8,128)S(1)} %get-tuple-element.100.refs_0_, f32[24,128]{1,0:T(8,128)S(1)} %collective-permute-done.7.refs_1_, f32[24,128]{1,0:T(8,128)S(1)} %collective-permute-done.8.refs_2_, f32[24,128]{1,0:T(8,128)S(1)} %collective-permute-done.9.refs_3_), custom_call_target="tpu_custom_call" | custom-call | flops 107374184 | bytes 209715 | tf_op jit(solution)/shard_map/pallas_call | solution.py:32
  84.6 4.0 %collective-permute-done.19.refs_2_ = bf16[192,256]{1,0:T(8,128)(2,1)S(1)} collective-permute-done((bf16[192,256]{1,0:T(8,128)(2,1)S(1)}, bf16[192,256]{1,0:T(8,128)(2,1)S(1)}, u32[]{:S(2)}, u32[]{:S(2)}) %collective-permute-start.19) | collective-permute-done | bytes 98336 | tf_op jit(solution)/shard_map/ppermute | solution.py:477
  (71 shorter events, 20.1 us)
Async XLA Ops:
  3.4 6.3 %collective-permute-start = (bf16[784,128]{1,0:T(8,128)(2,1)}, bf16[784,128]{1,0:T(8,128)(2,1)S(1)}, u32[]{:S(2)}, u32[]{:S(2)}) collective-permute-start(bf16[784,128]{1,0:T(8,128)(2,1)} %get-tuple-element.67), channel_id=1, source_target_pairs={{0,4},{4,8},{8,12},{12,0},{1,5},{5,9},{9,13},{13,1},{2,6},{6,10},{... | collective-permute-start | bytes 602120 | tf_op jit(solution)/shard_map/ppermute | solution.py:480
  3.9 7.6 %collective-permute-start.1 = (bf16[784,128]{1,0:T(8,128)(2,1)}, bf16[784,128]{1,0:T(8,128)(2,1)S(1)}, u32[]{:S(2)}, u32[]{:S(2)}) collective-permute-start(bf16[784,128]{1,0:T(8,128)(2,1)} %get-tuple-element.68), channel_id=1, source_target_pairs={{4,0},{8,4},{12,8},{0,12},{5,1},{9,5},{13,9},{1,13},{6,2},{10,6},{... | collective-permute-start | bytes 602120 | tf_op jit(solution)/shard_map/ppermute | solution.py:483
  11.6 6.5 %collective-permute-start.2 = (bf16[32,384]{1,0:T(8,128)(2,1)S(1)}, bf16[32,384]{1,0:T(8,128)(2,1)S(1)}, u32[]{:S(2)}, u32[]{:S(2)}) collective-permute-start(bf16[32,384]{1,0:T(8,128)(2,1)S(1)} %get-tuple-element.72), channel_id=1, source_target_pairs={{0,1},{1,2},{2,3},{3,0},{4,5},{5,6},{6,7},{7,4},{8,9},{9,10},{10,1... | collective-permute-start | bytes 73736 | tf_op jit(solution)/shard_map/ppermute | solution.py:472
  13.2 4.9 %collective-permute-start.3 = (bf16[32,384]{1,0:T(8,128)(2,1)S(1)}, bf16[32,384]{1,0:T(8,128)(2,1)S(1)}, u32[]{:S(2)}, u32[]{:S(2)}) collective-permute-start(bf16[32,384]{1,0:T(8,128)(2,1)S(1)} %get-tuple-element.77), channel_id=1, source_target_pairs={{0,3},{1,0},{2,1},{3,2},{4,7},{5,4},{6,5},{7,6},{8,11},{9,8},{10,9... | collective-permute-start | bytes 73736 | tf_op jit(solution)/shard_map/ppermute | solution.py:472
  21.1 21.9 %collective-permute-start.4 = (bf16[256,384]{1,0:T(8,128)(2,1)S(1)}, bf16[256,384]{1,0:T(8,128)(2,1)S(1)}, u32[]{:S(2)}, u32[]{:S(2)}) collective-permute-start(bf16[256,384]{1,0:T(8,128)(2,1)S(1)} %get-tuple-element.85), channel_id=1, source_target_pairs={{0,1},{1,0},{2,3},{3,2},{4,5},{5,4},{6,7},{7,6},{8,9},{9,8},{10,11... | collective-permute-start | bytes 589832 | tf_op jit(solution)/shard_map/ppermute | solution.py:477
  21.6 21.4 %collective-permute-start.5 = (bf16[256,384]{1,0:T(8,128)(2,1)S(1)}, bf16[256,384]{1,0:T(8,128)(2,1)S(1)}, u32[]{:S(2)}, u32[]{:S(2)}) collective-permute-start(bf16[256,384]{1,0:T(8,128)(2,1)S(1)} %get-tuple-element.86), channel_id=1, source_target_pairs={{0,2},{1,3},{2,0},{3,1},{4,6},{5,7},{6,4},{7,5},{8,10},{9,11},{10,... | collective-permute-start | bytes 589832 | tf_op jit(solution)/shard_map/ppermute | solution.py:477
  24.6 18.3 %collective-permute-start.6 = (bf16[256,384]{1,0:T(8,128)(2,1)S(1)}, bf16[256,384]{1,0:T(8,128)(2,1)S(1)}, u32[]{:S(2)}, u32[]{:S(2)}) collective-permute-start(bf16[256,384]{1,0:T(8,128)(2,1)S(1)} %get-tuple-element.87), channel_id=1, source_target_pairs={{0,3},{1,2},{2,1},{3,0},{4,7},{5,6},{6,5},{7,4},{8,11},{9,10},{10,... | collective-permute-start | bytes 589832 | tf_op jit(solution)/shard_map/ppermute | solution.py:477
  29.9 5.1 %collective-permute-start.7 = (f32[24,128]{1,0:T(8,128)S(1)}, f32[24,128]{1,0:T(8,128)S(1)}, u32[]{:S(2)}, u32[]{:S(2)}) collective-permute-start(f32[24,128]{1,0:T(8,128)S(1)} %get-tuple-element.97), channel_id=1, source_target_pairs={{0,1},{1,0},{2,3},{3,2},{4,5},{5,4},{6,7},{7,6},{8,9},{9,8},{10,11... | collective-permute-start | bytes 36872 | tf_op jit(solution)/shard_map/ppermute | solution.py:477
  30.0 13.0 %collective-permute-start.8 = (f32[24,128]{1,0:T(8,128)S(1)}, f32[24,128]{1,0:T(8,128)S(1)}, u32[]{:S(2)}, u32[]{:S(2)}) collective-permute-start(f32[24,128]{1,0:T(8,128)S(1)} %get-tuple-element.98), channel_id=1, source_target_pairs={{0,2},{1,3},{2,0},{3,1},{4,6},{5,7},{6,4},{7,5},{8,10},{9,11},{10,... | collective-permute-start | bytes 36872 | tf_op jit(solution)/shard_map/ppermute | solution.py:477
  35.0 7.9 %collective-permute-start.9 = (f32[24,128]{1,0:T(8,128)S(1)}, f32[24,128]{1,0:T(8,128)S(1)}, u32[]{:S(2)}, u32[]{:S(2)}) collective-permute-start(f32[24,128]{1,0:T(8,128)S(1)} %get-tuple-element.99), channel_id=1, source_target_pairs={{0,3},{1,2},{2,1},{3,0},{4,7},{5,6},{6,5},{7,4},{8,11},{9,10},{10,... | collective-permute-start | bytes 36872 | tf_op jit(solution)/shard_map/ppermute | solution.py:477
  44.7 8.9 %collective-permute-start.10 = (bf16[96,512]{1,0:T(8,128)(2,1)S(1)}, bf16[96,512]{1,0:T(8,128)(2,1)S(1)}, u32[]{:S(2)}, u32[]{:S(2)}) collective-permute-start(bf16[96,512]{1,0:T(8,128)(2,1)S(1)} %get-tuple-element.117), channel_id=1, source_target_pairs={{0,4},{4,8},{8,12},{12,0},{1,5},{5,9},{9,13},{13,1},{2,6},{6,10},{... | collective-permute-start | bytes 294920 | tf_op jit(solution)/shard_map/ppermute | solution.py:480
  44.8 8.9 %collective-permute-start.11 = (bf16[96,512]{1,0:T(8,128)(2,1)S(1)}, bf16[96,512]{1,0:T(8,128)(2,1)S(1)}, u32[]{:S(2)}, u32[]{:S(2)}) collective-permute-start(bf16[96,512]{1,0:T(8,128)(2,1)S(1)} %get-tuple-element.118), channel_id=1, source_target_pairs={{4,0},{8,4},{12,8},{0,12},{5,1},{9,5},{13,9},{1,13},{6,2},{10,6},{... | collective-permute-start | bytes 294920 | tf_op jit(solution)/shard_map/ppermute | solution.py:483
  46.5 7.5 %collective-permute-start.12 = (bf16[96,512]{1,0:T(8,128)(2,1)S(1)}, bf16[96,512]{1,0:T(8,128)(2,1)S(1)}, u32[]{:S(2)}, u32[]{:S(2)}) collective-permute-start(bf16[96,512]{1,0:T(8,128)(2,1)S(1)} %get-tuple-element.119), channel_id=1, source_target_pairs={{0,1},{1,2},{2,3},{3,0},{4,5},{5,6},{6,7},{7,4},{8,9},{9,10},{10,1... | collective-permute-start | bytes 294920 | tf_op jit(solution)/shard_map/ppermute | solution.py:472
  47.2 6.8 %collective-permute-start.13 = (bf16[96,512]{1,0:T(8,128)(2,1)S(1)}, bf16[96,512]{1,0:T(8,128)(2,1)S(1)}, u32[]{:S(2)}, u32[]{:S(2)}) collective-permute-start(bf16[96,512]{1,0:T(8,128)(2,1)S(1)} %get-tuple-element.120), channel_id=1, source_target_pairs={{0,3},{1,0},{2,1},{3,2},{4,7},{5,4},{6,5},{7,6},{8,11},{9,8},{10,9... | collective-permute-start | bytes 294920 | tf_op jit(solution)/shard_map/ppermute | solution.py:472
  58.0 8.9 %collective-permute-start.14 = (bf16[96,512]{1,0:T(8,128)(2,1)S(1)}, bf16[96,512]{1,0:T(8,128)(2,1)S(1)}, u32[]{:S(2)}, u32[]{:S(2)}) collective-permute-start(bf16[96,512]{1,0:T(8,128)(2,1)S(1)} %get-tuple-element.125), channel_id=1, source_target_pairs={{0,4},{4,8},{8,12},{12,0},{1,5},{5,9},{9,13},{13,1},{2,6},{6,10},{... | collective-permute-start | bytes 294920 | tf_op jit(solution)/shard_map/ppermute | solution.py:480
  58.0 8.8 %collective-permute-start.15 = (bf16[96,512]{1,0:T(8,128)(2,1)S(1)}, bf16[96,512]{1,0:T(8,128)(2,1)S(1)}, u32[]{:S(2)}, u32[]{:S(2)}) collective-permute-start(bf16[96,512]{1,0:T(8,128)(2,1)S(1)} %get-tuple-element.126), channel_id=1, source_target_pairs={{4,0},{8,4},{12,8},{0,12},{5,1},{9,5},{13,9},{1,13},{6,2},{10,6},{... | collective-permute-start | bytes 294920 | tf_op jit(solution)/shard_map/ppermute | solution.py:483
  59.8 7.2 %collective-permute-start.16 = (bf16[96,512]{1,0:T(8,128)(2,1)S(1)}, bf16[96,512]{1,0:T(8,128)(2,1)S(1)}, u32[]{:S(2)}, u32[]{:S(2)}) collective-permute-start(bf16[96,512]{1,0:T(8,128)(2,1)S(1)} %get-tuple-element.127), channel_id=1, source_target_pairs={{0,1},{1,2},{2,3},{3,0},{4,5},{5,6},{6,7},{7,4},{8,9},{9,10},{10,1... | collective-permute-start | bytes 294920 | tf_op jit(solution)/shard_map/ppermute | solution.py:472
  60.6 6.5 %collective-permute-start.17 = (bf16[96,512]{1,0:T(8,128)(2,1)S(1)}, bf16[96,512]{1,0:T(8,128)(2,1)S(1)}, u32[]{:S(2)}, u32[]{:S(2)}) collective-permute-start(bf16[96,512]{1,0:T(8,128)(2,1)S(1)} %get-tuple-element.128), channel_id=1, source_target_pairs={{0,3},{1,0},{2,1},{3,2},{4,7},{5,4},{6,5},{7,6},{8,11},{9,8},{10,9... | collective-permute-start | bytes 294920 | tf_op jit(solution)/shard_map/ppermute | solution.py:472
  69.1 10.1 %collective-permute-start.21 = (bf16[192,256]{1,0:T(8,128)(2,1)S(1)}, bf16[192,256]{1,0:T(8,128)(2,1)S(1)}, u32[]{:S(2)}, u32[]{:S(2)}) collective-permute-start(bf16[192,256]{1,0:T(8,128)(2,1)S(1)} %shard_map.204.refs_0_), channel_id=1, source_target_pairs={{0,1},{1,0},{2,3},{3,2},{4,5},{5,4},{6,7},{7,6},{8,9},{9,8},{10,11... | collective-permute-start | bytes 294920 | tf_op jit(solution)/shard_map/ppermute | solution.py:477
  70.5 12.6 %collective-permute-start.22 = (bf16[192,256]{1,0:T(8,128)(2,1)S(1)}, bf16[192,256]{1,0:T(8,128)(2,1)S(1)}, u32[]{:S(2)}, u32[]{:S(2)}) collective-permute-start(bf16[192,256]{1,0:T(8,128)(2,1)S(1)} %shard_map.204.refs_0_), channel_id=1, source_target_pairs={{0,2},{1,3},{2,0},{3,1},{4,6},{5,7},{6,4},{7,5},{8,10},{9,11},{10,... | collective-permute-start | bytes 294920 | tf_op jit(solution)/shard_map/ppermute | solution.py:477
  72.7 10.3 %collective-permute-start.23 = (bf16[192,256]{1,0:T(8,128)(2,1)S(1)}, bf16[192,256]{1,0:T(8,128)(2,1)S(1)}, u32[]{:S(2)}, u32[]{:S(2)}) collective-permute-start(bf16[192,256]{1,0:T(8,128)(2,1)S(1)} %shard_map.204.refs_0_), channel_id=1, source_target_pairs={{0,3},{1,2},{2,1},{3,0},{4,7},{5,6},{6,5},{7,4},{8,11},{9,10},{10,... | collective-permute-start | bytes 294920 | tf_op jit(solution)/shard_map/ppermute | solution.py:477
  75.6 9.0 %collective-permute-start.18 = (bf16[192,256]{1,0:T(8,128)(2,1)S(1)}, bf16[192,256]{1,0:T(8,128)(2,1)S(1)}, u32[]{:S(2)}, u32[]{:S(2)}) collective-permute-start(bf16[192,256]{1,0:T(8,128)(2,1)S(1)} %shard_map.203.refs_0_), channel_id=1, source_target_pairs={{0,1},{1,0},{2,3},{3,2},{4,5},{5,4},{6,7},{7,6},{8,9},{9,8},{10,11... | collective-permute-start | bytes 294920 | tf_op jit(solution)/shard_map/ppermute | solution.py:477
  76.0 12.6 %collective-permute-start.19 = (bf16[192,256]{1,0:T(8,128)(2,1)S(1)}, bf16[192,256]{1,0:T(8,128)(2,1)S(1)}, u32[]{:S(2)}, u32[]{:S(2)}) collective-permute-start(bf16[192,256]{1,0:T(8,128)(2,1)S(1)} %shard_map.203.refs_0_), channel_id=1, source_target_pairs={{0,2},{1,3},{2,0},{3,1},{4,6},{5,7},{6,4},{7,5},{8,10},{9,11},{10,... | collective-permute-start | bytes 294920 | tf_op jit(solution)/shard_map/ppermute | solution.py:477
  79.2 9.4 %collective-permute-start.20 = (bf16[192,256]{1,0:T(8,128)(2,1)S(1)}, bf16[192,256]{1,0:T(8,128)(2,1)S(1)}, u32[]{:S(2)}, u32[]{:S(2)}) collective-permute-start(bf16[192,256]{1,0:T(8,128)(2,1)S(1)} %shard_map.203.refs_0_), channel_id=1, source_target_pairs={{0,3},{1,2},{2,1},{3,0},{4,7},{5,6},{6,5},{7,4},{8,11},{9,10},{10,... | collective-permute-start | bytes 294920 | tf_op jit(solution)/shard_map/ppermute | solution.py:477
  (15 other events, 141.8 us)

commit v3 on v2

--- a/solution.py
+++ b/solution.py
@@ -396,7 +396,7 @@
 
 def layer_kernel(layer, only, wanted, chunk, *refs):
     local_ref, hidden_ref, terms_ref, owed_ref, gather_ref, scatter_ref, early_ref = refs[:7]
-    halo_refs, wu_ref = refs[7:11], refs[11]
+    halo_refs, wu_ref = refs[9:11] + refs[7:9], refs[11]
     last = only is not None
     if last:
         dec_ref, out_ref, known, sums = refs[12:]
@@ -426,7 +426,7 @@
     quantities, width = corr_refs[0].shape[0], u_ref.shape[1] // rows
     total = u_ref[member * quantities : (member + 1) * quantities, :]
     for s in range(slots):
-        total = total + dot(corr_refs[s][...], w_ref[s])
+        total = total + dot(corr_refs[s][...], w_ref[(slots - s) % slots])
     for r in range(rows):
         tile[pl.ds(r, quantities, stride=rows), :] = total[:, r * width : (r + 1) * width]
     size = quantities * rows
@@ -545,8 +545,7 @@
     parts, edge_sender, edge_receiver, outflow_node = lax.optimization_barrier(
         (parts, edge_sender, edge_receiver, outflow_node)
     )
-    got = [peer(parts[s], s) for s in range(lon - 1, 0, -1)]
-    parts = parts[:1] + got[::-1]
+    parts = parts[:1] + [peer(parts[s], s) for s in range(lon - 1, 0, -1)]
 
     known = 2 * nodes + 256 * -(-4 * wanted // 256)
     chunk = edges // 2
@@ -591,7 +590,6 @@
     )
     for layer in range(layers):
         halos = [shift(out[3], 1), shift(out[2], lon - 1), up(out[1]), down(out[0])]
-        halos = halos[2:] + halos[:2]
         early, terms = call(
             functools.partial(early_kernel, chunk),
             (shape((members, nodes, hid), F32), shape((members, edges, hid), F32)),
@@ -624,8 +622,7 @@
     corrs = [[v] + [peer(v, s) for s in range(lon - 1, 0, -1)] for v in corrs]
     out = None
     for m in range(members):
-        got = [corrs[m][0]] + corrs[m][:0:-1]
-        args = (u, onto, *got) if out is None else (u, onto, *got, out)
+        args = (u, onto, *corrs[m]) if out is None else (u, onto, *corrs[m], out)
         out = land(functools.partial(land_kernel, rows, lon, m), x, args, out is not None, rows * quantities, lon)
     return out.reshape(members, quantities, rows, width)
 

time: 90.6 us -> 89.3 us (0.986)
  starting transfers between devices: 38.1 us -> 36.3 us
    ppermute x12, starting transfers between devices: 20.5 us -> 18.7 us  [peer(): return lax.ppermute(v, 'lon', [(i, i ^ s) for i in range(lon)])]
where the time goes in v3:
time: 89.3 us; the launch traced here: 89 us
  Pallas kernels  37.3 us (42%)
  starting transfers between devices  36.3 us (41%)
  waiting for transfers between devices  12.6 us (14%)
  local copies, waits for them, and re-layouts  2.28 us (3%)
    pallas_call x15, Pallas kernels, call(): pl.pallas_call(kernel, out_shape=outs if single else tuple(outs), in_spec...  34.3 us
    ppermute x12, starting transfers between devices, peer(): return lax.ppermute(v, 'lon', [(i, i ^ s) for i in range(lon)])  18.7 us
    ppermute x6, starting transfers between devices, shift(): return lax.ppermute(v, 'lon', [(i, (i + s) % lon) for i in range(lon)])  11.6 us
    ppermute x12, waiting for transfers between devices, peer(): return lax.ppermute(v, 'lon', [(i, i ^ s) for i in range(lon)])  10.7 us
    ppermute x3, starting transfers between devices, down(): return lax.ppermute(v, 'lat', [((i + 1) % lat, i) for i in range(lat)])  5.48 us
    pallas_call x2, Pallas kernels, land(): pl.pallas_call(kernel, out_shape=shape(x.shape, F32), in_specs=spaces, ou...  3.05 us
    unnamed x30, local copies, waits for them, and re-layouts  2.28 us
    ppermute x3, waiting for transfers between devices, down(): return lax.ppermute(v, 'lat', [((i + 1) % lat, i) for i in range(lat)])  1.84 us
  transfers between devices with their start and end apart: 24, of which 6 were waited for; matrix products, arithmetic and copies ran while one was open for 0% of the time, Pallas kernels for 24%

profile of v3, /device:TPU:0, one launch (start us, length us, event | category | flops | bytes accessed | tf_op | source)
XLA Modules:
  0.0 89.0 jit_solution(1446041290928913586)
XLA Ops:
  0.0 3.3 %shard_map.190 = (bf16[784,128]{1,0:T(8,128)(2,1)}, bf16[784,128]{1,0:T(8,128)(2,1)}, f32[2,32,384]{2,1,0:T(8,128)}, f32[3,8,128]{2,1,0:T(8,128)}, f32[4,24,128]{2,1,0:T(8,128)}) custom-call(s32[1]{0:T(128)} %bitcast.2.me_ref, s32[16]{0:T(128)} %bitcast.18, f32[3072,128]{1,0:T(8,128)} %bitcast.10, f32[8,128]{1,0:T(8,128)} %refs_1_.2, f32[8,128]{1,0:T(8,128)} %refs_2_.2, ...), custom_call_target="tpu_custom_call" | custom-call | bytes 419430 | tf_op jit(solution)/shard_map/pallas_call | solution.py:32
  3.9 2.0 %collective-permute-start.1 = (bf16[784,128]{1,0:T(8,128)(2,1)}, bf16[784,128]{1,0:T(8,128)(2,1)S(1)}, u32[]{:S(2)}, u32[]{:S(2)}) collective-permute-start(bf16[784,128]{1,0:T(8,128)(2,1)} %get-tuple-element.68), channel_id=1, source_target_pairs={{4,0},{8,4},{12,8},{0,12},{5,1},{9,5},{13,9},{1,13},{6,2},{10,6},{... | collective-permute-start | bytes 602120 | tf_op jit(solution)/shard_map/ppermute | solution.py:483
  6.7 3.0 %shard_map.191.a_ref = bf16[4,256,1024]{2,1,0:T(8,128)(2,1)S(1)} custom-call(f32[4,24,128]{2,1,0:T(8,128)S(1)} %copy-done.7), custom_call_target="tpu_custom_call" | custom-call | flops 107374184 | bytes 209715 | tf_op jit(solution)/shard_map/pallas_call | solution.py:32
  9.6 1.8 %collective-permute-done.1.north_ref = bf16[784,128]{1,0:T(8,128)(2,1)S(1)} collective-permute-done((bf16[784,128]{1,0:T(8,128)(2,1)}, bf16[784,128]{1,0:T(8,128)(2,1)S(1)}, u32[]{:S(2)}, u32[]{:S(2)}) %collective-permute-start.1) | collective-permute-done | bytes 200736 | tf_op jit(solution)/shard_map/ppermute | solution.py:483
  13.2 2.2 %collective-permute-start.3 = (bf16[32,384]{1,0:T(8,128)(2,1)S(1)}, bf16[32,384]{1,0:T(8,128)(2,1)S(1)}, u32[]{:S(2)}, u32[]{:S(2)}) collective-permute-start(bf16[32,384]{1,0:T(8,128)(2,1)S(1)} %get-tuple-element.77), channel_id=1, source_target_pairs={{0,3},{1,0},{2,1},{3,2},{4,7},{5,4},{6,5},{7,6},{8,11},{9,8},{10,9... | collective-permute-start | bytes 73736 | tf_op jit(solution)/shard_map/ppermute | solution.py:472
  18.3 2.8 %shard_map.194 = (f32[384,1024]{1,0:T(8,128)S(1)}, f32[256,384]{1,0:T(8,128)S(1)}, bf16[256,384]{1,0:T(8,128)(2,1)S(1)}, bf16[256,384]{1,0:T(8,128)(2,1)S(1)}, bf16[256,384]{1,0:T(8,128)(2,1)S(1)}) custom-call(s32[1]{0:T(128)} %bitcast.lat_ref, f32[10,384,128]{2,1,0:T(8,128)S(1)} %get-tuple-element.75.mid_ref, f32[5,10,128]{2,1,0:T(8,128)S(1)} %get-tuple-element.76.rate, ...), custom_call_target="tpu_custom_call" | custom-call | flops 40265320 | bytes 838860 | tf_op jit(solution)/shard_map/pallas_call | solution.py:32
  21.1 3.0 %collective-permute-start.4 = (bf16[256,384]{1,0:T(8,128)(2,1)S(1)}, bf16[256,384]{1,0:T(8,128)(2,1)S(1)}, u32[]{:S(2)}, u32[]{:S(2)}) collective-permute-start(bf16[256,384]{1,0:T(8,128)(2,1)S(1)} %get-tuple-element.85), channel_id=1, source_target_pairs={{0,3},{1,2},{2,1},{3,0},{4,7},{5,6},{6,5},{7,4},{8,11},{9,10},{10,... | collective-permute-start | bytes 589832 | tf_op jit(solution)/shard_map/ppermute | solution.py:477
  26.3 3.6 %shard_map.195 = (bf16[1536,768]{1,0:T(8,128)(2,1)S(1)}, bf16[256,1536]{1,0:T(8,128)(2,1)S(1)}, s32[1]{0:T(128)}) custom-call(s32[1,1536]{1,0:T(1,128)S(1)} %bitcast.15, s32[1,1536]{1,0:T(1,128)S(1)} %bitcast.16), custom_call_target="tpu_custom_call" | custom-call | flops 11324620 | bytes 419430 | tf_op jit(solution)/shard_map/pallas_call | solution.py:32
  30.5 2.9 %collective-permute-start.8 = (f32[24,128]{1,0:T(8,128)S(1)}, f32[24,128]{1,0:T(8,128)S(1)}, u32[]{:S(2)}, u32[]{:S(2)}) collective-permute-start(f32[24,128]{1,0:T(8,128)S(1)} %get-tuple-element.98), channel_id=1, source_target_pairs={{0,2},{1,3},{2,0},{3,1},{4,6},{5,7},{6,4},{7,5},{8,10},{9,11},{10,... | collective-permute-start | bytes 36872 | tf_op jit(solution)/shard_map/ppermute | solution.py:477
  33.4 3.4 %collective-permute-done.7.refs_1_ = f32[24,128]{1,0:T(8,128)S(1)} collective-permute-done((f32[24,128]{1,0:T(8,128)S(1)}, f32[24,128]{1,0:T(8,128)S(1)}, u32[]{:S(2)}, u32[]{:S(2)}) %collective-permute-start.7) | collective-permute-done | bytes 12320 | tf_op jit(solution)/shard_map/ppermute | solution.py:477
  36.8 1.8 %collective-permute-start.9 = (f32[24,128]{1,0:T(8,128)S(1)}, f32[24,128]{1,0:T(8,128)S(1)}, u32[]{:S(2)}, u32[]{:S(2)}) collective-permute-start(f32[24,128]{1,0:T(8,128)S(1)} %get-tuple-element.99), channel_id=1, source_target_pairs={{0,3},{1,2},{2,1},{3,0},{4,7},{5,6},{6,5},{7,4},{8,11},{9,10},{10,... | collective-permute-start | bytes 36872 | tf_op jit(solution)/shard_map/ppermute | solution.py:477
  38.8 2.0 %collective-permute-done.8.refs_2_ = f32[24,128]{1,0:T(8,128)S(1)} collective-permute-done((f32[24,128]{1,0:T(8,128)S(1)}, f32[24,128]{1,0:T(8,128)S(1)}, u32[]{:S(2)}, u32[]{:S(2)}) %collective-permute-start.8) | collective-permute-done | bytes 12320 | tf_op jit(solution)/shard_map/ppermute | solution.py:477
  44.9 3.1 %collective-permute-start.11 = (bf16[96,512]{1,0:T(8,128)(2,1)S(1)}, bf16[96,512]{1,0:T(8,128)(2,1)S(1)}, u32[]{:S(2)}, u32[]{:S(2)}) collective-permute-start(bf16[96,512]{1,0:T(8,128)(2,1)S(1)} %get-tuple-element.118), channel_id=1, source_target_pairs={{0,3},{1,0},{2,1},{3,2},{4,7},{5,4},{6,5},{7,6},{8,11},{9,8},{10,9... | collective-permute-start | bytes 294920 | tf_op jit(solution)/shard_map/ppermute | solution.py:472
  49.7 3.3 %shard_map.200 = (f32[2,256,512]{2,1,0:T(8,128)S(1)}, f32[2,1536,512]{2,1,0:T(8,128)S(1)}) custom-call(s32[1]{0:T(128)} %get-tuple-element.104.local_ref.refs_0_, bf16[2,512,512]{2,1,0:T(8,128)(2,1)S(1)} %get-tuple-element.112.table_ref, bf16[1536,768]{1,0:T(8,128)(2,1)S(1)} %get-tuple-element.113.gather_ref.refs_4_, ...), custom_call_target="tpu_custom_call" | custom-call | flops 150000000 | bytes 419430 | tf_op jit(solution)/shard_map/pallas_call | solution.py:32
  53.1 4.0 %shard_map.201 = (f32[2,256,512]{2,1,0:T(8,128)S(1)}, bf16[2,512,512]{2,1,0:T(8,128)(2,1)S(1)}, bf16[96,512]{1,0:T(8,128)(2,1)S(1)}, bf16[96,512]{1,0:T(8,128)(2...) custom-call(s32[1]{0:T(128)} %get-tuple-element.104.local_ref.refs_0_, ...), custom_call_target="tpu_custom_call" | custom-call | flops 200000000 | bytes 629145 | tf_op jit(solution)/shard_map/pallas_call | solution.py:32
  57.2 3.8 %collective-permute-start.15 = (bf16[96,512]{1,0:T(8,128)(2,1)S(1)}, bf16[96,512]{1,0:T(8,128)(2,1)S(1)}, u32[]{:S(2)}, u32[]{:S(2)}) collective-permute-start(bf16[96,512]{1,0:T(8,128)(2,1)S(1)} %get-tuple-element.126), channel_id=1, source_target_pairs={{0,3},{1,0},{2,1},{3,2},{4,7},{5,4},{6,5},{7,6},{8,11},{9,8},{10,9... | collective-permute-start | bytes 294920 | tf_op jit(solution)/shard_map/ppermute | solution.py:472
  62.7 3.2 %shard_map.202 = (f32[2,256,512]{2,1,0:T(8,128)S(1)}, f32[2,1536,512]{2,1,0:T(8,128)S(1)}) custom-call(s32[1]{0:T(128)} %get-tuple-element.104.local_ref.refs_0_, bf16[2,512,512]{2,1,0:T(8,128)(2,1)S(1)} %get-tuple-element.122.table_ref, bf16[1536,768]{1,0:T(8,128)(2,1)S(1)} %get-tuple-element.113.gather_ref.refs_4_, ...), custom_call_target="tpu_custom_call" | custom-call | flops 150000000 | bytes 419430 | tf_op jit(solution)/shard_map/pallas_call | solution.py:32
  66.0 2.0 %shard_map.204.refs_0_ = bf16[192,256]{1,0:T(8,128)(2,1)S(1)} custom-call(s32[1]{0:T(128)} %get-tuple-element.104.local_ref.refs_0_, f32[2,256,512]{2,1,0:T(8,128)S(1)} %get-tuple-element.121.refs_1_, f32[2,1536,512]{2,1,0:T(8,128)S(1)} %get-tuple-element.123.refs_2_, bf16[192,256]{1,0:T(8,128)(2,1)S(1)} %get-tuple-element.110.refs_7_.refs_3_, ...), custom_call_target="tpu_custom_call" | custom-call | flops 100000000 | bytes 419430 | tf_op jit(solution)/shard_map/pallas_call | solution.py:32
  68.1 1.8 %collective-permute-start.21 = (bf16[192,256]{1,0:T(8,128)(2,1)S(1)}, bf16[192,256]{1,0:T(8,128)(2,1)S(1)}, u32[]{:S(2)}, u32[]{:S(2)}) collective-permute-start(bf16[192,256]{1,0:T(8,128)(2,1)S(1)} %shard_map.204.refs_0_), channel_id=1, source_target_pairs={{0,3},{1,2},{2,1},{3,0},{4,7},{5,6},{6,5},{7,4},{8,11},{9,10},{10,... | collective-permute-start | bytes 294920 | tf_op jit(solution)/shard_map/ppermute | solution.py:477
  69.8 2.7 %collective-permute-start.23 = (bf16[192,256]{1,0:T(8,128)(2,1)S(1)}, bf16[192,256]{1,0:T(8,128)(2,1)S(1)}, u32[]{:S(2)}, u32[]{:S(2)}) collective-permute-start(bf16[192,256]{1,0:T(8,128)(2,1)S(1)} %shard_map.204.refs_0_), channel_id=1, source_target_pairs={{0,1},{1,0},{2,3},{3,2},{4,5},{5,4},{6,7},{7,6},{8,9},{9,8},{10,11... | collective-permute-start | bytes 294920 | tf_op jit(solution)/shard_map/ppermute | solution.py:477
  72.5 2.0 %shard_map.203.refs_0_ = bf16[192,256]{1,0:T(8,128)(2,1)S(1)} custom-call(s32[1]{0:T(128)} %get-tuple-element.104.local_ref.refs_0_, f32[2,256,512]{2,1,0:T(8,128)S(1)} %get-tuple-element.121.refs_1_, f32[2,1536,512]{2,1,0:T(8,128)S(1)} %get-tuple-element.123.refs_2_, bf16[192,256]{1,0:T(8,128)(2,1)S(1)} %get-tuple-element.110.refs_7_.refs_3_, ...), custom_call_target="tpu_custom_call" | custom-call | flops 100000000 | bytes 419430 | tf_op jit(solution)/shard_map/pallas_call | solution.py:32
  76.3 2.7 %collective-permute-start.20 = (bf16[192,256]{1,0:T(8,128)(2,1)S(1)}, bf16[192,256]{1,0:T(8,128)(2,1)S(1)}, u32[]{:S(2)}, u32[]{:S(2)}) collective-permute-start(bf16[192,256]{1,0:T(8,128)(2,1)S(1)} %shard_map.203.refs_0_), channel_id=1, source_target_pairs={{0,1},{1,0},{2,3},{3,2},{4,5},{5,4},{6,7},{7,6},{8,9},{9,8},{10,11... | collective-permute-start | bytes 294920 | tf_op jit(solution)/shard_map/ppermute | solution.py:477
  79.0 3.0 %shard_map.197.w_ref = bf16[4,256,1024]{2,1,0:T(8,128)(2,1)S(1)} custom-call(f32[24,128]{1,0:T(8,128)S(1)} %get-tuple-element.100.refs_0_, f32[24,128]{1,0:T(8,128)S(1)} %collective-permute-done.7.refs_1_, f32[24,128]{1,0:T(8,128)S(1)} %collective-permute-done.8.refs_2_, f32[24,128]{1,0:T(8,128)S(1)} %collective-permute-done.9.refs_3_), custom_call_target="tpu_custom_call" | custom-call | flops 107374184 | bytes 209715 | tf_op jit(solution)/shard_map/pallas_call | solution.py:32
  84.9 2.4 %collective-permute-done.19.refs_2_ = bf16[192,256]{1,0:T(8,128)(2,1)S(1)} collective-permute-done((bf16[192,256]{1,0:T(8,128)(2,1)S(1)}, bf16[192,256]{1,0:T(8,128)(2,1)S(1)}, u32[]{:S(2)}, u32[]{:S(2)}) %collective-permute-start.19) | collective-permute-done | bytes 98336 | tf_op jit(solution)/shard_map/ppermute | solution.py:477
  (71 shorter events, 22.5 us)
Async XLA Ops:
  3.4 6.3 %collective-permute-start = (bf16[784,128]{1,0:T(8,128)(2,1)}, bf16[784,128]{1,0:T(8,128)(2,1)S(1)}, u32[]{:S(2)}, u32[]{:S(2)}) collective-permute-start(bf16[784,128]{1,0:T(8,128)(2,1)} %get-tuple-element.67), channel_id=1, source_target_pairs={{0,4},{4,8},{8,12},{12,0},{1,5},{5,9},{9,13},{13,1},{2,6},{6,10},{... | collective-permute-start | bytes 602120 | tf_op jit(solution)/shard_map/ppermute | solution.py:480
  3.9 7.6 %collective-permute-start.1 = (bf16[784,128]{1,0:T(8,128)(2,1)}, bf16[784,128]{1,0:T(8,128)(2,1)S(1)}, u32[]{:S(2)}, u32[]{:S(2)}) collective-permute-start(bf16[784,128]{1,0:T(8,128)(2,1)} %get-tuple-element.68), channel_id=1, source_target_pairs={{4,0},{8,4},{12,8},{0,12},{5,1},{9,5},{13,9},{1,13},{6,2},{10,6},{... | collective-permute-start | bytes 602120 | tf_op jit(solution)/shard_map/ppermute | solution.py:483
  11.6 6.5 %collective-permute-start.2 = (bf16[32,384]{1,0:T(8,128)(2,1)S(1)}, bf16[32,384]{1,0:T(8,128)(2,1)S(1)}, u32[]{:S(2)}, u32[]{:S(2)}) collective-permute-start(bf16[32,384]{1,0:T(8,128)(2,1)S(1)} %get-tuple-element.72), channel_id=1, source_target_pairs={{0,1},{1,2},{2,3},{3,0},{4,5},{5,6},{6,7},{7,4},{8,9},{9,10},{10,1... | collective-permute-start | bytes 73736 | tf_op jit(solution)/shard_map/ppermute | solution.py:472
  13.2 4.9 %collective-permute-start.3 = (bf16[32,384]{1,0:T(8,128)(2,1)S(1)}, bf16[32,384]{1,0:T(8,128)(2,1)S(1)}, u32[]{:S(2)}, u32[]{:S(2)}) collective-permute-start(bf16[32,384]{1,0:T(8,128)(2,1)S(1)} %get-tuple-element.77), channel_id=1, source_target_pairs={{0,3},{1,0},{2,1},{3,2},{4,7},{5,4},{6,5},{7,6},{8,11},{9,8},{10,9... | collective-permute-start | bytes 73736 | tf_op jit(solution)/shard_map/ppermute | solution.py:472
  21.1 21.3 %collective-permute-start.4 = (bf16[256,384]{1,0:T(8,128)(2,1)S(1)}, bf16[256,384]{1,0:T(8,128)(2,1)S(1)}, u32[]{:S(2)}, u32[]{:S(2)}) collective-permute-start(bf16[256,384]{1,0:T(8,128)(2,1)S(1)} %get-tuple-element.85), channel_id=1, source_target_pairs={{0,3},{1,2},{2,1},{3,0},{4,7},{5,6},{6,5},{7,4},{8,11},{9,10},{10,... | collective-permute-start | bytes 589832 | tf_op jit(solution)/shard_map/ppermute | solution.py:477
  24.1 18.3 %collective-permute-start.5 = (bf16[256,384]{1,0:T(8,128)(2,1)S(1)}, bf16[256,384]{1,0:T(8,128)(2,1)S(1)}, u32[]{:S(2)}, u32[]{:S(2)}) collective-permute-start(bf16[256,384]{1,0:T(8,128)(2,1)S(1)} %get-tuple-element.86), channel_id=1, source_target_pairs={{0,2},{1,3},{2,0},{3,1},{4,6},{5,7},{6,4},{7,5},{8,10},{9,11},{10,... | collective-permute-start | bytes 589832 | tf_op jit(solution)/shard_map/ppermute | solution.py:477
  24.1 18.3 %collective-permute-start.6 = (bf16[256,384]{1,0:T(8,128)(2,1)S(1)}, bf16[256,384]{1,0:T(8,128)(2,1)S(1)}, u32[]{:S(2)}, u32[]{:S(2)}) collective-permute-start(bf16[256,384]{1,0:T(8,128)(2,1)S(1)} %get-tuple-element.87), channel_id=1, source_target_pairs={{0,1},{1,0},{2,3},{3,2},{4,5},{5,4},{6,7},{7,6},{8,9},{9,8},{10,11... | collective-permute-start | bytes 589832 | tf_op jit(solution)/shard_map/ppermute | solution.py:477
  29.9 6.9 %collective-permute-start.7 = (f32[24,128]{1,0:T(8,128)S(1)}, f32[24,128]{1,0:T(8,128)S(1)}, u32[]{:S(2)}, u32[]{:S(2)}) collective-permute-start(f32[24,128]{1,0:T(8,128)S(1)} %get-tuple-element.97), channel_id=1, source_target_pairs={{0,1},{1,0},{2,3},{3,2},{4,5},{5,4},{6,7},{7,6},{8,9},{9,8},{10,11... | collective-permute-start | bytes 36872 | tf_op jit(solution)/shard_map/ppermute | solution.py:477
  30.5 10.2 %collective-permute-start.8 = (f32[24,128]{1,0:T(8,128)S(1)}, f32[24,128]{1,0:T(8,128)S(1)}, u32[]{:S(2)}, u32[]{:S(2)}) collective-permute-start(f32[24,128]{1,0:T(8,128)S(1)} %get-tuple-element.98), channel_id=1, source_target_pairs={{0,2},{1,3},{2,0},{3,1},{4,6},{5,7},{6,4},{7,5},{8,10},{9,11},{10,... | collective-permute-start | bytes 36872 | tf_op jit(solution)/shard_map/ppermute | solution.py:477
  36.8 5.5 %collective-permute-start.9 = (f32[24,128]{1,0:T(8,128)S(1)}, f32[24,128]{1,0:T(8,128)S(1)}, u32[]{:S(2)}, u32[]{:S(2)}) collective-permute-start(f32[24,128]{1,0:T(8,128)S(1)} %get-tuple-element.99), channel_id=1, source_target_pairs={{0,3},{1,2},{2,1},{3,0},{4,7},{5,6},{6,5},{7,4},{8,11},{9,10},{10,... | collective-permute-start | bytes 36872 | tf_op jit(solution)/shard_map/ppermute | solution.py:477
  44.1 8.9 %collective-permute-start.10 = (bf16[96,512]{1,0:T(8,128)(2,1)S(1)}, bf16[96,512]{1,0:T(8,128)(2,1)S(1)}, u32[]{:S(2)}, u32[]{:S(2)}) collective-permute-start(bf16[96,512]{1,0:T(8,128)(2,1)S(1)} %get-tuple-element.117), channel_id=1, source_target_pairs={{0,1},{1,2},{2,3},{3,0},{4,5},{5,6},{6,7},{7,4},{8,9},{9,10},{10,1... | collective-permute-start | bytes 294920 | tf_op jit(solution)/shard_map/ppermute | solution.py:472
  44.9 8.2 %collective-permute-start.11 = (bf16[96,512]{1,0:T(8,128)(2,1)S(1)}, bf16[96,512]{1,0:T(8,128)(2,1)S(1)}, u32[]{:S(2)}, u32[]{:S(2)}) collective-permute-start(bf16[96,512]{1,0:T(8,128)(2,1)S(1)} %get-tuple-element.118), channel_id=1, source_target_pairs={{0,3},{1,0},{2,1},{3,2},{4,7},{5,4},{6,5},{7,6},{8,11},{9,8},{10,9... | collective-permute-start | bytes 294920 | tf_op jit(solution)/shard_map/ppermute | solution.py:472
  48.0 5.1 %collective-permute-start.12 = (bf16[96,512]{1,0:T(8,128)(2,1)S(1)}, bf16[96,512]{1,0:T(8,128)(2,1)S(1)}, u32[]{:S(2)}, u32[]{:S(2)}) collective-permute-start(bf16[96,512]{1,0:T(8,128)(2,1)S(1)} %get-tuple-element.119), channel_id=1, source_target_pairs={{0,4},{4,8},{8,12},{12,0},{1,5},{5,9},{9,13},{13,1},{2,6},{6,10},{... | collective-permute-start | bytes 294920 | tf_op jit(solution)/shard_map/ppermute | solution.py:480
  48.0 5.1 %collective-permute-start.13 = (bf16[96,512]{1,0:T(8,128)(2,1)S(1)}, bf16[96,512]{1,0:T(8,128)(2,1)S(1)}, u32[]{:S(2)}, u32[]{:S(2)}) collective-permute-start(bf16[96,512]{1,0:T(8,128)(2,1)S(1)} %get-tuple-element.120), channel_id=1, source_target_pairs={{4,0},{8,4},{12,8},{0,12},{5,1},{9,5},{13,9},{1,13},{6,2},{10,6},{... | collective-permute-start | bytes 294920 | tf_op jit(solution)/shard_map/ppermute | solution.py:483
  57.1 8.9 %collective-permute-start.14 = (bf16[96,512]{1,0:T(8,128)(2,1)S(1)}, bf16[96,512]{1,0:T(8,128)(2,1)S(1)}, u32[]{:S(2)}, u32[]{:S(2)}) collective-permute-start(bf16[96,512]{1,0:T(8,128)(2,1)S(1)} %get-tuple-element.125), channel_id=1, source_target_pairs={{0,1},{1,2},{2,3},{3,0},{4,5},{5,6},{6,7},{7,4},{8,9},{9,10},{10,1... | collective-permute-start | bytes 294920 | tf_op jit(solution)/shard_map/ppermute | solution.py:472
  57.2 8.8 %collective-permute-start.15 = (bf16[96,512]{1,0:T(8,128)(2,1)S(1)}, bf16[96,512]{1,0:T(8,128)(2,1)S(1)}, u32[]{:S(2)}, u32[]{:S(2)}) collective-permute-start(bf16[96,512]{1,0:T(8,128)(2,1)S(1)} %get-tuple-element.126), channel_id=1, source_target_pairs={{0,3},{1,0},{2,1},{3,2},{4,7},{5,4},{6,5},{7,6},{8,11},{9,8},{10,9... | collective-permute-start | bytes 294920 | tf_op jit(solution)/shard_map/ppermute | solution.py:472
  61.0 5.0 %collective-permute-start.16 = (bf16[96,512]{1,0:T(8,128)(2,1)S(1)}, bf16[96,512]{1,0:T(8,128)(2,1)S(1)}, u32[]{:S(2)}, u32[]{:S(2)}) collective-permute-start(bf16[96,512]{1,0:T(8,128)(2,1)S(1)} %get-tuple-element.127), channel_id=1, source_target_pairs={{0,4},{4,8},{8,12},{12,0},{1,5},{5,9},{9,13},{13,1},{2,6},{6,10},{... | collective-permute-start | bytes 294920 | tf_op jit(solution)/shard_map/ppermute | solution.py:480
  61.0 5.0 %collective-permute-start.17 = (bf16[96,512]{1,0:T(8,128)(2,1)S(1)}, bf16[96,512]{1,0:T(8,128)(2,1)S(1)}, u32[]{:S(2)}, u32[]{:S(2)}) collective-permute-start(bf16[96,512]{1,0:T(8,128)(2,1)S(1)} %get-tuple-element.128), channel_id=1, source_target_pairs={{4,0},{8,4},{12,8},{0,12},{5,1},{9,5},{13,9},{1,13},{6,2},{10,6},{... | collective-permute-start | bytes 294920 | tf_op jit(solution)/shard_map/ppermute | solution.py:483
  68.1 8.3 %collective-permute-start.21 = (bf16[192,256]{1,0:T(8,128)(2,1)S(1)}, bf16[192,256]{1,0:T(8,128)(2,1)S(1)}, u32[]{:S(2)}, u32[]{:S(2)}) collective-permute-start(bf16[192,256]{1,0:T(8,128)(2,1)S(1)} %shard_map.204.refs_0_), channel_id=1, source_target_pairs={{0,3},{1,2},{2,1},{3,0},{4,7},{5,6},{6,5},{7,4},{8,11},{9,10},{10,... | collective-permute-start | bytes 294920 | tf_op jit(solution)/shard_map/ppermute | solution.py:477
  69.8 13.5 %collective-permute-start.22 = (bf16[192,256]{1,0:T(8,128)(2,1)S(1)}, bf16[192,256]{1,0:T(8,128)(2,1)S(1)}, u32[]{:S(2)}, u32[]{:S(2)}) collective-permute-start(bf16[192,256]{1,0:T(8,128)(2,1)S(1)} %shard_map.204.refs_0_), channel_id=1, source_target_pairs={{0,2},{1,3},{2,0},{3,1},{4,6},{5,7},{6,4},{7,5},{8,10},{9,11},{10,... | collective-permute-start | bytes 294920 | tf_op jit(solution)/shard_map/ppermute | solution.py:477
  69.8 13.5 %collective-permute-start.23 = (bf16[192,256]{1,0:T(8,128)(2,1)S(1)}, bf16[192,256]{1,0:T(8,128)(2,1)S(1)}, u32[]{:S(2)}, u32[]{:S(2)}) collective-permute-start(bf16[192,256]{1,0:T(8,128)(2,1)S(1)} %shard_map.204.refs_0_), channel_id=1, source_target_pairs={{0,1},{1,0},{2,3},{3,2},{4,5},{5,4},{6,7},{7,6},{8,9},{9,8},{10,11... | collective-permute-start | bytes 294920 | tf_op jit(solution)/shard_map/ppermute | solution.py:477
  74.6 10.3 %collective-permute-start.18 = (bf16[192,256]{1,0:T(8,128)(2,1)S(1)}, bf16[192,256]{1,0:T(8,128)(2,1)S(1)}, u32[]{:S(2)}, u32[]{:S(2)}) collective-permute-start(bf16[192,256]{1,0:T(8,128)(2,1)S(1)} %shard_map.203.refs_0_), channel_id=1, source_target_pairs={{0,3},{1,2},{2,1},{3,0},{4,7},{5,6},{6,5},{7,4},{8,11},{9,10},{10,... | collective-permute-start | bytes 294920 | tf_op jit(solution)/shard_map/ppermute | solution.py:477
  76.3 10.9 %collective-permute-start.19 = (bf16[192,256]{1,0:T(8,128)(2,1)S(1)}, bf16[192,256]{1,0:T(8,128)(2,1)S(1)}, u32[]{:S(2)}, u32[]{:S(2)}) collective-permute-start(bf16[192,256]{1,0:T(8,128)(2,1)S(1)} %shard_map.203.refs_0_), channel_id=1, source_target_pairs={{0,2},{1,3},{2,0},{3,1},{4,6},{5,7},{6,4},{7,5},{8,10},{9,11},{10,... | collective-permute-start | bytes 294920 | tf_op jit(solution)/shard_map/ppermute | solution.py:477
  76.3 10.9 %collective-permute-start.20 = (bf16[192,256]{1,0:T(8,128)(2,1)S(1)}, bf16[192,256]{1,0:T(8,128)(2,1)S(1)}, u32[]{:S(2)}, u32[]{:S(2)}) collective-permute-start(bf16[192,256]{1,0:T(8,128)(2,1)S(1)} %shard_map.203.refs_0_), channel_id=1, source_target_pairs={{0,1},{1,0},{2,3},{3,2},{4,5},{5,4},{6,7},{7,6},{8,9},{9,8},{10,11... | collective-permute-start | bytes 294920 | tf_op jit(solution)/shard_map/ppermute | solution.py:477
  (15 other events, 140.1 us)

commit v4 on v3

--- a/solution.py
+++ b/solution.py
@@ -66,8 +66,8 @@
     return 1.0 - pe + ne - pn + nn - 4.0 * d, pe + d, d - ne, pn + d, d - nn
 
 
-def edge_kernel(rows, slots, me_ref, owner_ref, *refs):
-    homes, (up_ref, down_ref, side_ref, rate_ref, in_ref) = refs[:8], refs[8:13]
+def edge_kernel(rows, slots, me_ref, lat_ref, owner_ref, *refs):
+    homes, (first_ref, second_ref, side_ref, rate_ref, in_ref) = refs[:8], refs[8:13]
     x_ref, halo_ref, block, taken, *tables, sems = refs[13:]
     held = [x_ref, *(rate_ref.at[j] for j in range(3)), halo_ref, *tables]
     copies = [pltpu.make_async_copy(a, b, sems.at[k]) for k, (a, b) in enumerate(zip(homes, held))]
@@ -84,15 +84,17 @@
     def row(r):
         return x_ref[pl.ds(r, count, stride=rows), :].astype(BF16)
 
-    for out_ref, near, far, q in ((up_ref, rows - 1, rows - 2, 1), (down_ref, 0, 1, 0)):
+    odd = lax.rem(lat_ref[0], 2)
+    for out_ref, south in ((first_ref, odd), (second_ref, 1 - odd)):
+        near, far = (1 - south) * (rows - 1), south + (1 - south) * (rows - 2)
         out_ref[0:count, :] = row(near)
         out_ref[count : 2 * count, :] = row(far)
         block[...] = jnp.zeros(block.shape, F32)
         for j in range(3):
-            hi, lo = split(rate_ref[j, near : near + 1, :])
+            hi, lo = split(rate_ref[j, pl.ds(near, 1), :])
             block[j : j + 1, :] = hi
             block[j + 3 : j + 4, :] = lo
-        block[6:7, 0:wanted] = halo_ref[q : q + 1, :].astype(F32)
+        block[6:7, 0:wanted] = halo_ref[pl.ds(1 - south, 1), :].astype(F32)
         out_ref[2 * count : 2 * count + 16, :] = block[...].astype(BF16)
     lane = iota((rows, count), 1)
     for i, (c, q) in enumerate(((width - 1, 3), (0, 2))):
@@ -111,7 +113,17 @@
             side_ref[i, rows + r : rows + r + 1, :] = got[k + 1 : k + 2, :]
 
 
-def side_kernel(rows, south_ref, north_ref, side_ref, east_ref, west_ref):
+def side_kernel(rows, lat_ref, first_ref, second_ref, side_ref, east_ref, west_ref, south_ref, north_ref):
+    @pl.when(lax.rem(lat_ref[0], 2) == 0)
+    def _():
+        south_ref[...] = second_ref[...]
+        north_ref[...] = first_ref[...]
+
+    @pl.when(lax.rem(lat_ref[0], 2) == 1)
+    def _():
+        south_ref[...] = first_ref[...]
+        north_ref[...] = second_ref[...]
+
     count, width = side_ref.shape[2], south_ref.shape[1]
     pick = pick_columns(width)
     south = dot(pick, south_ref[0:count, :], 1, 1)
@@ -276,8 +288,8 @@
         part_refs[s][...] = dot(a_ref[s], flat[...], 1, 1).astype(part_refs[s].dtype)
 
 
-def silu(v):
-    return 0.5 * v * (1.0 + jnp.tanh(0.5 * v))
+def silu_of_half(h):
+    return h + h * jnp.tanh(h)
 
 
 def normalize(v):
@@ -303,10 +315,10 @@
     cols = dot(order[...], keys, 1, 1)
     sender, receiver = cols[:, 0:1] + nodes * cols[:, 1:2], cols[:, 2:3]
     lane = iota((edges, nodes), 1).astype(F32)
-    gather_ref[:, 0:nodes] = jnp.where(sender == lane, 1.0, 0.0).astype(BF16)
-    gather_ref[:, nodes : 2 * nodes] = jnp.where(receiver == lane, 1.0, 0.0).astype(BF16)
+    gather_ref[:, 0:nodes] = jnp.where(sender == lane, 0.5, 0.0).astype(BF16)
+    gather_ref[:, nodes : 2 * nodes] = jnp.where(receiver == lane, 0.5, 0.0).astype(BF16)
     rest = (iota((edges, known - 2 * nodes), 1) + nodes).astype(F32)
-    gather_ref[:, 2 * nodes :] = jnp.where(sender == rest, 1.0, 0.0).astype(BF16)
+    gather_ref[:, 2 * nodes :] = jnp.where(sender == rest, 0.5, 0.0).astype(BF16)
     row = dot(keys, order[...], 1, 1)[2:3, :]
     scatter_ref[...] = jnp.where(row == iota((nodes, edges), 0).astype(F32), 1.0, 0.0).astype(BF16)
 
@@ -344,7 +356,7 @@
         total = total + ref[...].astype(F32)
     total = total.astype(BF16)
     for m in range(hidden_ref.shape[0]):
-        hidden = silu(dot(total, pad_ref[m]))
+        hidden = silu_of_half(0.5 * dot(total, pad_ref[m]))
         hidden_ref[m] = hidden
         project(m, hidden, owed, ws_ref[0], wr_ref[0], table_ref, out_refs, wanted, nodes)
 
@@ -368,7 +380,7 @@
         def _():
             for m in range(members):
                 found = [
-                    silu(dot(gather_ref[pl.ds(at + k, n), 0:depth], table_ref[m])).astype(BF16)
+                    silu_of_half(dot(gather_ref[pl.ds(at + k, n), 0:depth], table_ref[m])).astype(BF16)
                     for k, n in pieces(chunk)
                 ]
                 sums_ref[m] += dot(scatter_ref[:, pl.ds(at, chunk)], jnp.concatenate(found, 0))
@@ -390,7 +402,7 @@
             found = []
             for k, n in pieces(chunk):
                 v = terms_ref[m, pl.ds(at + k, n), :] + dot(gather_ref[pl.ds(at + k, n), depth:], known[m])
-                found.append(silu(v).astype(BF16))
+                found.append(silu_of_half(v).astype(BF16))
             sums_ref[m] += dot(scatter_ref[:, pl.ds(at, chunk)], jnp.concatenate(found, 0))
 
 
@@ -488,12 +500,12 @@
     tall = 2 * count + 16
     tables = (inflow_node, inflow_cell, inflow_weight)
     taken = pltpu.SMEM((lon,), I32)
-    to_north, to_south, side, wind, in_lists = call(
+    first, second, side, wind, in_lists = call(
         functools.partial(edge_kernel, rows, lon),
         [shape((tall, width), BF16), shape((tall, width), BF16), shape((2, 4 * rows, count), F32),
          shape((3, rows, width), F32), shape((lon, 3 * cap, entries), F32)],
-        (me, inflow_owner.reshape(blocks), x, *rates, halo, *tables),
-        smem=2,
+        (me, lat_at, inflow_owner.reshape(blocks), x, *rates, halo, *tables),
+        smem=3,
         away=8,
         scratch=[
             pltpu.VMEM(x.shape, F32),
@@ -506,13 +518,17 @@
         vmem=56,
         cost=cost(0, 8 * MIB),
     )
-    south, north = up(to_north), down(to_south)
+    first, second = (
+        lax.ppermute(v, "lat", [(i, j if 0 <= (j := ((i - k) ^ 1) + k) < lat else i) for i in range(lat)])
+        for k, v in enumerate((first, second))
+    )
     into = build(lon, nodes, cells, (in_lists,))
     side, into = lax.optimization_barrier((side, into))
-    to_east, to_west = call(
+    to_east, to_west, south, north = call(
         functools.partial(side_kernel, rows),
-        (shape((4 * rows, count), BF16), shape((4 * rows, count), BF16)),
-        (south, north, side),
+        [shape((4 * rows, count), BF16)] * 2 + [shape((tall, width), BF16)] * 2,
+        (lat_at, first, second, side),
+        smem=1,
         vmem=4,
         cost=cost(0, 4 * MIB),
     )

time: 89.3 us -> 88.1 us (0.987)
  local copies, waits for them, and re-layouts: 2.28 us -> 0.86 us
    ppermute x0 -> x2, starting transfers between devices: none -> 2.09 us  [body(): lax.ppermute(v, 'lat', [(i, j if 0 <= (j := ((i - k ^ 1) + k)) < lat else...]
    ppermute x3 -> x2, starting transfers between devices: 5.48 us -> 3.49 us  [down(): return lax.ppermute(v, 'lat', [((i + 1) % lat, i) for i in range(lat)])]
    ppermute x12, waiting for transfers between devices: 10.7 us -> 12.6 us  [peer(): return lax.ppermute(v, 'lon', [(i, i ^ s) for i in range(lon)])]
    ppermute x3 -> x2, waiting for transfers between devices: 1.84 us -> 0.01 us  [down(): return lax.ppermute(v, 'lat', [((i + 1) % lat, i) for i in range(lat)])]
    unnamed x30, local copies, waits for them, and re-layouts: 2.28 us -> 0.86 us
    ppermute x6, starting transfers between devices: 11.6 us -> 12.7 us  [shift(): return lax.ppermute(v, 'lon', [(i, (i + s) % lon) for i in range(lon)])]
  transfers between devices with their start and end apart: 24 -> 24, of which waited for: 6 -> 7; matrix products, arithmetic and copies ran while one was open for 0% -> 0% of each run, Pallas kernels for 24% -> 24%
where the time goes in v4:
time: 88.1 us; the launch traced here: 87.8 us
  Pallas kernels  36.9 us (42%)
  starting transfers between devices  36.3 us (41%)
  waiting for transfers between devices  13.2 us (15%)
    pallas_call x15, Pallas kernels, call(): pl.pallas_call(kernel, out_shape=outs if single else tuple(outs), in_spec...  33.9 us
    ppermute x12, starting transfers between devices, peer(): return lax.ppermute(v, 'lon', [(i, i ^ s) for i in range(lon)])  18.1 us
    ppermute x6, starting transfers between devices, shift(): return lax.ppermute(v, 'lon', [(i, (i + s) % lon) for i in range(lon)])  12.7 us
    ppermute x12, waiting for transfers between devices, peer(): return lax.ppermute(v, 'lon', [(i, i ^ s) for i in range(lon)])  12.6 us
    ppermute x2, starting transfers between devices, down(): return lax.ppermute(v, 'lat', [((i + 1) % lat, i) for i in range(lat)])  3.49 us
    pallas_call x2, Pallas kernels, land(): pl.pallas_call(kernel, out_shape=shape(x.shape, F32), in_specs=spaces, ou...  3.04 us
    ppermute x2, starting transfers between devices, body(): lax.ppermute(v, 'lat', [(i, j if 0 <= (j := ((i - k ^ 1) + k)) < lat else...  2.09 us
  transfers between devices with their start and end apart: 24, of which 7 were waited for; matrix products, arithmetic and copies ran while one was open for 0% of the time, Pallas kernels for 24%

profile of v4, /device:TPU:0, one launch (start us, length us, event | category | flops | bytes accessed | tf_op | source)
XLA Modules:
  0.0 87.8 jit_solution(6246928067212180769)
XLA Ops:
  0.0 3.5 %shard_map.190 = (bf16[784,128]{1,0:T(8,128)(2,1)}, bf16[784,128]{1,0:T(8,128)(2,1)}, f32[2,32,384]{2,1,0:T(8,128)}, f32[3,8,128]{2,1,0:T(8,128)}, f32[4,24,128]{2,1,0:T(8,128)}) custom-call(s32[1]{0:T(128)} %bitcast.2.me_ref, s32[1]{0:T(128)} %bitcast.lat_ref, s32[16]{0:T(128)} %bitcast.18, f32[3072,128]{1,0:T(8,128)} %bitcast.10, f32[8,128]{1,0:T(8,128)} %refs_1_.2, ...), custom_call_target="tpu_custom_call" | custom-call | bytes 419430 | tf_op jit(solution)/shard_map/pallas_call | solution.py:32
  6.4 3.0 %shard_map.191.a_ref = bf16[4,256,1024]{2,1,0:T(8,128)(2,1)S(1)} custom-call(f32[4,24,128]{2,1,0:T(8,128)S(1)} %copy-done.7), custom_call_target="tpu_custom_call" | custom-call | flops 107374184 | bytes 209715 | tf_op jit(solution)/shard_map/pallas_call | solution.py:32
  9.7 2.6 %collective-permute-start.2 = (bf16[32,384]{1,0:T(8,128)(2,1)S(1)}, bf16[32,384]{1,0:T(8,128)(2,1)S(1)}, u32[]{:S(2)}, u32[]{:S(2)}) collective-permute-start(bf16[32,384]{1,0:T(8,128)(2,1)S(1)} %get-tuple-element.74), channel_id=1, source_target_pairs={{0,1},{1,2},{2,3},{3,0},{4,5},{5,6},{6,7},{7,4},{8,9},{9,10},{10,1... | collective-permute-start | bytes 73736 | tf_op jit(solution)/shard_map/ppermute | solution.py:484
  12.3 2.3 %collective-permute-start.3 = (bf16[32,384]{1,0:T(8,128)(2,1)S(1)}, bf16[32,384]{1,0:T(8,128)(2,1)S(1)}, u32[]{:S(2)}, u32[]{:S(2)}) collective-permute-start(bf16[32,384]{1,0:T(8,128)(2,1)S(1)} %get-tuple-element.81), channel_id=1, source_target_pairs={{0,3},{1,0},{2,1},{3,2},{4,7},{5,4},{6,5},{7,6},{8,11},{9,8},{10,9... | collective-permute-start | bytes 73736 | tf_op jit(solution)/shard_map/ppermute | solution.py:484
  16.5 2.8 %shard_map.194 = (f32[384,1024]{1,0:T(8,128)S(1)}, f32[256,384]{1,0:T(8,128)S(1)}, bf16[256,384]{1,0:T(8,128)(2,1)S(1)}, bf16[256,384]{1,0:T(8,128)(2,1)S(1)}, bf16[256,384]{1,0:T(8,128)(2,1)S(1)}) custom-call(s32[1]{0:T(128)} %bitcast.lat_ref, f32[10,384,128]{2,1,0:T(8,128)S(1)} %get-tuple-element.79.mid_ref, f32[5,10,128]{2,1,0:T(8,128)S(1)} %get-tuple-element.80.rate, ...), custom_call_target="tpu_custom_call" | custom-call | flops 40265320 | bytes 838860 | tf_op jit(solution)/shard_map/pallas_call | solution.py:32
  19.3 3.9 %collective-permute-start.4 = (bf16[256,384]{1,0:T(8,128)(2,1)S(1)}, bf16[256,384]{1,0:T(8,128)(2,1)S(1)}, u32[]{:S(2)}, u32[]{:S(2)}) collective-permute-start(bf16[256,384]{1,0:T(8,128)(2,1)S(1)} %get-tuple-element.89), channel_id=1, source_target_pairs={{0,3},{1,2},{2,1},{3,0},{4,7},{5,6},{6,5},{7,4},{8,11},{9,10},{10,... | collective-permute-start | bytes 589832 | tf_op jit(solution)/shard_map/ppermute | solution.py:489
  24.6 3.6 %shard_map.195 = (bf16[1536,768]{1,0:T(8,128)(2,1)S(1)}, bf16[256,1536]{1,0:T(8,128)(2,1)S(1)}, s32[1]{0:T(128)}) custom-call(s32[1,1536]{1,0:T(1,128)S(1)} %bitcast.15, s32[1,1536]{1,0:T(1,128)S(1)} %bitcast.16), custom_call_target="tpu_custom_call" | custom-call | flops 11324620 | bytes 419430 | tf_op jit(solution)/shard_map/pallas_call | solution.py:32
  29.6 2.9 %collective-permute-start.8 = (f32[24,128]{1,0:T(8,128)S(1)}, f32[24,128]{1,0:T(8,128)S(1)}, u32[]{:S(2)}, u32[]{:S(2)}) collective-permute-start(f32[24,128]{1,0:T(8,128)S(1)} %get-tuple-element.102), channel_id=1, source_target_pairs={{0,2},{1,3},{2,0},{3,1},{4,6},{5,7},{6,4},{7,5},{8,10},{9,11},{10,... | collective-permute-start | bytes 36872 | tf_op jit(solution)/shard_map/ppermute | solution.py:489
  32.6 4.5 %collective-permute-done.7.refs_1_ = f32[24,128]{1,0:T(8,128)S(1)} collective-permute-done((f32[24,128]{1,0:T(8,128)S(1)}, f32[24,128]{1,0:T(8,128)S(1)}, u32[]{:S(2)}, u32[]{:S(2)}) %collective-permute-start.7) | collective-permute-done | bytes 12320 | tf_op jit(solution)/shard_map/ppermute | solution.py:489
  37.5 3.5 %collective-permute-done.8.refs_2_ = f32[24,128]{1,0:T(8,128)S(1)} collective-permute-done((f32[24,128]{1,0:T(8,128)S(1)}, f32[24,128]{1,0:T(8,128)S(1)}, u32[]{:S(2)}, u32[]{:S(2)}) %collective-permute-start.8) | collective-permute-done | bytes 12320 | tf_op jit(solution)/shard_map/ppermute | solution.py:489
  42.6 1.8 %shard_map.199 = (f32[2,256,512]{2,1,0:T(8,128)S(1)}, bf16[2,512,512]{2,1,0:T(8,128)(2,1)S(1)}, bf16[96,512]{1,0:T(8,128)(2,1)S(1)}, bf16[96,512]{1,0:T(8,128)(2...) custom-call(f32[256,384]{1,0:T(8,128)S(1)} %get-tuple-element.109.refs_0_, ...), custom_call_target="tpu_custom_call" | custom-call | flops 100000000 | bytes 419430 | tf_op jit(solution)/shard_map/pallas_call | solution.py:32
  45.1 3.1 %collective-permute-start.11 = (bf16[96,512]{1,0:T(8,128)(2,1)S(1)}, bf16[96,512]{1,0:T(8,128)(2,1)S(1)}, u32[]{:S(2)}, u32[]{:S(2)}) collective-permute-start(bf16[96,512]{1,0:T(8,128)(2,1)S(1)} %get-tuple-element.122), channel_id=1, source_target_pairs={{0,3},{1,0},{2,1},{3,2},{4,7},{5,4},{6,5},{7,6},{8,11},{9,8},{10,9... | collective-permute-start | bytes 294920 | tf_op jit(solution)/shard_map/ppermute | solution.py:484
  48.2 1.7 %collective-permute-start.13 = (bf16[96,512]{1,0:T(8,128)(2,1)S(1)}, bf16[96,512]{1,0:T(8,128)(2,1)S(1)}, u32[]{:S(2)}, u32[]{:S(2)}) collective-permute-start(bf16[96,512]{1,0:T(8,128)(2,1)S(1)} %get-tuple-element.124), channel_id=1, source_target_pairs={{4,0},{8,4},{12,8},{0,12},{5,1},{9,5},{13,9},{1,13},{6,2},{10,6},{... | collective-permute-start | bytes 294920 | tf_op jit(solution)/shard_map/ppermute | solution.py:495
  50.0 3.2 %shard_map.200 = (f32[2,256,512]{2,1,0:T(8,128)S(1)}, f32[2,1536,512]{2,1,0:T(8,128)S(1)}) custom-call(s32[1]{0:T(128)} %get-tuple-element.108.local_ref.refs_0_, bf16[2,512,512]{2,1,0:T(8,128)(2,1)S(1)} %get-tuple-element.116.table_ref, bf16[1536,768]{1,0:T(8,128)(2,1)S(1)} %get-tuple-element.117.gather_ref.refs_4_, ...), custom_call_target="tpu_custom_call" | custom-call | flops 150000000 | bytes 419430 | tf_op jit(solution)/shard_map/pallas_call | solution.py:32
  53.3 3.7 %shard_map.201 = (f32[2,256,512]{2,1,0:T(8,128)S(1)}, bf16[2,512,512]{2,1,0:T(8,128)(2,1)S(1)}, bf16[96,512]{1,0:T(8,128)(2,1)S(1)}, bf16[96,512]{1,0:T(8,128)(2...) custom-call(s32[1]{0:T(128)} %get-tuple-element.108.local_ref.refs_0_, ...), custom_call_target="tpu_custom_call" | custom-call | flops 200000000 | bytes 629145 | tf_op jit(solution)/shard_map/pallas_call | solution.py:32
  57.0 3.8 %collective-permute-start.15 = (bf16[96,512]{1,0:T(8,128)(2,1)S(1)}, bf16[96,512]{1,0:T(8,128)(2,1)S(1)}, u32[]{:S(2)}, u32[]{:S(2)}) collective-permute-start(bf16[96,512]{1,0:T(8,128)(2,1)S(1)} %get-tuple-element.130), channel_id=1, source_target_pairs={{0,3},{1,0},{2,1},{3,2},{4,7},{5,4},{6,5},{7,6},{8,11},{9,8},{10,9... | collective-permute-start | bytes 294920 | tf_op jit(solution)/shard_map/ppermute | solution.py:484
  60.9 1.7 %collective-permute-start.17 = (bf16[96,512]{1,0:T(8,128)(2,1)S(1)}, bf16[96,512]{1,0:T(8,128)(2,1)S(1)}, u32[]{:S(2)}, u32[]{:S(2)}) collective-permute-start(bf16[96,512]{1,0:T(8,128)(2,1)S(1)} %get-tuple-element.132), channel_id=1, source_target_pairs={{4,0},{8,4},{12,8},{0,12},{5,1},{9,5},{13,9},{1,13},{6,2},{10,6},{... | collective-permute-start | bytes 294920 | tf_op jit(solution)/shard_map/ppermute | solution.py:495
  62.6 3.2 %shard_map.202 = (f32[2,256,512]{2,1,0:T(8,128)S(1)}, f32[2,1536,512]{2,1,0:T(8,128)S(1)}) custom-call(s32[1]{0:T(128)} %get-tuple-element.108.local_ref.refs_0_, bf16[2,512,512]{2,1,0:T(8,128)(2,1)S(1)} %get-tuple-element.126.table_ref, bf16[1536,768]{1,0:T(8,128)(2,1)S(1)} %get-tuple-element.117.gather_ref.refs_4_, ...), custom_call_target="tpu_custom_call" | custom-call | flops 150000000 | bytes 419430 | tf_op jit(solution)/shard_map/pallas_call | solution.py:32
  65.8 1.9 %shard_map.204.refs_0_ = bf16[192,256]{1,0:T(8,128)(2,1)S(1)} custom-call(s32[1]{0:T(128)} %get-tuple-element.108.local_ref.refs_0_, f32[2,256,512]{2,1,0:T(8,128)S(1)} %get-tuple-element.125.refs_1_, f32[2,1536,512]{2,1,0:T(8,128)S(1)} %get-tuple-element.127.refs_2_, bf16[192,256]{1,0:T(8,128)(2,1)S(1)} %get-tuple-element.114.refs_7_.refs_3_, ...), custom_call_target="tpu_custom_call" | custom-call | flops 100000000 | bytes 419430 | tf_op jit(solution)/shard_map/pallas_call | solution.py:32
  69.3 2.9 %collective-permute-start.23 = (bf16[192,256]{1,0:T(8,128)(2,1)S(1)}, bf16[192,256]{1,0:T(8,128)(2,1)S(1)}, u32[]{:S(2)}, u32[]{:S(2)}) collective-permute-start(bf16[192,256]{1,0:T(8,128)(2,1)S(1)} %shard_map.204.refs_0_), channel_id=1, source_target_pairs={{0,1},{1,0},{2,3},{3,2},{4,5},{5,4},{6,7},{7,6},{8,9},{9,8},{10,11... | collective-permute-start | bytes 294920 | tf_op jit(solution)/shard_map/ppermute | solution.py:489
  72.2 1.9 %shard_map.203.refs_0_ = bf16[192,256]{1,0:T(8,128)(2,1)S(1)} custom-call(s32[1]{0:T(128)} %get-tuple-element.108.local_ref.refs_0_, f32[2,256,512]{2,1,0:T(8,128)S(1)} %get-tuple-element.125.refs_1_, f32[2,1536,512]{2,1,0:T(8,128)S(1)} %get-tuple-element.127.refs_2_, bf16[192,256]{1,0:T(8,128)(2,1)S(1)} %get-tuple-element.114.refs_7_.refs_3_, ...), custom_call_target="tpu_custom_call" | custom-call | flops 100000000 | bytes 419430 | tf_op jit(solution)/shard_map/pallas_call | solution.py:32
  75.7 2.9 %collective-permute-start.20 = (bf16[192,256]{1,0:T(8,128)(2,1)S(1)}, bf16[192,256]{1,0:T(8,128)(2,1)S(1)}, u32[]{:S(2)}, u32[]{:S(2)}) collective-permute-start(bf16[192,256]{1,0:T(8,128)(2,1)S(1)} %shard_map.203.refs_0_), channel_id=1, source_target_pairs={{0,1},{1,0},{2,3},{3,2},{4,5},{5,4},{6,7},{7,6},{8,9},{9,8},{10,11... | collective-permute-start | bytes 294920 | tf_op jit(solution)/shard_map/ppermute | solution.py:489
  78.6 3.0 %shard_map.197.w_ref = bf16[4,256,1024]{2,1,0:T(8,128)(2,1)S(1)} custom-call(f32[24,128]{1,0:T(8,128)S(1)} %get-tuple-element.104.refs_0_, f32[24,128]{1,0:T(8,128)S(1)} %collective-permute-done.7.refs_1_, f32[24,128]{1,0:T(8,128)S(1)} %collective-permute-done.8.refs_2_, f32[24,128]{1,0:T(8,128)S(1)} %collective-permute-done.9.refs_3_), custom_call_target="tpu_custom_call" | custom-call | flops 107374184 | bytes 209715 | tf_op jit(solution)/shard_map/pallas_call | solution.py:32
  83.4 2.7 %collective-permute-done.19.refs_2_ = bf16[192,256]{1,0:T(8,128)(2,1)S(1)} collective-permute-done((bf16[192,256]{1,0:T(8,128)(2,1)S(1)}, bf16[192,256]{1,0:T(8,128)(2,1)S(1)}, u32[]{:S(2)}, u32[]{:S(2)}) %collective-permute-start.19) | collective-permute-done | bytes 98336 | tf_op jit(solution)/shard_map/ppermute | solution.py:489
  (71 shorter events, 17.0 us)
Async XLA Ops:
  3.5 5.9 %collective-permute-start = (bf16[784,128]{1,0:T(8,128)(2,1)}, bf16[784,128]{1,0:T(8,128)(2,1)S(1)}, u32[]{:S(2)}, u32[]{:S(2)}) collective-permute-start(bf16[784,128]{1,0:T(8,128)(2,1)} %get-tuple-element.69), channel_id=1, source_target_pairs={{0,4},{4,0},{8,12},{12,8},{1,5},{5,1},{9,13},{13,9},{2,6},{6,2},{1... | collective-permute-start | bytes 602120 | tf_op jit(solution)/shard_map/ppermute | solution.py:522
  4.1 5.4 %collective-permute-start.1 = (bf16[784,128]{1,0:T(8,128)(2,1)}, bf16[784,128]{1,0:T(8,128)(2,1)S(1)}, u32[]{:S(2)}, u32[]{:S(2)}) collective-permute-start(bf16[784,128]{1,0:T(8,128)(2,1)} %get-tuple-element.70), channel_id=1, source_target_pairs={{0,0},{4,8},{8,4},{12,12},{1,1},{5,9},{9,5},{13,13},{2,2},{6,10},{... | collective-permute-start | bytes 602120 | tf_op jit(solution)/shard_map/ppermute | solution.py:522
  9.7 6.5 %collective-permute-start.2 = (bf16[32,384]{1,0:T(8,128)(2,1)S(1)}, bf16[32,384]{1,0:T(8,128)(2,1)S(1)}, u32[]{:S(2)}, u32[]{:S(2)}) collective-permute-start(bf16[32,384]{1,0:T(8,128)(2,1)S(1)} %get-tuple-element.74), channel_id=1, source_target_pairs={{0,1},{1,2},{2,3},{3,0},{4,5},{5,6},{6,7},{7,4},{8,9},{9,10},{10,1... | collective-permute-start | bytes 73736 | tf_op jit(solution)/shard_map/ppermute | solution.py:484
  12.3 4.1 %collective-permute-start.3 = (bf16[32,384]{1,0:T(8,128)(2,1)S(1)}, bf16[32,384]{1,0:T(8,128)(2,1)S(1)}, u32[]{:S(2)}, u32[]{:S(2)}) collective-permute-start(bf16[32,384]{1,0:T(8,128)(2,1)S(1)} %get-tuple-element.81), channel_id=1, source_target_pairs={{0,3},{1,0},{2,1},{3,2},{4,7},{5,4},{6,5},{7,6},{8,11},{9,8},{10,9... | collective-permute-start | bytes 73736 | tf_op jit(solution)/shard_map/ppermute | solution.py:484
  19.3 23.2 %collective-permute-start.4 = (bf16[256,384]{1,0:T(8,128)(2,1)S(1)}, bf16[256,384]{1,0:T(8,128)(2,1)S(1)}, u32[]{:S(2)}, u32[]{:S(2)}) collective-permute-start(bf16[256,384]{1,0:T(8,128)(2,1)S(1)} %get-tuple-element.89), channel_id=1, source_target_pairs={{0,3},{1,2},{2,1},{3,0},{4,7},{5,6},{6,5},{7,4},{8,11},{9,10},{10,... | collective-permute-start | bytes 589832 | tf_op jit(solution)/shard_map/ppermute | solution.py:489
  23.2 19.4 %collective-permute-start.5 = (bf16[256,384]{1,0:T(8,128)(2,1)S(1)}, bf16[256,384]{1,0:T(8,128)(2,1)S(1)}, u32[]{:S(2)}, u32[]{:S(2)}) collective-permute-start(bf16[256,384]{1,0:T(8,128)(2,1)S(1)} %get-tuple-element.90), channel_id=1, source_target_pairs={{0,2},{1,3},{2,0},{3,1},{4,6},{5,7},{6,4},{7,5},{8,10},{9,11},{10,... | collective-permute-start | bytes 589832 | tf_op jit(solution)/shard_map/ppermute | solution.py:489
  23.2 19.4 %collective-permute-start.6 = (bf16[256,384]{1,0:T(8,128)(2,1)S(1)}, bf16[256,384]{1,0:T(8,128)(2,1)S(1)}, u32[]{:S(2)}, u32[]{:S(2)}) collective-permute-start(bf16[256,384]{1,0:T(8,128)(2,1)S(1)} %get-tuple-element.91), channel_id=1, source_target_pairs={{0,1},{1,0},{2,3},{3,2},{4,5},{5,4},{6,7},{7,6},{8,9},{9,8},{10,11... | collective-permute-start | bytes 589832 | tf_op jit(solution)/shard_map/ppermute | solution.py:489
  28.2 8.9 %collective-permute-start.7 = (f32[24,128]{1,0:T(8,128)S(1)}, f32[24,128]{1,0:T(8,128)S(1)}, u32[]{:S(2)}, u32[]{:S(2)}) collective-permute-start(f32[24,128]{1,0:T(8,128)S(1)} %get-tuple-element.101), channel_id=1, source_target_pairs={{0,1},{1,0},{2,3},{3,2},{4,5},{5,4},{6,7},{7,6},{8,9},{9,8},{10,11... | collective-permute-start | bytes 36872 | tf_op jit(solution)/shard_map/ppermute | solution.py:489
  29.6 11.3 %collective-permute-start.8 = (f32[24,128]{1,0:T(8,128)S(1)}, f32[24,128]{1,0:T(8,128)S(1)}, u32[]{:S(2)}, u32[]{:S(2)}) collective-permute-start(f32[24,128]{1,0:T(8,128)S(1)} %get-tuple-element.102), channel_id=1, source_target_pairs={{0,2},{1,3},{2,0},{3,1},{4,6},{5,7},{6,4},{7,5},{8,10},{9,11},{10,... | collective-permute-start | bytes 36872 | tf_op jit(solution)/shard_map/ppermute | solution.py:489
  37.1 5.5 %collective-permute-start.9 = (f32[24,128]{1,0:T(8,128)S(1)}, f32[24,128]{1,0:T(8,128)S(1)}, u32[]{:S(2)}, u32[]{:S(2)}) collective-permute-start(f32[24,128]{1,0:T(8,128)S(1)} %get-tuple-element.103), channel_id=1, source_target_pairs={{0,3},{1,2},{2,1},{3,0},{4,7},{5,6},{6,5},{7,4},{8,11},{9,10},{10,... | collective-permute-start | bytes 36872 | tf_op jit(solution)/shard_map/ppermute | solution.py:489
  44.4 8.9 %collective-permute-start.10 = (bf16[96,512]{1,0:T(8,128)(2,1)S(1)}, bf16[96,512]{1,0:T(8,128)(2,1)S(1)}, u32[]{:S(2)}, u32[]{:S(2)}) collective-permute-start(bf16[96,512]{1,0:T(8,128)(2,1)S(1)} %get-tuple-element.121), channel_id=1, source_target_pairs={{0,1},{1,2},{2,3},{3,0},{4,5},{5,6},{6,7},{7,4},{8,9},{9,10},{10,1... | collective-permute-start | bytes 294920 | tf_op jit(solution)/shard_map/ppermute | solution.py:484
  45.1 8.1 %collective-permute-start.11 = (bf16[96,512]{1,0:T(8,128)(2,1)S(1)}, bf16[96,512]{1,0:T(8,128)(2,1)S(1)}, u32[]{:S(2)}, u32[]{:S(2)}) collective-permute-start(bf16[96,512]{1,0:T(8,128)(2,1)S(1)} %get-tuple-element.122), channel_id=1, source_target_pairs={{0,3},{1,0},{2,1},{3,2},{4,7},{5,4},{6,5},{7,6},{8,11},{9,8},{10,9... | collective-permute-start | bytes 294920 | tf_op jit(solution)/shard_map/ppermute | solution.py:484
  48.2 5.0 %collective-permute-start.12 = (bf16[96,512]{1,0:T(8,128)(2,1)S(1)}, bf16[96,512]{1,0:T(8,128)(2,1)S(1)}, u32[]{:S(2)}, u32[]{:S(2)}) collective-permute-start(bf16[96,512]{1,0:T(8,128)(2,1)S(1)} %get-tuple-element.123), channel_id=1, source_target_pairs={{0,4},{4,8},{8,12},{12,0},{1,5},{5,9},{9,13},{13,1},{2,6},{6,10},{... | collective-permute-start | bytes 294920 | tf_op jit(solution)/shard_map/ppermute | solution.py:492
  48.2 5.0 %collective-permute-start.13 = (bf16[96,512]{1,0:T(8,128)(2,1)S(1)}, bf16[96,512]{1,0:T(8,128)(2,1)S(1)}, u32[]{:S(2)}, u32[]{:S(2)}) collective-permute-start(bf16[96,512]{1,0:T(8,128)(2,1)S(1)} %get-tuple-element.124), channel_id=1, source_target_pairs={{4,0},{8,4},{12,8},{0,12},{5,1},{9,5},{13,9},{1,13},{6,2},{10,6},{... | collective-permute-start | bytes 294920 | tf_op jit(solution)/shard_map/ppermute | solution.py:495
  57.0 8.8 %collective-permute-start.14 = (bf16[96,512]{1,0:T(8,128)(2,1)S(1)}, bf16[96,512]{1,0:T(8,128)(2,1)S(1)}, u32[]{:S(2)}, u32[]{:S(2)}) collective-permute-start(bf16[96,512]{1,0:T(8,128)(2,1)S(1)} %get-tuple-element.129), channel_id=1, source_target_pairs={{0,1},{1,2},{2,3},{3,0},{4,5},{5,6},{6,7},{7,4},{8,9},{9,10},{10,1... | collective-permute-start | bytes 294920 | tf_op jit(solution)/shard_map/ppermute | solution.py:484
  57.0 8.8 %collective-permute-start.15 = (bf16[96,512]{1,0:T(8,128)(2,1)S(1)}, bf16[96,512]{1,0:T(8,128)(2,1)S(1)}, u32[]{:S(2)}, u32[]{:S(2)}) collective-permute-start(bf16[96,512]{1,0:T(8,128)(2,1)S(1)} %get-tuple-element.130), channel_id=1, source_target_pairs={{0,3},{1,0},{2,1},{3,2},{4,7},{5,4},{6,5},{7,6},{8,11},{9,8},{10,9... | collective-permute-start | bytes 294920 | tf_op jit(solution)/shard_map/ppermute | solution.py:484
  60.9 5.0 %collective-permute-start.16 = (bf16[96,512]{1,0:T(8,128)(2,1)S(1)}, bf16[96,512]{1,0:T(8,128)(2,1)S(1)}, u32[]{:S(2)}, u32[]{:S(2)}) collective-permute-start(bf16[96,512]{1,0:T(8,128)(2,1)S(1)} %get-tuple-element.131), channel_id=1, source_target_pairs={{0,4},{4,8},{8,12},{12,0},{1,5},{5,9},{9,13},{13,1},{2,6},{6,10},{... | collective-permute-start | bytes 294920 | tf_op jit(solution)/shard_map/ppermute | solution.py:492
  60.9 5.0 %collective-permute-start.17 = (bf16[96,512]{1,0:T(8,128)(2,1)S(1)}, bf16[96,512]{1,0:T(8,128)(2,1)S(1)}, u32[]{:S(2)}, u32[]{:S(2)}) collective-permute-start(bf16[96,512]{1,0:T(8,128)(2,1)S(1)} %get-tuple-element.132), channel_id=1, source_target_pairs={{4,0},{8,4},{12,8},{0,12},{5,1},{9,5},{13,9},{1,13},{6,2},{10,6},{... | collective-permute-start | bytes 294920 | tf_op jit(solution)/shard_map/ppermute | solution.py:495
  67.8 7.9 %collective-permute-start.21 = (bf16[192,256]{1,0:T(8,128)(2,1)S(1)}, bf16[192,256]{1,0:T(8,128)(2,1)S(1)}, u32[]{:S(2)}, u32[]{:S(2)}) collective-permute-start(bf16[192,256]{1,0:T(8,128)(2,1)S(1)} %shard_map.204.refs_0_), channel_id=1, source_target_pairs={{0,3},{1,2},{2,1},{3,0},{4,7},{5,6},{6,5},{7,4},{8,11},{9,10},{10,... | collective-permute-start | bytes 294920 | tf_op jit(solution)/shard_map/ppermute | solution.py:489
  69.3 12.6 %collective-permute-start.22 = (bf16[192,256]{1,0:T(8,128)(2,1)S(1)}, bf16[192,256]{1,0:T(8,128)(2,1)S(1)}, u32[]{:S(2)}, u32[]{:S(2)}) collective-permute-start(bf16[192,256]{1,0:T(8,128)(2,1)S(1)} %shard_map.204.refs_0_), channel_id=1, source_target_pairs={{0,2},{1,3},{2,0},{3,1},{4,6},{5,7},{6,4},{7,5},{8,10},{9,11},{10,... | collective-permute-start | bytes 294920 | tf_op jit(solution)/shard_map/ppermute | solution.py:489
  69.3 12.6 %collective-permute-start.23 = (bf16[192,256]{1,0:T(8,128)(2,1)S(1)}, bf16[192,256]{1,0:T(8,128)(2,1)S(1)}, u32[]{:S(2)}, u32[]{:S(2)}) collective-permute-start(bf16[192,256]{1,0:T(8,128)(2,1)S(1)} %shard_map.204.refs_0_), channel_id=1, source_target_pairs={{0,1},{1,0},{2,3},{3,2},{4,5},{5,4},{6,7},{7,6},{8,9},{9,8},{10,11... | collective-permute-start | bytes 294920 | tf_op jit(solution)/shard_map/ppermute | solution.py:489
  74.1 9.3 %collective-permute-start.18 = (bf16[192,256]{1,0:T(8,128)(2,1)S(1)}, bf16[192,256]{1,0:T(8,128)(2,1)S(1)}, u32[]{:S(2)}, u32[]{:S(2)}) collective-permute-start(bf16[192,256]{1,0:T(8,128)(2,1)S(1)} %shard_map.203.refs_0_), channel_id=1, source_target_pairs={{0,3},{1,2},{2,1},{3,0},{4,7},{5,6},{6,5},{7,4},{8,11},{9,10},{10,... | collective-permute-start | bytes 294920 | tf_op jit(solution)/shard_map/ppermute | solution.py:489
  75.6 10.5 %collective-permute-start.19 = (bf16[192,256]{1,0:T(8,128)(2,1)S(1)}, bf16[192,256]{1,0:T(8,128)(2,1)S(1)}, u32[]{:S(2)}, u32[]{:S(2)}) collective-permute-start(bf16[192,256]{1,0:T(8,128)(2,1)S(1)} %shard_map.203.refs_0_), channel_id=1, source_target_pairs={{0,2},{1,3},{2,0},{3,1},{4,6},{5,7},{6,4},{7,5},{8,10},{9,11},{10,... | collective-permute-start | bytes 294920 | tf_op jit(solution)/shard_map/ppermute | solution.py:489
  75.7 10.4 %collective-permute-start.20 = (bf16[192,256]{1,0:T(8,128)(2,1)S(1)}, bf16[192,256]{1,0:T(8,128)(2,1)S(1)}, u32[]{:S(2)}, u32[]{:S(2)}) collective-permute-start(bf16[192,256]{1,0:T(8,128)(2,1)S(1)} %shard_map.203.refs_0_), channel_id=1, source_target_pairs={{0,1},{1,0},{2,3},{3,2},{4,5},{5,4},{6,7},{7,6},{8,9},{9,8},{10,11... | collective-permute-start | bytes 294920 | tf_op jit(solution)/shard_map/ppermute | solution.py:489
  (15 other events, 155.2 us)
